TPU v7x, 32 devices: a whole 2x2x4 slice. The times are simulated.
32 devices in a mesh: groups: 2 (over y), user: 4 (over z), item: 2 (over x), rep: 2 (over core).
Axes of the slice: x: 2, y: 2, z: 4, core: 2. Of those that a mesh axis runs over, the one named last changes fastest.
Arguments:
- user_emb: bfloat16 [64, 16384], P(None, ('groups', 'user')), parts along dimension 1, may hold values from -2 to 2
- item_emb: bfloat16 [64, 8192], P(None, ('groups', 'item')), parts along dimension 1, may hold values from -2 to 2
- user_deg: int32 [16384], P(('groups', 'user')), parts along dimension 0, may hold values from 16 to 256
- item_deg: int32 [8192], P(('groups', 'item')), parts along dimension 0, may hold values from 16 to 256
- block_vals: bfloat16 [9216, 128, 128], P(('groups', 'user', 'item', 'rep')), parts along dimension 0, may hold values from 0 to 1
- block_row: int32 [9216], P(('groups', 'user', 'item', 'rep')), parts along dimension 0, may hold values from 0 to 15
- block_col: int32 [9216], P(('groups', 'user', 'item', 'rep')), parts along dimension 0, may hold values from 0 to 15
- block_count: int32 [32], P(('groups', 'user', 'item', 'rep')), parts along dimension 0, may hold values from 36 to 288, as said below
- trip_user: int32 [8192], P(('groups', 'user', 'item', 'rep')), parts along dimension 0, may hold values from 0 to 2047
- trip_pos: int32 [8192], P(('groups', 'user', 'item', 'rep')), parts along dimension 0, may hold values from 0 to 2047
- trip_neg: int32 [8192], P(('groups', 'user', 'item', 'rep')), parts along dimension 0, may hold values from 0 to 2047
Outputs:
- grad_user: float32 [64, 16384], P(None, ('groups', 'user')), parts along dimension 1
- grad_item: float32 [64, 8192], P(None, ('groups', 'item')), parts along dimension 1
There are 2 independent parts, one for each index of `groups`. A program takes and returns all parts, laid end to end along the dimension named above; each array names one. Nothing has to cross between parts.
Inputs may be any that keep to these rules, and one draw needn't show every extreme that they name: `block_count`: every draw has a device with exactly 288 live slots; slots at or past a device's count hold arbitrary values and are left out of R.
All inputs are finite; a program needn't handle non-finite values.
Results may differ from a plain program's by a relative error of at most 0.00076.
Values sent between devices are 32-bit elements; how exact they have to be, the bound alone decides.
No kernel may reach another device: no remote copies, remote signals or barrier semaphores. Data moves between devices by JAX's collectives and lax.ppermute only.
A program may use at most 128 MiB of HBM per device.

v0:
```python
import functools

import jax
import jax.numpy as jnp
from jax import lax
from jax.experimental import pallas as pl
from jax.experimental.pallas import tpu as pltpu
from jax.sharding import PartitionSpec as P

F32 = jnp.float32
BF16 = jnp.bfloat16
GROUP = 8
CHUNK = 32

VMEM = pl.BlockSpec(memory_space=pltpu.VMEM)
SMEM = pl.BlockSpec(memory_space=pltpu.SMEM)
ANY = pl.BlockSpec(memory_space=pl.ANY)


def call(kernel, outs, ins, specs, scratch=(), flops=0, moved=0):
    return pl.pallas_call(
        kernel,
        out_shape=outs,
        in_specs=specs,
        out_specs=jax.tree.map(lambda _: VMEM, outs),
        scratch_shapes=list(scratch),
        cost_estimate=pl.CostEstimate(flops=flops, bytes_accessed=moved, transcendentals=0),
        compiler_params=pltpu.CompilerParams(vmem_limit_bytes=48 * 1024 * 1024),
    )(*ins)


def shape(*dims):
    return jax.ShapeDtypeStruct(dims, F32)


def split3(values):
    high = values.astype(BF16)
    rest = values - high.astype(F32)
    middle = rest.astype(BF16)
    low = (rest - middle.astype(F32)).astype(BF16)
    return high, middle, low


def scale_of(deg_ref, block):
    return lax.rsqrt(deg_ref[pl.ds(block, 1), :].astype(F32))


def hot(ids, start, rows):
    place = lax.broadcasted_iota(jnp.int32, (rows, ids.shape[1]), 0) + start
    return jnp.where(place == ids, 1.0, 0.0)


def start_blocks(count, vals, buf, sems):
    for part in range(vals.shape[0] // CHUNK):
        @pl.when(part * CHUNK < count)
        def _():
            span = pl.ds(part * CHUNK, CHUNK)
            pltpu.make_async_copy(vals.at[span], buf.at[span], sems.at[part]).start()


def multiply_blocks(count, source_ids, target_ids, vals, buf, sems, source, total, across):
    trash = total.shape[0] - 1
    total[...] = jnp.zeros_like(total)
    contract = (((1,), (1,)), ((), ())) if across else (((1,), (0,)), ((), ()))

    def group(index, _):
        first = index * GROUP
        targets, terms = [], []
        for step in range(GROUP):
            slot = first + step
            live = slot < count
            origin = jnp.where(live, source_ids[slot], 0)
            targets.append(jnp.where(live, target_ids[slot], trash))
            terms.append(
                lax.dot_general(source[origin], buf[slot], contract, preferred_element_type=F32)
            )
        for target, term in zip(targets, terms):
            total[target] += term
        return 0

    per = CHUNK // GROUP
    for part in range(vals.shape[0] // CHUNK):
        @pl.when(part * CHUNK < count)
        def _():
            span = pl.ds(part * CHUNK, CHUNK)
            pltpu.make_async_copy(vals.at[span], buf.at[span], sems.at[part]).wait()
            groups = jnp.minimum(per, (count - part * CHUNK + GROUP - 1) // GROUP)
            lax.fori_loop(part * per, part * per + groups, group, 0)


def product_scratch(slots, size, width, sources, targets):
    return [
        pltpu.VMEM((slots, size, size), BF16),
        pltpu.SemaphoreType.DMA((slots // CHUNK,)),
        pltpu.VMEM((sources, width, size), BF16),
        pltpu.VMEM((targets + 1, width, size), F32),
    ]


def first_pass(across, count, source_ids, target_ids, emb, source_deg, target_deg, vals, out,
               buf, sems, source, total):
    start_blocks(count[0], vals, buf, sems)
    size = source.shape[2]
    for block in range(source.shape[0]):
        piece = emb[:, block * size:(block + 1) * size].astype(F32)
        source[block] = (scale_of(source_deg, block) * piece).astype(BF16)
    multiply_blocks(count[0], source_ids, target_ids, vals, buf, sems, source, total, across)
    for block in range(out.shape[0]):
        out[block] = scale_of(target_deg, block) * total[block]


def table_of(blocks, table):
    count, width, size = blocks.shape
    for block in range(count):
        span = slice(block * size, (block + 1) * size)
        for part, piece in enumerate(split3(blocks[block])):
            table[part * width:(part + 1) * width, span] = piece


def fold(stacked, width):
    return (
        stacked[:width] + stacked[width:2 * width] + stacked[2 * width:3 * width]
    )


def pick(table, ids_ref, peer, rows, tile):
    total = None
    for start in range(0, table.shape[1], tile):
        chosen = hot(ids_ref[peer, pl.ds(rows[0], 1), :], start, tile)
        if len(rows) == 2:
            chosen = chosen - hot(ids_ref[peer, pl.ds(rows[1], 1), :], start, tile)
        term = jnp.dot(
            table[:, start:start + tile], chosen.astype(BF16), preferred_element_type=F32
        )
        total = term if total is None else total + term
    return total


def gather(rows, blocks, ids, keep, send, table):
    width = blocks.shape[1]
    tile = 2 * blocks.shape[2]
    table_of(blocks, table)

    def one(peer, _):
        keep[peer] = fold(pick(table, ids, peer, rows, tile), width)
        send[peer] = fold(pick(table, ids, peer, [row + 3 for row in rows], tile), width)
        return 0

    lax.fori_loop(0, ids.shape[0], one, 0)


def gather_base(user_emb, item_emb, ids, user_out, item_out):
    user_out[...] = pick(user_emb, ids, 0, [0], 256)
    item_out[...] = pick(item_emb, ids, 0, [1, 2], 256)


def add_split(peers, keep, received, *outs):
    for peer in range(peers):
        outs[peer][...] = keep[peer] + received[peer]


def add_all(refs):
    total = refs[0][...]
    for ref in refs[1:]:
        total = total + ref[...]
    return total


def slopes(user_parts, item_parts, *refs):
    users, items = refs[:user_parts], refs[user_parts:user_parts + item_parts]
    pieces, pushed = refs[user_parts + item_parts:]
    user_rows = 0.5 * add_all(users)
    difference = 0.5 * add_all(items)
    margin = jnp.sum(user_rows * difference, axis=0, keepdims=True)
    slope = -jax.nn.sigmoid(-margin)
    pieces[...] = slope * difference
    pushed[...] = slope * user_rows


def second_pass(across, rows, chunks, count, source_ids, target_ids, ids, source_deg, target_deg,
                vals, *refs):
    pieces = refs[:len(chunks)]
    half_grad, keep, send, buf, sems, source, total, table = refs[len(chunks):]
    start_blocks(count[0], vals, buf, sems)
    blocks, width, size = source.shape
    tile = 2 * size
    trips = ids.shape[2]
    for place, piece in enumerate(pieces):
        for part, value in enumerate(split3(piece[...])):
            table[place, part * width:(part + 1) * width, :] = value
    for start in range(0, blocks * size, tile):
        total_here = jnp.zeros((3 * width, tile), F32)
        for place, (peer, other) in enumerate(chunks):
            chosen = hot(ids[peer, pl.ds(rows[0] + 3 * other, 1), :], start, tile)
            if len(rows) == 2:
                chosen = chosen - hot(ids[peer, pl.ds(rows[1] + 3 * other, 1), :], start, tile)
            total_here = total_here + lax.dot_general(
                table[place], chosen.astype(BF16), (((1,), (1,)), ((), ())),
                preferred_element_type=F32,
            )
        grad = fold(total_here, width)
        for offset in range(0, tile, size):
            block = (start + offset) // size
            mine = grad[:, offset:offset + size]
            half_grad[block] = 0.5 * mine
            source[block] = (scale_of(source_deg, block) * mine * 0.5).astype(BF16)
    multiply_blocks(count[0], source_ids, target_ids, vals, buf, sems, source, total, across)
    me = lax.axis_index("rep")
    half = keep.shape[1]
    for block in range(keep.shape[0]):
        scale = scale_of(target_deg, block)
        keep[block] = scale * total[block, pl.ds(pl.multiple_of(me * half, half), half), :]
        send[block] = scale * total[block, pl.ds(pl.multiple_of((1 - me) * half, half), half), :]


def add_deal(peers, keep, received, *outs):
    me = lax.axis_index("user")
    per = outs[0].shape[0]
    for offset in range(peers):
        there = lax.rem(me + offset, peers) * per
        for block in range(per):
            outs[offset][block] = keep[there + block] + received[there + block]


def add_two(keep, received, out):
    out[...] = keep[...] + received[...]


def sum_parts(*refs):
    refs[-1][...] = add_all(refs[:-1])


def finish_users(parts, half_grad, *refs):
    mine, other = refs[:parts], refs[parts:2 * parts]
    out = refs[-1]
    me = lax.axis_index("rep")
    blocks, width, size = half_grad.shape
    half = width // 2
    for block in range(blocks):
        span = slice(block * size, (block + 1) * size)
        for rank, group in ((me, mine), (1 - me, other)):
            rows = pl.ds(pl.multiple_of(rank * half, half), half)
            total = half_grad[block, rows, :]
            for ref in group:
                total = total + ref[block]
            out[rows, span] = total


def finish_items(peers, half_grad, *refs):
    mine, other = refs[:peers], refs[peers:2 * peers]
    out = refs[-1]
    me = lax.axis_index("rep")
    place = lax.axis_index("user")
    blocks, width, size = half_grad.shape
    half = width // 2
    per = blocks // peers
    for offset in range(peers):
        there = lax.rem(place + offset, peers) * per
        for block in range(per):
            span = pl.ds(pl.multiple_of((there + block) * size, size), size)
            for rank, group in ((me, mine), (1 - me, other)):
                rows = pl.ds(pl.multiple_of(rank * half, half), half)
                out[rows, span] = half_grad[there + block, rows, :] + group[offset][block]


def shift(values, axis, count, offset):
    return lax.ppermute(values, axis, [(i, (i + offset) % count) for i in range(count)])


def on_device(users, items, user_emb, item_emb, user_deg, item_deg, block_vals, block_row,
              block_col, block_count, trip_user, trip_pos, trip_neg):
    width = user_emb.shape[0]
    slots, size, _ = block_vals.shape
    user_blocks = user_emb.shape[1] // size
    item_blocks = item_emb.shape[1] // size
    trips = trip_user.shape[0]
    half = width // 2
    swap = functools.partial(shift, axis="rep", count=2, offset=1)
    user_deg = user_deg.reshape(user_blocks, size)
    item_deg = item_deg.reshape(item_blocks, size)

    ids = jnp.stack([trip_user, trip_pos, trip_neg])
    ids = jnp.concatenate([ids, swap(ids)])
    ids_user = jnp.stack([ids] + [shift(ids, "item", items, -o) for o in range(1, items)])
    ids_item = jnp.stack([ids] + [shift(ids, "user", users, -o) for o in range(1, users)])

    product_flops = 2 * slots * size * size * width
    product_bytes = slots * size * size * 2

    def first(across, emb, source_deg, target_deg, source_ids, target_ids, sources, targets):
        return call(
            functools.partial(first_pass, across),
            shape(targets, width, size),
            (block_count, source_ids, target_ids, emb, source_deg, target_deg, block_vals),
            [SMEM, SMEM, SMEM, VMEM, VMEM, VMEM, ANY],
            product_scratch(slots, size, width, sources, targets),
            product_flops, product_bytes,
        )

    def picked(rows, table, peer_ids):
        peers = peer_ids.shape[0]
        blocks = table.shape[0]
        return call(
            functools.partial(gather, rows),
            [shape(peers, width, trips)] * 2,
            (table, peer_ids),
            [VMEM, VMEM],
            [pltpu.VMEM((3 * width, blocks * size), BF16)],
            2 * peers * 2 * 3 * width * blocks * size * trips, 4 * blocks * width * size,
        )

    def reduced(rows, table, peer_ids, axis):
        peers = peer_ids.shape[0]
        keep, send = picked(rows, table, peer_ids)
        received = swap(send)
        dealt = call(
            functools.partial(add_split, peers),
            [shape(width, trips)] * peers,
            (keep, received), [VMEM, VMEM],
            moved=12 * peers * width * trips,
        )
        return [dealt[0]] + [shift(dealt[o], axis, peers, o) for o in range(1, peers)]

    item_table = first(False, user_emb, user_deg, item_deg, block_row, block_col,
                       user_blocks, item_blocks)
    item_parts = reduced([1, 2], item_table, ids_item, "user")
    user_table = first(True, item_emb, item_deg, user_deg, block_col, block_row,
                       item_blocks, user_blocks)
    user_parts = reduced([0], user_table, ids_user, "item")
    user_base, item_base = call(
        gather_base, [shape(width, trips)] * 2, (user_emb, item_emb, ids_item),
        [VMEM, VMEM, VMEM], (), 4 * width * trips * size * (user_blocks + item_blocks),
        2 * width * size * (user_blocks + item_blocks),
    )
    user_parts.append(user_base)
    item_parts.append(item_base)
    pieces, pushed = call(
        functools.partial(slopes, len(user_parts), len(item_parts)),
        [shape(width, trips)] * 2,
        (*user_parts, *item_parts), [VMEM] * (len(user_parts) + len(item_parts)),
        moved=4 * width * trips * (len(user_parts) + len(item_parts) + 2),
    )

    def shared(own, axis, peers):
        arrays, chunks = [own, swap(own)], [(0, 0), (0, 1)]
        for offset in range(1, peers):
            come = shift(own, axis, peers, offset)
            arrays += [come, swap(come)]
            chunks += [(peers - offset, 0), (peers - offset, 1)]
        return arrays, chunks

    def second(across, rows, own, axis, peer_ids, source_deg, target_deg, source_ids, target_ids,
               sources, targets):
        arrays, chunks = shared(own, axis, peer_ids.shape[0])
        return call(
            functools.partial(second_pass, across, rows, chunks),
            [shape(sources, width, size), shape(targets, half, size), shape(targets, half, size)],
            (block_count, source_ids, target_ids, peer_ids, source_deg, target_deg, block_vals,
             *arrays),
            [SMEM, SMEM, SMEM, VMEM, VMEM, VMEM, ANY] + [VMEM] * len(arrays),
            product_scratch(slots, size, width, sources, targets)
            + [pltpu.VMEM((len(arrays), 3 * width, trips), BF16)],
            product_flops + 2 * len(arrays) * 3 * width * trips * sources * size, product_bytes,
        )

    user_half_grad, item_keep, item_send = second(
        False, [0], pieces, "item", ids_user, user_deg, item_deg, block_row, block_col,
        user_blocks, item_blocks)
    item_half_grad, user_keep, user_send = second(
        True, [1, 2], pushed, "user", ids_item, item_deg, user_deg, block_col, block_row,
        item_blocks, user_blocks)

    per = item_blocks // users
    dealt = call(
        functools.partial(add_deal, users), [shape(per, half, size)] * users,
        (item_keep, swap(item_send)), [VMEM, VMEM], moved=12 * item_blocks * half * size,
    )
    parts = [dealt[0]] + [shift(dealt[o], "user", users, o) for o in range(1, users)]
    own = call(sum_parts, shape(per, half, size), tuple(parts), [VMEM] * users,
               moved=4 * (users + 1) * per * half * size)
    mine = [own] + [shift(own, "user", users, -o) for o in range(1, users)]
    other = [swap(part) for part in mine]
    grad_item = call(
        functools.partial(finish_items, users), shape(width, item_blocks * size),
        (item_half_grad, *mine, *other), [VMEM] * (2 * users + 1),
        moved=12 * item_blocks * width * size,
    )

    own = call(add_two, shape(user_blocks, half, size), (user_keep, swap(user_send)),
               [VMEM, VMEM], moved=12 * user_blocks * half * size)
    mine = [own] + [shift(own, "item", items, o) for o in range(1, items)]
    other = [swap(part) for part in mine]
    grad_user = call(
        functools.partial(finish_users, items), shape(width, user_blocks * size),
        (user_half_grad, *mine, *other), [VMEM] * (2 * items + 1),
        moved=12 * user_blocks * width * size,
    )
    return (grad_user, grad_item)


def solution(mesh):
    return jax.shard_map(
        functools.partial(on_device, mesh.shape["user"], mesh.shape["item"]),
        mesh=mesh,
        in_specs=(
            P(None, ("groups", "user")),
            P(None, ("groups", "item")),
            P(("groups", "user")),
            P(("groups", "item")),
            P(("groups", "user", "item", "rep"), None, None),
            P(("groups", "user", "item", "rep")),
            P(("groups", "user", "item", "rep")),
            P(("groups", "user", "item", "rep")),
            P(("groups", "user", "item", "rep")),
            P(("groups", "user", "item", "rep")),
            P(("groups", "user", "item", "rep")),
        ),
        out_specs=(P(None, ("groups", "user")), P(None, ("groups", "item"))),
        check_vma=False,
    )
```

profile of v0, /device:TPU:0, one launch (start us, length us, event | category | flops | bytes accessed | tf_op | source)
XLA Modules:
  0.0 114.4 jit_solution(17202127846773436054)
XLA Ops:
  0.6 0.8 pad_add_fusion.3
  1.4 0.5 collective-permute-start
  2.5 0.0 copy-start.1
  2.5 0.9 copy-done.1
  3.5 0.7 copy-done.3
  4.2 0.7 copy-done.5
  4.9 0.7 copy-done.7
  5.5 0.7 copy-done.9
  6.3 5.3 %shard_map.126.blocks = f32[16,64,128]{2,1,0:T(8,128)S(1)} custom-call(s32[1]{0:T(128)S(6)} %copy.13.count, s32[288]{0:T(512)S(1)} %copy-done.7, s32[288]{0:T(512)S(1)} %copy-done.9, bf16[64,2048]{1,0:T(8,128)(2,1)S(1)} %copy-done.1, s32[16,128]{1,0:T(8,128)S(1)} %bitcast.11, s32[16,128]{1,0:T(8,128)S(1)} %bitcast.15, bf16[288,128,128]{2,1,0:T(8,128)(2,1)} %vals.7), custom_call_target="tpu_custom_call" | custom-call | flops 603979776 | bytes 9437184 | tf_op jit(solution)/shard_map/pallas_call | solution.py:21
  11.6 0.0 copy-start.2
  11.6 0.0 copy-start.10
  11.7 8.8 %collective-permute-start.4 = (s32[6,256]{1,0:T(8,128)S(1)}, s32[6,256]{1,0:T(8,128)S(1)}, u32[]{:S(2)}, u32[]{:S(2)}) collective-permute-start(s32[6,256]{1,0:T(8,128)S(1)} %get-tuple-element.51), channel_id=1, source_target_pairs={{0,12},{4,0},{8,4},{12,8},{1,13},{5,1},{9,5},{13,9},{2,14},{6,2},{... | collective-permute-start | bytes 18440 | tf_op jit(solution)/shard_map/ppermute | solution.py:267
  20.5 0.6 collective-permute-start.6
  21.2 6.5 %shard_map.122.blocks = f32[16,64,128]{2,1,0:T(8,128)S(1)} custom-call(s32[1]{0:T(128)S(6)} %copy.13.count, s32[288]{0:T(512)S(1)} %copy-done.9, s32[288]{0:T(512)S(1)} %copy-done.8, bf16[64,2048]{1,0:T(8,128)(2,1)S(1)} %copy-done, s32[16,128]{1,0:T(8,128)S(1)} %bitcast.16, s32[16,128]{1,0:T(8,128)S(1)} %bitcast.12, bf16[288,128,128]{2,1,0:T(8,128)(2,1)} %vals.7), custom_call_target="tpu_custom_call" | custom-call | flops 603979776 | bytes 9437184 | tf_op jit(solution)/shard_map/pallas_call | solution.py:21
  27.7 0.1 collective-permute-start.1
  27.8 4.3 %shard_map.127 = (f32[4,64,256]{2,1,0:T(8,128)S(1)}, f32[4,64,256]{2,1,0:T(8,128)S(1)}) custom-call(f32[16,64,128]{2,1,0:T(8,128)S(1)} %shard_map.126.blocks, s32[4,6,256]{2,1,0:T(8,128)S(1)} %pad_add_fusion.ids), custom_call_target="tpu_custom_call" | custom-call | flops 1610612736 | bytes 524288 | tf_op jit(solution)/shard_map/pallas_call | solution.py:21
  32.1 0.1 collective-permute-start.7
  32.2 1.3 %shard_map.123 = (f32[2,64,256]{2,1,0:T(8,128)S(1)}, f32[2,64,256]{2,1,0:T(8,128)S(1)}) custom-call(f32[16,64,128]{2,1,0:T(8,128)S(1)} %shard_map.122.blocks, s32[2,6,256]{2,1,0:T(8,128)S(1)} %pad_add_fusion.1.ids), custom_call_target="tpu_custom_call" | custom-call | flops 805306368 | bytes 524288 | tf_op jit(solution)/shard_map/pallas_call | solution.py:21
  33.6 0.5 collective-permute-start.2
  34.1 1.0 collective-permute-done.2.received
  35.1 2.1 %collective-permute-start.3 = (f32[64,256]{1,0:T(8,128)S(1)}, f32[64,256]{1,0:T(8,128)S(1)}, u32[]{:S(2)}, u32[]{:S(2)}) collective-permute-start(f32[64,256]{1,0:T(8,128)S(1)} %get-tuple-element.29), channel_id=1, source_target_pairs={{0,2},{2,0},{1,3},{3,1},{4,6},{6,4},{5,7},{7,5},{8,10},{10,8},{9,1... | collective-permute-start | bytes 196616 | tf_op jit(solution)/shard_map/ppermute | solution.py:267
  37.2 9.0 %collective-permute-start.10 = (f32[64,256]{1,0:T(8,128)S(1)}, f32[64,256]{1,0:T(8,128)S(1)}, u32[]{:S(2)}, u32[]{:S(2)}) collective-permute-start(f32[64,256]{1,0:T(8,128)S(1)} %get-tuple-element.36), channel_id=1, source_target_pairs={{0,12},{4,0},{8,4},{12,8},{1,13},{5,1},{9,5},{13,9},{2,14},{6,2},{... | collective-permute-start | bytes 196616 | tf_op jit(solution)/shard_map/ppermute | solution.py:267
  46.2 0.6 collective-permute-start.9
  46.8 0.6 shard_map.125
  47.5 1.2 %collective-permute-done.10.refs_6_ = f32[64,256]{1,0:T(8,128)S(1)} collective-permute-done((f32[64,256]{1,0:T(8,128)S(1)}, f32[64,256]{1,0:T(8,128)S(1)}, u32[]{:S(2)}, u32[]{:S(2)}) %collective-permute-start.10) | collective-permute-done | bytes 65568 | tf_op jit(solution)/shard_map/ppermute | solution.py:267
  48.7 3.9 %collective-permute-done.8.refs_4_ = f32[64,256]{1,0:T(8,128)S(1)} collective-permute-done((f32[64,256]{1,0:T(8,128)S(1)}, f32[64,256]{1,0:T(8,128)S(1)}, u32[]{:S(2)}, u32[]{:S(2)}) %collective-permute-start.8) | collective-permute-done | bytes 65568 | tf_op jit(solution)/shard_map/ppermute | solution.py:267
  52.6 1.3 %collective-permute-done.9.refs_5_ = f32[64,256]{1,0:T(8,128)S(1)} collective-permute-done((f32[64,256]{1,0:T(8,128)S(1)}, f32[64,256]{1,0:T(8,128)S(1)}, u32[]{:S(2)}, u32[]{:S(2)}) %collective-permute-start.9) | collective-permute-done | bytes 65568 | tf_op jit(solution)/shard_map/ppermute | solution.py:267
  53.9 0.1 shard_map.129
  53.9 0.1 collective-permute-start.15
  54.0 2.3 %collective-permute-start.17 = (f32[64,256]{1,0:T(8,128)S(1)}, f32[64,256]{1,0:T(8,128)S(1)}, u32[]{:S(2)}, u32[]{:S(2)}) collective-permute-start(f32[64,256]{1,0:T(8,128)S(1)} %get-tuple-element.40.refs_0_), channel_id=1, source_target_pairs={{0,8},{4,12},{8,0},{12,4},{1,9},{5,13},{9,1},{13,5},{2,10},{6,14},... | collective-permute-start | bytes 196616 | tf_op jit(solution)/shard_map/ppermute | solution.py:267
  56.3 1.5 %collective-permute-start.19 = (f32[64,256]{1,0:T(8,128)S(1)}, f32[64,256]{1,0:T(8,128)S(1)}, u32[]{:S(2)}, u32[]{:S(2)}) collective-permute-start(f32[64,256]{1,0:T(8,128)S(1)} %get-tuple-element.40.refs_0_), channel_id=1, source_target_pairs={{0,12},{4,0},{8,4},{12,8},{1,13},{5,1},{9,5},{13,9},{2,14},{6,2},{... | collective-permute-start | bytes 196616 | tf_op jit(solution)/shard_map/ppermute | solution.py:267
  57.8 2.2 %collective-permute-done.15.refs_2_ = f32[64,256]{1,0:T(8,128)S(1)} collective-permute-done((f32[64,256]{1,0:T(8,128)S(1)}, f32[64,256]{1,0:T(8,128)S(1)}, u32[]{:S(2)}, u32[]{:S(2)}) %collective-permute-start.15) | collective-permute-done | bytes 65568 | tf_op jit(solution)/shard_map/ppermute | solution.py:267
  60.1 0.5 collective-permute-start.18
  60.6 0.2 collective-permute-done.19.refs_6_
  60.8 1.2 %collective-permute-start.12 = (f32[64,256]{1,0:T(8,128)S(1)}, f32[64,256]{1,0:T(8,128)S(1)}, u32[]{:S(2)}, u32[]{:S(2)}) collective-permute-start(f32[64,256]{1,0:T(8,128)S(1)} %get-tuple-element.38.refs_0_), channel_id=1, source_target_pairs={{0,2},{2,0},{1,3},{3,1},{4,6},{6,4},{5,7},{7,5},{8,10},{10,8},{9,1... | collective-permute-start | bytes 196616 | tf_op jit(solution)/shard_map/ppermute | solution.py:267
  62.0 0.1 collective-permute-done.20.refs_7_
  62.0 10.6 %shard_map.131 = (f32[16,64,128]{2,1,0:T(8,128)S(1)}, f32[16,32,128]{2,1,0:T(8,128)S(1)}, f32[16,32,128]{2,1,0:T(8,128)S(1)}) custom-call(s32[1]{0:T(128)S(6)} %copy.13.count, s32[288]{0:T(512)S(1)} %copy-done.10, s32[288]{0:T(512)S(1)} %copy-done.8, s32[4,6,256]{2,1,0:T(8,128)S(1)} %pad_add_fusion.ids, s32[16,128]{1,0:T(8,128)S(1)} %bitcast.17, ...), custom_call_target="tpu_custom_call" | custom-call | flops 2214592512 | bytes 9437184 | tf_op jit(solution)/shard_map/pallas_call | solution.py:21
  72.6 0.1 collective-permute-start.21
  72.7 0.5 collective-permute-start.11
  73.2 0.1 collective-permute-start.13
  73.2 1.0 collective-permute-done.11.refs_1_
  74.3 0.1 collective-permute-done.13.refs_3_
  74.4 6.6 %shard_map.130 = (f32[16,64,128]{2,1,0:T(8,128)S(1)}, f32[16,32,128]{2,1,0:T(8,128)S(1)}, f32[16,32,128]{2,1,0:T(8,128)S(1)}) custom-call(s32[1]{0:T(128)S(6)} %copy.13.count, s32[288]{0:T(512)S(1)} %copy-done.8, s32[288]{0:T(512)S(1)} %copy-done.10, s32[2,6,256]{2,1,0:T(8,128)S(1)} %pad_add_fusion.1.ids, s32[16,128]{1,0:T(8,128)S(1)} %bitcast.14, ...), custom_call_target="tpu_custom_call" | custom-call | flops 1409286144 | bytes 9437184 | tf_op jit(solution)/shard_map/pallas_call | solution.py:21
  81.0 0.1 collective-permute-start.25
  81.1 0.1 collective-permute-start.22
  81.2 1.4 %collective-permute-done.25.received = f32[16,32,128]{2,1,0:T(8,128)S(1)} collective-permute-done((f32[16,32,128]{2,1,0:T(8,128)S(1)}, f32[16,32,128]{2,1,0:T(8,128)S(1)}, u32[]{:S(2)}, u32[]{:S(2)}) %collective-permute-start.25) | collective-permute-done | bytes 262176 | tf_op jit(solution)/shard_map/ppermute | solution.py:267
  82.6 2.2 %collective-permute-start.26 = (f32[4,32,128]{2,1,0:T(8,128)S(1)}, f32[4,32,128]{2,1,0:T(8,128)S(1)}, u32[]{:S(2)}, u32[]{:S(2)}) collective-permute-start(f32[4,32,128]{2,1,0:T(8,128)S(1)} %get-tuple-element.47), channel_id=1, source_target_pairs={{0,4},{4,8},{8,12},{12,0},{1,5},{5,9},{9,13},{13,1},{2,6},{6,10},{... | collective-permute-start | bytes 196616 | tf_op jit(solution)/shard_map/ppermute | solution.py:267
  84.9 11.4 %collective-permute-start.27 = (f32[4,32,128]{2,1,0:T(8,128)S(1)}, f32[4,32,128]{2,1,0:T(8,128)S(1)}, u32[]{:S(2)}, u32[]{:S(2)}) collective-permute-start(f32[4,32,128]{2,1,0:T(8,128)S(1)} %get-tuple-element.48), channel_id=1, source_target_pairs={{0,8},{4,12},{8,0},{12,4},{1,9},{5,13},{9,1},{13,5},{2,10},{6,14},... | collective-permute-start | bytes 196616 | tf_op jit(solution)/shard_map/ppermute | solution.py:267
  96.3 0.5 collective-permute-start.24
  96.8 1.9 %collective-permute-done.26.refs_1_ = f32[4,32,128]{2,1,0:T(8,128)S(1)} collective-permute-done((f32[4,32,128]{2,1,0:T(8,128)S(1)}, f32[4,32,128]{2,1,0:T(8,128)S(1)}, u32[]{:S(2)}, u32[]{:S(2)}) %collective-permute-start.26) | collective-permute-done | bytes 65568 | tf_op jit(solution)/shard_map/ppermute | solution.py:267
  98.7 2.3 %collective-permute-done.27.refs_2_ = f32[4,32,128]{2,1,0:T(8,128)S(1)} collective-permute-done((f32[4,32,128]{2,1,0:T(8,128)S(1)}, f32[4,32,128]{2,1,0:T(8,128)S(1)}, u32[]{:S(2)}, u32[]{:S(2)}) %collective-permute-start.27) | collective-permute-done | bytes 65568 | tf_op jit(solution)/shard_map/ppermute | solution.py:267
  101.0 0.5 collective-permute-done.28.refs_3_
  101.5 2.3 %collective-permute-start.29 = (f32[4,32,128]{2,1,0:T(8,128)S(1)}, f32[4,32,128]{2,1,0:T(8,128)S(1)}, u32[]{:S(2)}, u32[]{:S(2)}) collective-permute-start(f32[4,32,128]{2,1,0:T(8,128)S(1)} %shard_map.135.refs_0_), channel_id=1, source_target_pairs={{0,12},{4,0},{8,4},{12,8},{1,13},{5,1},{9,5},{13,9},{2,14},{6,2},{... | collective-permute-start | bytes 196616 | tf_op jit(solution)/shard_map/ppermute | solution.py:267
  103.8 0.6 collective-permute-start.30
  104.4 0.1 collective-permute-start.31
  104.5 1.9 %collective-permute-done.29.refs_1_ = f32[4,32,128]{2,1,0:T(8,128)S(1)} collective-permute-done((f32[4,32,128]{2,1,0:T(8,128)S(1)}, f32[4,32,128]{2,1,0:T(8,128)S(1)}, u32[]{:S(2)}, u32[]{:S(2)}) %collective-permute-start.29) | collective-permute-done | bytes 65568 | tf_op jit(solution)/shard_map/ppermute | solution.py:267
  106.4 4.5 %collective-permute-done.30.refs_2_ = f32[4,32,128]{2,1,0:T(8,128)S(1)} collective-permute-done((f32[4,32,128]{2,1,0:T(8,128)S(1)}, f32[4,32,128]{2,1,0:T(8,128)S(1)}, u32[]{:S(2)}, u32[]{:S(2)}) %collective-permute-start.30) | collective-permute-done | bytes 65568 | tf_op jit(solution)/shard_map/ppermute | solution.py:267
  110.9 0.5 collective-permute-start.34
  111.4 0.1 collective-permute-start.35
  111.5 0.7 collective-permute-done.33.refs_5_
  112.1 0.2 collective-permute-done.34.refs_6_
  112.3 0.4 collective-permute-done.35.refs_7_
  112.7 0.9 shard_map.136
  113.5 0.9 shard_map.133
  (55 shorter events, 0.2 us)
Async XLA Ops:
  0.6 20.5 %copy-start = (bf16[64,2048]{1,0:T(8,128)(2,1)S(1)}, bf16[64,2048]{1,0:T(8,128)(2,1)}, u32[]{:S(2)}) copy-start(bf16[64,2048]{1,0:T(8,128)(2,1)} %item_emb.1) | copy-start | bytes 786436
  1.4 10.2 %collective-permute-start = (s32[3,256]{1,0:T(4,128)S(1)}, s32[3,256]{1,0:T(4,128)S(1)}, u32[]{:S(2)}, u32[]{:S(2)}) collective-permute-start(s32[3,256]{1,0:T(4,128)S(1)} %pad_add_fusion.3), channel_id=1, source_target_pairs={{0,1},{1,0},{2,3},{3,2},{4,5},{5,4},{6,7},{7,6},{8,9},{9,8},{10,11... | collective-permute-start | bytes 9224 | tf_op jit(solution)/shard_map/ppermute | solution.py:267
  2.5 1.0 copy-start.1
  3.5 0.7 copy-start.3
  4.2 0.7 copy-start.5
  4.9 0.7 copy-start.7
  5.5 0.7 copy-start.9
  6.2 5.4 %copy-start.11 = (s32[256]{0:T(256)S(1)}, s32[256]{0:T(256)}, u32[]{:S(2)}) copy-start(s32[256]{0:T(256)} %param.21) | copy-start | bytes 3076
  6.2 5.4 %copy-start.12 = (s32[256]{0:T(256)S(1)}, s32[256]{0:T(256)}, u32[]{:S(2)}) copy-start(s32[256]{0:T(256)} %param.20) | copy-start | bytes 3076
  6.2 5.4 %copy-start.13 = (s32[256]{0:T(256)S(1)}, s32[256]{0:T(256)}, u32[]{:S(2)}) copy-start(s32[256]{0:T(256)} %param.19) | copy-start | bytes 3076
  6.2 14.9 %copy-start.4 = (s32[2048]{0:T(1024)S(1)}, s32[2048]{0:T(1024)}, u32[]{:S(2)}) copy-start(s32[2048]{0:T(1024)} %param.13) | copy-start | bytes 24580
  6.2 14.9 %copy-start.6 = (s32[2048]{0:T(1024)S(1)}, s32[2048]{0:T(1024)}, u32[]{:S(2)}) copy-start(s32[2048]{0:T(1024)} %param.14) | copy-start | bytes 24580
  6.2 14.9 %copy-start.8 = (s32[288]{0:T(512)S(1)}, s32[288]{0:T(512)}, u32[]{:S(2)}) copy-start(s32[288]{0:T(512)} %target_ids.7) | copy-start | bytes 3460
  11.6 35.2 %copy-start.2 = (bf16[64,2048]{1,0:T(8,128)(2,1)S(1)}, bf16[64,2048]{1,0:T(8,128)(2,1)}, u32[]{:S(2)}) copy-start(bf16[64,2048]{1,0:T(8,128)(2,1)} %emb.3) | copy-start | bytes 786436
  11.6 50.4 %copy-start.10 = (s32[288]{0:T(512)S(1)}, s32[288]{0:T(512)}, u32[]{:S(2)}) copy-start(s32[288]{0:T(512)} %source_ids.7) | copy-start | bytes 3460
  11.7 16.1 %collective-permute-start.4 = (s32[6,256]{1,0:T(8,128)S(1)}, s32[6,256]{1,0:T(8,128)S(1)}, u32[]{:S(2)}, u32[]{:S(2)}) collective-permute-start(s32[6,256]{1,0:T(8,128)S(1)} %get-tuple-element.51), channel_id=1, source_target_pairs={{0,12},{4,0},{8,4},{12,8},{1,13},{5,1},{9,5},{13,9},{2,14},{6,2},{... | collective-permute-start | bytes 18440 | tf_op jit(solution)/shard_map/ppermute | solution.py:267
  20.5 7.3 %collective-permute-start.5 = (s32[6,256]{1,0:T(8,128)S(1)}, s32[6,256]{1,0:T(8,128)S(1)}, u32[]{:S(2)}, u32[]{:S(2)}) collective-permute-start(s32[6,256]{1,0:T(8,128)S(1)} %get-tuple-element.51), channel_id=1, source_target_pairs={{0,8},{4,12},{8,0},{12,4},{1,9},{5,13},{9,1},{13,5},{2,10},{6,14},... | collective-permute-start | bytes 18440 | tf_op jit(solution)/shard_map/ppermute | solution.py:267
  20.5 7.3 %collective-permute-start.6 = (s32[6,256]{1,0:T(8,128)S(1)}, s32[6,256]{1,0:T(8,128)S(1)}, u32[]{:S(2)}, u32[]{:S(2)}) collective-permute-start(s32[6,256]{1,0:T(8,128)S(1)} %get-tuple-element.51), channel_id=1, source_target_pairs={{0,4},{4,8},{8,12},{12,0},{1,5},{5,9},{9,13},{13,1},{2,6},{6,10},{... | collective-permute-start | bytes 18440 | tf_op jit(solution)/shard_map/ppermute | solution.py:267
  27.7 4.5 %collective-permute-start.1 = (s32[6,256]{1,0:T(8,128)S(1)}, s32[6,256]{1,0:T(8,128)S(1)}, u32[]{:S(2)}, u32[]{:S(2)}) collective-permute-start(s32[6,256]{1,0:T(8,128)S(1)} %get-tuple-element.51), channel_id=1, source_target_pairs={{0,2},{2,0},{1,3},{3,1},{4,6},{6,4},{5,7},{7,5},{8,10},{10,8},{9,1... | collective-permute-start | bytes 18440 | tf_op jit(solution)/shard_map/ppermute | solution.py:267
  32.1 5.1 %collective-permute-start.7 = (f32[4,64,256]{2,1,0:T(8,128)S(1)}, f32[4,64,256]{2,1,0:T(8,128)S(1)}, u32[]{:S(2)}, u32[]{:S(2)}) collective-permute-start(f32[4,64,256]{2,1,0:T(8,128)S(1)} %get-tuple-element.32), channel_id=1, source_target_pairs={{0,1},{1,0},{2,3},{3,2},{4,5},{5,4},{6,7},{7,6},{8,9},{9,8},{10,11... | collective-permute-start | bytes 786440 | tf_op jit(solution)/shard_map/ppermute | solution.py:267
  33.6 1.5 %collective-permute-start.2 = (f32[2,64,256]{2,1,0:T(8,128)S(1)}, f32[2,64,256]{2,1,0:T(8,128)S(1)}, u32[]{:S(2)}, u32[]{:S(2)}) collective-permute-start(f32[2,64,256]{2,1,0:T(8,128)S(1)} %get-tuple-element.27), channel_id=1, source_target_pairs={{0,1},{1,0},{2,3},{3,2},{4,5},{5,4},{6,7},{7,6},{8,9},{9,8},{10,11... | collective-permute-start | bytes 393224 | tf_op jit(solution)/shard_map/ppermute | solution.py:267
  35.1 12.4 %collective-permute-start.3 = (f32[64,256]{1,0:T(8,128)S(1)}, f32[64,256]{1,0:T(8,128)S(1)}, u32[]{:S(2)}, u32[]{:S(2)}) collective-permute-start(f32[64,256]{1,0:T(8,128)S(1)} %get-tuple-element.29), channel_id=1, source_target_pairs={{0,2},{2,0},{1,3},{3,1},{4,6},{6,4},{5,7},{7,5},{8,10},{10,8},{9,1... | collective-permute-start | bytes 196616 | tf_op jit(solution)/shard_map/ppermute | solution.py:267
  37.2 11.4 %collective-permute-start.10 = (f32[64,256]{1,0:T(8,128)S(1)}, f32[64,256]{1,0:T(8,128)S(1)}, u32[]{:S(2)}, u32[]{:S(2)}) collective-permute-start(f32[64,256]{1,0:T(8,128)S(1)} %get-tuple-element.36), channel_id=1, source_target_pairs={{0,12},{4,0},{8,4},{12,8},{1,13},{5,1},{9,5},{13,9},{2,14},{6,2},{... | collective-permute-start | bytes 196616 | tf_op jit(solution)/shard_map/ppermute | solution.py:267
  46.2 6.4 %collective-permute-start.8 = (f32[64,256]{1,0:T(8,128)S(1)}, f32[64,256]{1,0:T(8,128)S(1)}, u32[]{:S(2)}, u32[]{:S(2)}) collective-permute-start(f32[64,256]{1,0:T(8,128)S(1)} %get-tuple-element.34), channel_id=1, source_target_pairs={{0,4},{4,8},{8,12},{12,0},{1,5},{5,9},{9,13},{13,1},{2,6},{6,10},{... | collective-permute-start | bytes 196616 | tf_op jit(solution)/shard_map/ppermute | solution.py:267
  46.2 7.7 %collective-permute-start.9 = (f32[64,256]{1,0:T(8,128)S(1)}, f32[64,256]{1,0:T(8,128)S(1)}, u32[]{:S(2)}, u32[]{:S(2)}) collective-permute-start(f32[64,256]{1,0:T(8,128)S(1)} %get-tuple-element.35), channel_id=1, source_target_pairs={{0,8},{4,12},{8,0},{12,4},{1,9},{5,13},{9,1},{13,5},{2,10},{6,14},... | collective-permute-start | bytes 196616 | tf_op jit(solution)/shard_map/ppermute | solution.py:267
  53.9 6.1 %collective-permute-start.15 = (f32[64,256]{1,0:T(8,128)S(1)}, f32[64,256]{1,0:T(8,128)S(1)}, u32[]{:S(2)}, u32[]{:S(2)}) collective-permute-start(f32[64,256]{1,0:T(8,128)S(1)} %get-tuple-element.40.refs_0_), channel_id=1, source_target_pairs={{0,4},{4,8},{8,12},{12,0},{1,5},{5,9},{9,13},{13,1},{2,6},{6,10},{... | collective-permute-start | bytes 196616 | tf_op jit(solution)/shard_map/ppermute | solution.py:267
  54.0 6.1 %collective-permute-start.17 = (f32[64,256]{1,0:T(8,128)S(1)}, f32[64,256]{1,0:T(8,128)S(1)}, u32[]{:S(2)}, u32[]{:S(2)}) collective-permute-start(f32[64,256]{1,0:T(8,128)S(1)} %get-tuple-element.40.refs_0_), channel_id=1, source_target_pairs={{0,8},{4,12},{8,0},{12,4},{1,9},{5,13},{9,1},{13,5},{2,10},{6,14},... | collective-permute-start | bytes 196616 | tf_op jit(solution)/shard_map/ppermute | solution.py:267
  56.3 4.5 %collective-permute-start.19 = (f32[64,256]{1,0:T(8,128)S(1)}, f32[64,256]{1,0:T(8,128)S(1)}, u32[]{:S(2)}, u32[]{:S(2)}) collective-permute-start(f32[64,256]{1,0:T(8,128)S(1)} %get-tuple-element.40.refs_0_), channel_id=1, source_target_pairs={{0,12},{4,0},{8,4},{12,8},{1,13},{5,1},{9,5},{13,9},{2,14},{6,2},{... | collective-permute-start | bytes 196616 | tf_op jit(solution)/shard_map/ppermute | solution.py:267
  57.8 4.1 %collective-permute-start.14 = (f32[64,256]{1,0:T(8,128)S(1)}, f32[64,256]{1,0:T(8,128)S(1)}, u32[]{:S(2)}, u32[]{:S(2)}) collective-permute-start(f32[64,256]{1,0:T(8,128)S(1)} %get-tuple-element.40.refs_0_), channel_id=1, source_target_pairs={{0,1},{1,0},{2,3},{3,2},{4,5},{5,4},{6,7},{7,6},{8,9},{9,8},{10,11... | collective-permute-start | bytes 196616 | tf_op jit(solution)/shard_map/ppermute | solution.py:267
  60.1 1.9 %collective-permute-start.16 = (f32[64,256]{1,0:T(8,128)S(1)}, f32[64,256]{1,0:T(8,128)S(1)}, u32[]{:S(2)}, u32[]{:S(2)}) collective-permute-start(f32[64,256]{1,0:T(8,128)S(1)} %collective-permute-done.15.refs_2_), channel_id=1, source_target_pairs={{0,1},{1,0},{2,3},{3,2},{4,5},{5,4},{6,7},{7,6},{8,9},{9,8},{10,11... | collective-permute-start | bytes 196616 | tf_op jit(solution)/shard_map/ppermute | solution.py:267
  60.1 1.9 %collective-permute-start.18 = (f32[64,256]{1,0:T(8,128)S(1)}, f32[64,256]{1,0:T(8,128)S(1)}, u32[]{:S(2)}, u32[]{:S(2)}) collective-permute-start(f32[64,256]{1,0:T(8,128)S(1)} %collective-permute-done.17.refs_4_), channel_id=1, source_target_pairs={{0,1},{1,0},{2,3},{3,2},{4,5},{5,4},{6,7},{7,6},{8,9},{9,8},{10,11... | collective-permute-start | bytes 196616 | tf_op jit(solution)/shard_map/ppermute | solution.py:267
  60.8 1.3 %collective-permute-start.20 = (f32[64,256]{1,0:T(8,128)S(1)}, f32[64,256]{1,0:T(8,128)S(1)}, u32[]{:S(2)}, u32[]{:S(2)}) collective-permute-start(f32[64,256]{1,0:T(8,128)S(1)} %collective-permute-done.19.refs_6_), channel_id=1, source_target_pairs={{0,1},{1,0},{2,3},{3,2},{4,5},{5,4},{6,7},{7,6},{8,9},{9,8},{10,11... | collective-permute-start | bytes 196616 | tf_op jit(solution)/shard_map/ppermute | solution.py:267
  60.8 12.4 %collective-permute-start.12 = (f32[64,256]{1,0:T(8,128)S(1)}, f32[64,256]{1,0:T(8,128)S(1)}, u32[]{:S(2)}, u32[]{:S(2)}) collective-permute-start(f32[64,256]{1,0:T(8,128)S(1)} %get-tuple-element.38.refs_0_), channel_id=1, source_target_pairs={{0,2},{2,0},{1,3},{3,1},{4,6},{6,4},{5,7},{7,5},{8,10},{10,8},{9,1... | collective-permute-start | bytes 196616 | tf_op jit(solution)/shard_map/ppermute | solution.py:267
  72.6 8.5 %collective-permute-start.21 = (f32[16,32,128]{2,1,0:T(8,128)S(1)}, f32[16,32,128]{2,1,0:T(8,128)S(1)}, u32[]{:S(2)}, u32[]{:S(2)}) collective-permute-start(f32[16,32,128]{2,1,0:T(8,128)S(1)} %get-tuple-element.42), channel_id=1, source_target_pairs={{0,1},{1,0},{2,3},{3,2},{4,5},{5,4},{6,7},{7,6},{8,9},{9,8},{10,11... | collective-permute-start | bytes 786440 | tf_op jit(solution)/shard_map/ppermute | solution.py:267
  72.7 1.6 %collective-permute-start.11 = (f32[64,256]{1,0:T(8,128)S(1)}, f32[64,256]{1,0:T(8,128)S(1)}, u32[]{:S(2)}, u32[]{:S(2)}) collective-permute-start(f32[64,256]{1,0:T(8,128)S(1)} %get-tuple-element.38.refs_0_), channel_id=1, source_target_pairs={{0,1},{1,0},{2,3},{3,2},{4,5},{5,4},{6,7},{7,6},{8,9},{9,8},{10,11... | collective-permute-start | bytes 196616 | tf_op jit(solution)/shard_map/ppermute | solution.py:267
  73.2 1.3 %collective-permute-start.13 = (f32[64,256]{1,0:T(8,128)S(1)}, f32[64,256]{1,0:T(8,128)S(1)}, u32[]{:S(2)}, u32[]{:S(2)}) collective-permute-start(f32[64,256]{1,0:T(8,128)S(1)} %collective-permute-done.12.refs_2_), channel_id=1, source_target_pairs={{0,1},{1,0},{2,3},{3,2},{4,5},{5,4},{6,7},{7,6},{8,9},{9,8},{10,11... | collective-permute-start | bytes 196616 | tf_op jit(solution)/shard_map/ppermute | solution.py:267
  81.0 1.6 %collective-permute-start.25 = (f32[16,32,128]{2,1,0:T(8,128)S(1)}, f32[16,32,128]{2,1,0:T(8,128)S(1)}, u32[]{:S(2)}, u32[]{:S(2)}) collective-permute-start(f32[16,32,128]{2,1,0:T(8,128)S(1)} %get-tuple-element.45), channel_id=1, source_target_pairs={{0,1},{1,0},{2,3},{3,2},{4,5},{5,4},{6,7},{7,6},{8,9},{9,8},{10,11... | collective-permute-start | bytes 786440 | tf_op jit(solution)/shard_map/ppermute | solution.py:267
  81.1 15.2 %collective-permute-start.22 = (f32[16,32,128]{2,1,0:T(8,128)S(1)}, f32[16,32,128]{2,1,0:T(8,128)S(1)}, u32[]{:S(2)}, u32[]{:S(2)}) collective-permute-start(f32[16,32,128]{2,1,0:T(8,128)S(1)} %shard_map.132.refs_0_), channel_id=1, source_target_pairs={{0,2},{2,0},{1,3},{3,1},{4,6},{6,4},{5,7},{7,5},{8,10},{10,8},{9,1... | collective-permute-start | bytes 786440 | tf_op jit(solution)/shard_map/ppermute | solution.py:267
  82.6 16.1 %collective-permute-start.26 = (f32[4,32,128]{2,1,0:T(8,128)S(1)}, f32[4,32,128]{2,1,0:T(8,128)S(1)}, u32[]{:S(2)}, u32[]{:S(2)}) collective-permute-start(f32[4,32,128]{2,1,0:T(8,128)S(1)} %get-tuple-element.47), channel_id=1, source_target_pairs={{0,4},{4,8},{8,12},{12,0},{1,5},{5,9},{9,13},{13,1},{2,6},{6,10},{... | collective-permute-start | bytes 196616 | tf_op jit(solution)/shard_map/ppermute | solution.py:267
  84.9 16.2 %collective-permute-start.27 = (f32[4,32,128]{2,1,0:T(8,128)S(1)}, f32[4,32,128]{2,1,0:T(8,128)S(1)}, u32[]{:S(2)}, u32[]{:S(2)}) collective-permute-start(f32[4,32,128]{2,1,0:T(8,128)S(1)} %get-tuple-element.48), channel_id=1, source_target_pairs={{0,8},{4,12},{8,0},{12,4},{1,9},{5,13},{9,1},{13,5},{2,10},{6,14},... | collective-permute-start | bytes 196616 | tf_op jit(solution)/shard_map/ppermute | solution.py:267
  96.3 5.2 %collective-permute-start.28 = (f32[4,32,128]{2,1,0:T(8,128)S(1)}, f32[4,32,128]{2,1,0:T(8,128)S(1)}, u32[]{:S(2)}, u32[]{:S(2)}) collective-permute-start(f32[4,32,128]{2,1,0:T(8,128)S(1)} %get-tuple-element.49), channel_id=1, source_target_pairs={{0,12},{4,0},{8,4},{12,8},{1,13},{5,1},{9,5},{13,9},{2,14},{6,2},{... | collective-permute-start | bytes 196616 | tf_op jit(solution)/shard_map/ppermute | solution.py:267
  96.3 17.2 %collective-permute-start.23 = (f32[16,32,128]{2,1,0:T(8,128)S(1)}, f32[16,32,128]{2,1,0:T(8,128)S(1)}, u32[]{:S(2)}, u32[]{:S(2)}) collective-permute-start(f32[16,32,128]{2,1,0:T(8,128)S(1)} %shard_map.132.refs_0_), channel_id=1, source_target_pairs={{0,1},{1,0},{2,3},{3,2},{4,5},{5,4},{6,7},{7,6},{8,9},{9,8},{10,11... | collective-permute-start | bytes 786440 | tf_op jit(solution)/shard_map/ppermute | solution.py:267
  96.3 17.2 %collective-permute-start.24 = (f32[16,32,128]{2,1,0:T(8,128)S(1)}, f32[16,32,128]{2,1,0:T(8,128)S(1)}, u32[]{:S(2)}, u32[]{:S(2)}) collective-permute-start(f32[16,32,128]{2,1,0:T(8,128)S(1)} %collective-permute-done.22.refs_1_), channel_id=1, source_target_pairs={{0,1},{1,0},{2,3},{3,2},{4,5},{5,4},{6,7},{7,6},{8,9},{9,8},{10,11... | collective-permute-start | bytes 786440 | tf_op jit(solution)/shard_map/ppermute | solution.py:267
  101.5 4.8 %collective-permute-start.29 = (f32[4,32,128]{2,1,0:T(8,128)S(1)}, f32[4,32,128]{2,1,0:T(8,128)S(1)}, u32[]{:S(2)}, u32[]{:S(2)}) collective-permute-start(f32[4,32,128]{2,1,0:T(8,128)S(1)} %shard_map.135.refs_0_), channel_id=1, source_target_pairs={{0,12},{4,0},{8,4},{12,8},{1,13},{5,1},{9,5},{13,9},{2,14},{6,2},{... | collective-permute-start | bytes 196616 | tf_op jit(solution)/shard_map/ppermute | solution.py:267
  103.8 7.0 %collective-permute-start.30 = (f32[4,32,128]{2,1,0:T(8,128)S(1)}, f32[4,32,128]{2,1,0:T(8,128)S(1)}, u32[]{:S(2)}, u32[]{:S(2)}) collective-permute-start(f32[4,32,128]{2,1,0:T(8,128)S(1)} %shard_map.135.refs_0_), channel_id=1, source_target_pairs={{0,8},{4,12},{8,0},{12,4},{1,9},{5,13},{9,1},{13,5},{2,10},{6,14},... | collective-permute-start | bytes 196616 | tf_op jit(solution)/shard_map/ppermute | solution.py:267
  104.4 6.5 %collective-permute-start.31 = (f32[4,32,128]{2,1,0:T(8,128)S(1)}, f32[4,32,128]{2,1,0:T(8,128)S(1)}, u32[]{:S(2)}, u32[]{:S(2)}) collective-permute-start(f32[4,32,128]{2,1,0:T(8,128)S(1)} %shard_map.135.refs_0_), channel_id=1, source_target_pairs={{0,4},{4,8},{8,12},{12,0},{1,5},{5,9},{9,13},{13,1},{2,6},{6,10},{... | collective-permute-start | bytes 196616 | tf_op jit(solution)/shard_map/ppermute | solution.py:267
  106.4 5.0 %collective-permute-start.32 = (f32[4,32,128]{2,1,0:T(8,128)S(1)}, f32[4,32,128]{2,1,0:T(8,128)S(1)}, u32[]{:S(2)}, u32[]{:S(2)}) collective-permute-start(f32[4,32,128]{2,1,0:T(8,128)S(1)} %shard_map.135.refs_0_), channel_id=1, source_target_pairs={{0,1},{1,0},{2,3},{3,2},{4,5},{5,4},{6,7},{7,6},{8,9},{9,8},{10,11... | collective-permute-start | bytes 196616 | tf_op jit(solution)/shard_map/ppermute | solution.py:267
  110.9 1.3 %collective-permute-start.33 = (f32[4,32,128]{2,1,0:T(8,128)S(1)}, f32[4,32,128]{2,1,0:T(8,128)S(1)}, u32[]{:S(2)}, u32[]{:S(2)}) collective-permute-start(f32[4,32,128]{2,1,0:T(8,128)S(1)} %collective-permute-done.29.refs_1_), channel_id=1, source_target_pairs={{0,1},{1,0},{2,3},{3,2},{4,5},{5,4},{6,7},{7,6},{8,9},{9,8},{10,11... | collective-permute-start | bytes 196616 | tf_op jit(solution)/shard_map/ppermute | solution.py:267
  110.9 1.4 %collective-permute-start.34 = (f32[4,32,128]{2,1,0:T(8,128)S(1)}, f32[4,32,128]{2,1,0:T(8,128)S(1)}, u32[]{:S(2)}, u32[]{:S(2)}) collective-permute-start(f32[4,32,128]{2,1,0:T(8,128)S(1)} %collective-permute-done.30.refs_2_), channel_id=1, source_target_pairs={{0,1},{1,0},{2,3},{3,2},{4,5},{5,4},{6,7},{7,6},{8,9},{9,8},{10,11... | collective-permute-start | bytes 196616 | tf_op jit(solution)/shard_map/ppermute | solution.py:267
  111.4 1.3 %collective-permute-start.35 = (f32[4,32,128]{2,1,0:T(8,128)S(1)}, f32[4,32,128]{2,1,0:T(8,128)S(1)}, u32[]{:S(2)}, u32[]{:S(2)}) collective-permute-start(f32[4,32,128]{2,1,0:T(8,128)S(1)} %collective-permute-done.31.refs_3_), channel_id=1, source_target_pairs={{0,1},{1,0},{2,3},{3,2},{4,5},{5,4},{6,7},{7,6},{8,9},{9,8},{10,11... | collective-permute-start | bytes 196616 | tf_op jit(solution)/shard_map/ppermute | solution.py:267
where the time goes:
time: 115 us; the launch traced here: 114 us
  starting transfers between devices  46.4 us (40%)
  Pallas kernels  37.1 us (32%)
  waiting for transfers between devices  24.8 us (22%)
  local copies, waits for them, and re-layouts  3.74 us (3%)
  between operations  1.61 us (1%)
    ppermute x36, starting transfers between devices, shift(): lax.ppermute(values, axis, [(i, (i + offset) % count) for i in range(coun...  46.4 us
    pallas_call x15, Pallas kernels, call(): pl.pallas_call(kernel, out_shape=outs, in_specs=specs, out_specs=jax.tree...  37.1 us
    ppermute x36, waiting for transfers between devices, shift(): lax.ppermute(values, axis, [(i, (i + offset) % count) for i in range(coun...  24.8 us
    unnamed x28, local copies, waits for them, and re-layouts  3.74 us
  transfers between devices with their start and end apart: 36, of which 18 were waited for; matrix products, arithmetic and copies ran while one was open for 0% of the time, Pallas kernels for 32%

commit v1 on v0

--- a/solution.py
+++ b/solution.py
@@ -9,15 +9,16 @@
 
 F32 = jnp.float32
 BF16 = jnp.bfloat16
-GROUP = 8
-CHUNK = 32
+PACK = 4
+GROUP = 4
 
 VMEM = pl.BlockSpec(memory_space=pltpu.VMEM)
 SMEM = pl.BlockSpec(memory_space=pltpu.SMEM)
 ANY = pl.BlockSpec(memory_space=pl.ANY)
-
-
-def call(kernel, outs, ins, specs, scratch=(), flops=0, moved=0):
+HBM = pl.BlockSpec(memory_space=pltpu.HBM)
+
+
+def call(kernel, outs, ins, specs, scratch=(), flops=0, moved=0, room=24):
     return pl.pallas_call(
         kernel,
         out_shape=outs,
@@ -25,7 +26,7 @@
         out_specs=jax.tree.map(lambda _: VMEM, outs),
         scratch_shapes=list(scratch),
         cost_estimate=pl.CostEstimate(flops=flops, bytes_accessed=moved, transcendentals=0),
-        compiler_params=pltpu.CompilerParams(vmem_limit_bytes=48 * 1024 * 1024),
+        compiler_params=pltpu.CompilerParams(vmem_limit_bytes=room * 1024 * 1024),
     )(*ins)
 
 
@@ -41,79 +42,106 @@
     return high, middle, low
 
 
-def scale_of(deg_ref, block):
-    return lax.rsqrt(deg_ref[pl.ds(block, 1), :].astype(F32))
-
-
 def hot(ids, start, rows):
     place = lax.broadcasted_iota(jnp.int32, (rows, ids.shape[1]), 0) + start
     return jnp.where(place == ids, 1.0, 0.0)
 
 
-def start_blocks(count, vals, buf, sems):
-    for part in range(vals.shape[0] // CHUNK):
-        @pl.when(part * CHUNK < count)
-        def _():
-            span = pl.ds(part * CHUNK, CHUNK)
-            pltpu.make_async_copy(vals.at[span], buf.at[span], sems.at[part]).start()
-
-
-def multiply_blocks(count, source_ids, target_ids, vals, buf, sems, source, total, across):
-    trash = total.shape[0] - 1
+def sort_slots(keys, sources, count, blocks):
+    lanes = keys.shape[1]
+    rows = 2 * blocks
+    place = lax.broadcasted_iota(jnp.int32, (1, lanes), 1)
+    live = place < count
+    mine = (lax.broadcasted_iota(jnp.int32, (rows, lanes), 0) == keys) & live
+    mine = jnp.where(mine, 1.0, 0.0)
+    earlier = lax.broadcasted_iota(jnp.int32, (lanes, lanes), 0) < lax.broadcasted_iota(
+        jnp.int32, (lanes, lanes), 1)
+    before = jnp.dot(mine.astype(BF16), jnp.where(earlier, 1.0, 0.0).astype(BF16),
+                     preferred_element_type=F32)
+    packs = jnp.floor((jnp.sum(mine, axis=1, keepdims=True) + (PACK - 1)) * (1.0 / PACK))
+    packs = jnp.broadcast_to(packs, (rows, 128))
+    lower = lax.broadcasted_iota(jnp.int32, (rows, rows), 1) < lax.broadcasted_iota(
+        jnp.int32, (rows, rows), 0)
+    first = jnp.dot(jnp.where(lower, 1.0, 0.0).astype(BF16), packs.astype(BF16),
+                    preferred_element_type=F32)
+    position = jnp.sum(mine * (first[:, :1] * PACK + before), axis=0, keepdims=True)
+    position = jnp.where(live, position.astype(jnp.int32), -1)
+    match = lax.broadcasted_iota(jnp.int32, (lanes, lanes), 0) == position
+    row = lax.broadcasted_iota(jnp.int32, (16, lanes), 0)
+    values = jnp.where(row == 0, place // 16, jnp.where(row == 1, place % 16, jnp.where(
+        row == 2, sources, jnp.where(row == 3, keys, jnp.where(row == 4, 1, 0)))))
+    values = jnp.where(live, values, 0).astype(F32)
+    found = lax.dot_general(values.astype(BF16), jnp.where(match, 1.0, 0.0).astype(BF16),
+                            (((1,), (1,)), ((), ())), preferred_element_type=F32)
+    found = found.astype(jnp.int32)
+    valid = found[4:5] > 0
+    total = jnp.broadcast_to(jnp.sum(packs[:, :1], axis=0, keepdims=True), (1, lanes))
+    row = lax.broadcasted_iota(jnp.int32, (8, lanes), 0)
+    slot = found[0:1] * 16 + found[1:2]
+    source = jnp.where(valid, found[2:3], blocks)
+    target = jnp.where(valid, found[3:4], blocks)
+    return jnp.where(row == 0, slot, jnp.where(row == 1, source, jnp.where(
+        row == 2, target, total.astype(jnp.int32))))
+
+
+def multiply_blocks(order, vals, source, total, across):
     total[...] = jnp.zeros_like(total)
     contract = (((1,), (1,)), ((), ())) if across else (((1,), (0,)), ((), ()))
 
     def group(index, _):
-        first = index * GROUP
         targets, terms = [], []
         for step in range(GROUP):
-            slot = first + step
-            live = slot < count
-            origin = jnp.where(live, source_ids[slot], 0)
-            targets.append(jnp.where(live, target_ids[slot], trash))
-            terms.append(
-                lax.dot_general(source[origin], buf[slot], contract, preferred_element_type=F32)
-            )
+            places = [(index * GROUP + step) * PACK + each for each in range(PACK)]
+            left = jnp.concatenate([source[order[1, place]] for place in places], axis=1)
+            right = jnp.concatenate([vals[order[0, place]] for place in places],
+                                    axis=1 if across else 0)
+            targets.append(order[2, places[0]])
+            terms.append(lax.dot_general(left, right, contract, preferred_element_type=F32))
         for target, term in zip(targets, terms):
             total[target] += term
         return 0
 
-    per = CHUNK // GROUP
-    for part in range(vals.shape[0] // CHUNK):
-        @pl.when(part * CHUNK < count)
-        def _():
-            span = pl.ds(part * CHUNK, CHUNK)
-            pltpu.make_async_copy(vals.at[span], buf.at[span], sems.at[part]).wait()
-            groups = jnp.minimum(per, (count - part * CHUNK + GROUP - 1) // GROUP)
-            lax.fori_loop(part * per, part * per + groups, group, 0)
-
-
-def product_scratch(slots, size, width, sources, targets):
-    return [
-        pltpu.VMEM((slots, size, size), BF16),
-        pltpu.SemaphoreType.DMA((slots // CHUNK,)),
-        pltpu.VMEM((sources, width, size), BF16),
-        pltpu.VMEM((targets + 1, width, size), F32),
-    ]
-
-
-def first_pass(across, count, source_ids, target_ids, emb, source_deg, target_deg, vals, out,
-               buf, sems, source, total):
-    start_blocks(count[0], vals, buf, sems)
-    size = source.shape[2]
-    for block in range(source.shape[0]):
-        piece = emb[:, block * size:(block + 1) * size].astype(F32)
-        source[block] = (scale_of(source_deg, block) * piece).astype(BF16)
-    multiply_blocks(count[0], source_ids, target_ids, vals, buf, sems, source, total, across)
-    for block in range(out.shape[0]):
-        out[block] = scale_of(target_deg, block) * total[block]
-
-
-def table_of(blocks, table):
-    count, width, size = blocks.shape
-    for block in range(count):
+    lax.fori_loop(0, (order[3, 0] + GROUP - 1) // GROUP, group, 0)
+
+
+def begin(out):
+    out[...] = jnp.zeros_like(out)
+
+
+def stack_ids(user, positive, negative, after, out):
+    for row, ids in enumerate((user, positive, negative)):
+        out[row:row + 1, :] = ids[...]
+
+
+def prepare(count, rows, columns, user_emb, item_emb, user_deg, item_deg, after,
+            user_source, item_source, user_scale, item_scale, item_order, user_order, keys):
+    live = count[0]
+    slots = rows.shape[0]
+    keys[...] = jnp.zeros_like(keys)
+    keys[0:1, 0:slots] = rows[...].reshape(1, slots)
+    keys[1:2, 0:slots] = columns[...].reshape(1, slots)
+    users, items = keys[0:1, :], keys[1:2, :]
+    item_order[...] = sort_slots(items, users, live, item_scale.shape[0])
+    user_order[...] = sort_slots(users, items, live, user_scale.shape[0])
+    for emb, deg, scale, into in ((user_emb, user_deg, user_scale, user_source),
+                                  (item_emb, item_deg, item_scale, item_source)):
+        scale[...] = lax.rsqrt(deg[...].astype(F32))
+        blocks, size = scale.shape
+        for block in range(blocks):
+            piece = emb[:, block * size:(block + 1) * size].astype(F32)
+            into[block] = (scale[block:block + 1, :] * piece).astype(BF16)
+        into[blocks] = jnp.zeros(into.shape[1:], BF16)
+
+
+def first_pass(across, order, vals, source, total):
+    multiply_blocks(order, vals, source, total, across)
+
+
+def table_of(blocks, scale, table):
+    _, width, size = blocks.shape
+    for block in range(scale.shape[0]):
         span = slice(block * size, (block + 1) * size)
-        for part, piece in enumerate(split3(blocks[block])):
+        for part, piece in enumerate(split3(scale[block:block + 1, :] * blocks[block])):
             table[part * width:(part + 1) * width, span] = piece
 
 
@@ -136,10 +164,10 @@
     return total
 
 
-def gather(rows, blocks, ids, keep, send, table):
+def gather(rows, blocks, scale, ids, keep, send, table):
     width = blocks.shape[1]
     tile = 2 * blocks.shape[2]
-    table_of(blocks, table)
+    table_of(blocks, scale, table)
 
     def one(peer, _):
         keep[peer] = fold(pick(table, ids, peer, rows, tile), width)
@@ -177,14 +205,11 @@
     pushed[...] = slope * user_rows
 
 
-def second_pass(across, rows, chunks, count, source_ids, target_ids, ids, source_deg, target_deg,
-                vals, *refs):
+def second_pass(across, rows, chunks, order, ids, source_scale, target_scale, vals, after, *refs):
     pieces = refs[:len(chunks)]
-    half_grad, keep, send, buf, sems, source, total, table = refs[len(chunks):]
-    start_blocks(count[0], vals, buf, sems)
-    blocks, width, size = source.shape
+    half_grad, keep, send, source, total, table = refs[len(chunks):]
+    blocks, width, size = half_grad.shape
     tile = 2 * size
-    trips = ids.shape[2]
     for place, piece in enumerate(pieces):
         for part, value in enumerate(split3(piece[...])):
             table[place, part * width:(part + 1) * width, :] = value
@@ -203,12 +228,13 @@
             block = (start + offset) // size
             mine = grad[:, offset:offset + size]
             half_grad[block] = 0.5 * mine
-            source[block] = (scale_of(source_deg, block) * mine * 0.5).astype(BF16)
-    multiply_blocks(count[0], source_ids, target_ids, vals, buf, sems, source, total, across)
+            source[block] = (source_scale[block:block + 1, :] * mine * 0.5).astype(BF16)
+    source[blocks] = jnp.zeros((width, size), BF16)
+    multiply_blocks(order, vals, source, total, across)
     me = lax.axis_index("rep")
     half = keep.shape[1]
     for block in range(keep.shape[0]):
-        scale = scale_of(target_deg, block)
+        scale = target_scale[block:block + 1, :]
         keep[block] = scale * total[block, pl.ds(pl.multiple_of(me * half, half), half), :]
         send[block] = scale * total[block, pl.ds(pl.multiple_of((1 - me) * half, half), half), :]
 
@@ -279,39 +305,58 @@
     user_deg = user_deg.reshape(user_blocks, size)
     item_deg = item_deg.reshape(item_blocks, size)
 
-    ids = jnp.stack([trip_user, trip_pos, trip_neg])
-    ids = jnp.concatenate([ids, swap(ids)])
-    ids_user = jnp.stack([ids] + [shift(ids, "item", items, -o) for o in range(1, items)])
-    ids_item = jnp.stack([ids] + [shift(ids, "user", users, -o) for o in range(1, users)])
-
     product_flops = 2 * slots * size * size * width
     product_bytes = slots * size * size * 2
-
-    def first(across, emb, source_deg, target_deg, source_ids, target_ids, sources, targets):
-        return call(
-            functools.partial(first_pass, across),
-            shape(targets, width, size),
-            (block_count, source_ids, target_ids, emb, source_deg, target_deg, block_vals),
-            [SMEM, SMEM, SMEM, VMEM, VMEM, VMEM, ANY],
-            product_scratch(slots, size, width, sources, targets),
-            product_flops, product_bytes,
-        )
-
-    def picked(rows, table, peer_ids):
+    started = call(begin, shape(8, size), (), [], (), 16 * product_flops, product_bytes)
+    ids = call(
+        stack_ids, jax.ShapeDtypeStruct((3, trips), jnp.int32),
+        [each.reshape(1, trips) for each in (trip_user, trip_pos, trip_neg)] + [started],
+        [VMEM, VMEM, VMEM, ANY],
+    )
+    both = jnp.concatenate([ids, swap(ids)])
+    ids_user = jnp.stack([both] + [shift(both, "item", items, -o) for o in range(1, items)])
+    ids_item = jnp.stack([both] + [shift(both, "user", users, -o) for o in range(1, users)])
+
+    lanes = -(-slots // size) * size
+
+    order_shape = jax.ShapeDtypeStruct((8, lanes), jnp.int32)
+    def source_shape(blocks):
+        return jax.ShapeDtypeStruct((blocks + 1, width, size), BF16)
+
+    (user_source, item_source, user_scale, item_scale, item_order, user_order) = call(
+        prepare,
+        [source_shape(user_blocks), source_shape(item_blocks), shape(user_blocks, size),
+         shape(item_blocks, size), order_shape, order_shape],
+        (block_count, block_row, block_col, user_emb, item_emb, user_deg, item_deg, ids),
+        [SMEM, VMEM, VMEM, VMEM, VMEM, VMEM, VMEM, ANY],
+        [pltpu.VMEM((8, lanes), jnp.int32)], product_flops, product_bytes,
+    )
+    item_table = call(
+        functools.partial(first_pass, False), shape(item_blocks + 1, width, size),
+        (item_order, block_vals, user_source), [SMEM, VMEM, VMEM], (),
+        product_flops, product_bytes,
+    )
+    user_table = call(
+        functools.partial(first_pass, True), shape(user_blocks + 1, width, size),
+        (user_order, block_vals, item_source), [SMEM, VMEM, VMEM], (),
+        product_flops, product_bytes,
+    )
+
+    def picked(rows, table, scale, peer_ids):
         peers = peer_ids.shape[0]
-        blocks = table.shape[0]
+        blocks = scale.shape[0]
         return call(
             functools.partial(gather, rows),
             [shape(peers, width, trips)] * 2,
-            (table, peer_ids),
-            [VMEM, VMEM],
+            (table, scale, peer_ids),
+            [VMEM, VMEM, VMEM],
             [pltpu.VMEM((3 * width, blocks * size), BF16)],
             2 * peers * 2 * 3 * width * blocks * size * trips, 4 * blocks * width * size,
         )
 
-    def reduced(rows, table, peer_ids, axis):
+    def reduced(rows, table, scale, peer_ids, axis):
         peers = peer_ids.shape[0]
-        keep, send = picked(rows, table, peer_ids)
+        keep, send = picked(rows, table, scale, peer_ids)
         received = swap(send)
         dealt = call(
             functools.partial(add_split, peers),
@@ -321,12 +366,8 @@
         )
         return [dealt[0]] + [shift(dealt[o], axis, peers, o) for o in range(1, peers)]
 
-    item_table = first(False, user_emb, user_deg, item_deg, block_row, block_col,
-                       user_blocks, item_blocks)
-    item_parts = reduced([1, 2], item_table, ids_item, "user")
-    user_table = first(True, item_emb, item_deg, user_deg, block_col, block_row,
-                       item_blocks, user_blocks)
-    user_parts = reduced([0], user_table, ids_user, "item")
+    item_parts = reduced([1, 2], item_table, item_scale, ids_item, "user")
+    user_parts = reduced([0], user_table, user_scale, ids_user, "item")
     user_base, item_base = call(
         gather_base, [shape(width, trips)] * 2, (user_emb, item_emb, ids_item),
         [VMEM, VMEM, VMEM], (), 4 * width * trips * size * (user_blocks + item_blocks),
@@ -349,26 +390,24 @@
             chunks += [(peers - offset, 0), (peers - offset, 1)]
         return arrays, chunks
 
-    def second(across, rows, own, axis, peer_ids, source_deg, target_deg, source_ids, target_ids,
-               sources, targets):
+    def second(across, rows, own, axis, peer_ids, order, source_scale, target_scale, after):
         arrays, chunks = shared(own, axis, peer_ids.shape[0])
+        sources, targets = source_scale.shape[0], target_scale.shape[0]
         return call(
             functools.partial(second_pass, across, rows, chunks),
             [shape(sources, width, size), shape(targets, half, size), shape(targets, half, size)],
-            (block_count, source_ids, target_ids, peer_ids, source_deg, target_deg, block_vals,
-             *arrays),
-            [SMEM, SMEM, SMEM, VMEM, VMEM, VMEM, ANY] + [VMEM] * len(arrays),
-            product_scratch(slots, size, width, sources, targets)
-            + [pltpu.VMEM((len(arrays), 3 * width, trips), BF16)],
+            (order, peer_ids, source_scale, target_scale, block_vals, after, *arrays),
+            [SMEM, VMEM, VMEM, VMEM, VMEM, ANY] + [VMEM] * len(arrays),
+            [pltpu.VMEM((sources + 1, width, size), BF16),
+             pltpu.VMEM((targets + 1, width, size), F32),
+             pltpu.VMEM((len(arrays), 3 * width, trips), BF16)],
             product_flops + 2 * len(arrays) * 3 * width * trips * sources * size, product_bytes,
         )
 
     user_half_grad, item_keep, item_send = second(
-        False, [0], pieces, "item", ids_user, user_deg, item_deg, block_row, block_col,
-        user_blocks, item_blocks)
+        False, [0], pieces, "item", ids_user, item_order, user_scale, item_scale, pieces)
     item_half_grad, user_keep, user_send = second(
-        True, [1, 2], pushed, "user", ids_item, item_deg, user_deg, block_col, block_row,
-        item_blocks, user_blocks)
+        True, [1, 2], pushed, "user", ids_item, user_order, item_scale, user_scale, item_send)
 
     per = item_blocks // users
     dealt = call(

time: 115 us -> 91.9 us (0.80)
  Pallas kernels: 37.1 us -> 23.8 us
  starting transfers between devices: 46.4 us -> 36.9 us
  local copies, waits for them, and re-layouts: 3.74 us -> 1.24 us
  waiting for transfers between devices: 24.8 us -> 27.1 us
    pallas_call x15 -> x18, Pallas kernels: 37.1 us -> 23.8 us  [call(): pl.pallas_call(kernel, out_shape=outs, in_specs=specs, out_specs=jax.tree...]
    ppermute x36, starting transfers between devices: 46.4 us -> 36.9 us  [shift(): lax.ppermute(values, axis, [(i, (i + offset) % count) for i in range(coun...]
    unnamed x28 -> x20, local copies, waits for them, and re-layouts: 3.74 us -> 1.24 us
    ppermute x36, waiting for transfers between devices: 24.8 us -> 27.1 us  [shift(): lax.ppermute(values, axis, [(i, (i + offset) % count) for i in range(coun...]
  transfers between devices with their start and end apart: 36 -> 36, of which waited for: 18 -> 17; matrix products, arithmetic and copies ran while one was open for 0% -> 0% of each run, Pallas kernels for 32% -> 18%
where the time goes in v1:
time: 91.9 us; the launch traced here: 91.2 us
  starting transfers between devices  36.9 us (40%)
  waiting for transfers between devices  27.1 us (29%)
  Pallas kernels  23.8 us (26%)
  between operations  2.22 us (2%)
  local copies, waits for them, and re-layouts  1.24 us (1%)
    ppermute x36, starting transfers between devices, shift(): lax.ppermute(values, axis, [(i, (i + offset) % count) for i in range(coun...  36.9 us
    ppermute x36, waiting for transfers between devices, shift(): lax.ppermute(values, axis, [(i, (i + offset) % count) for i in range(coun...  27.1 us
    pallas_call x18, Pallas kernels, call(): pl.pallas_call(kernel, out_shape=outs, in_specs=specs, out_specs=jax.tree...  23.8 us
  transfers between devices with their start and end apart: 36, of which 17 were waited for; matrix products, arithmetic and copies ran while one was open for 0% of the time, Pallas kernels for 18%

profile of v1, /device:TPU:0, one launch (start us, length us, event | category | flops | bytes accessed | tf_op | source)
XLA Modules:
  0.0 91.2 jit_solution(11663520407533841237)
XLA Ops:
  0.7 0.6 copy-done.3
  1.3 0.0 copy-done.2
  1.3 0.0 copy-done.1
  1.3 0.5 collective-permute-start
  3.1 0.9 %shard_map.124 = (bf16[17,64,128]{2,1,0:T(8,128)(2,1)S(1)}, bf16[17,64,128]{2,1,0:T(8,128)(2,1)S(1)}, f32[16,128]{1,0:T(8,128)S(1)}, f32[16,128]{1,0:T(8,128)S(1...) custom-call(s32[1]{0:T(128)S(6)} %copy.13.count, s32[288]{0:T(512)S(1)} %copy-done.8, s32[288]{0:T(512)S(1)} %copy-done.9, ...), custom_call_target="tpu_custom_call" | custom-call | flops 603979776 | bytes 9437184 | tf_op jit(solution)/shard_map/pallas_call | solution.py:22
  4.0 0.6 copy-done
  4.6 2.6 %shard_map.125.blocks = f32[17,64,128]{2,1,0:T(8,128)S(1)} custom-call(s32[8,384]{1,0:T(8,128)S(1)} %get-tuple-element.35.order, bf16[288,128,128]{2,1,0:T(8,128)(2,1)S(1)} %copy-done, bf16[17,64,128]{2,1,0:T(8,128)(2,1)S(1)} %get-tuple-element.36.source), custom_call_target="tpu_custom_call" | custom-call | flops 603979776 | bytes 9437184 | tf_op jit(solution)/shard_map/pallas_call | solution.py:22
  7.2 0.0 collective-permute-done
  7.3 4.7 %collective-permute-start.5 = (s32[6,256]{1,0:T(8,128)S(1)}, s32[6,256]{1,0:T(8,128)S(1)}, u32[]{:S(2)}, u32[]{:S(2)}) collective-permute-start(s32[6,256]{1,0:T(8,128)S(1)} %get-tuple-element.63), channel_id=1, source_target_pairs={{0,8},{4,12},{8,0},{12,4},{1,9},{5,13},{9,1},{13,5},{2,10},{6,14},... | collective-permute-start | bytes 18440 | tf_op jit(solution)/shard_map/ppermute | solution.py:293
  12.0 4.7 %collective-permute-start.4 = (s32[6,256]{1,0:T(8,128)S(1)}, s32[6,256]{1,0:T(8,128)S(1)}, u32[]{:S(2)}, u32[]{:S(2)}) collective-permute-start(s32[6,256]{1,0:T(8,128)S(1)} %get-tuple-element.63), channel_id=1, source_target_pairs={{0,12},{4,0},{8,4},{12,8},{1,13},{5,1},{9,5},{13,9},{2,14},{6,2},{... | collective-permute-start | bytes 18440 | tf_op jit(solution)/shard_map/ppermute | solution.py:293
  16.7 0.5 collective-permute-start.6
  17.2 1.9 %shard_map.129.blocks = f32[17,64,128]{2,1,0:T(8,128)S(1)} custom-call(s32[8,384]{1,0:T(8,128)S(1)} %get-tuple-element.32.order, bf16[288,128,128]{2,1,0:T(8,128)(2,1)S(1)} %copy-done, bf16[17,64,128]{2,1,0:T(8,128)(2,1)S(1)} %get-tuple-element.42.source), custom_call_target="tpu_custom_call" | custom-call | flops 603979776 | bytes 9437184 | tf_op jit(solution)/shard_map/pallas_call | solution.py:22
  19.1 0.1 collective-permute-start.1
  19.2 0.0 collective-permute-done.5
  19.2 0.0 collective-permute-done.4
  19.2 2.9 %collective-permute-done.6 = s32[6,256]{1,0:T(8,128)S(1)} collective-permute-done((s32[6,256]{1,0:T(8,128)S(1)}, s32[6,256]{1,0:T(8,128)S(1)}, u32[]{:S(2)}, u32[]{:S(2)}) %collective-permute-start.6) | collective-permute-done | bytes 6176 | tf_op jit(solution)/shard_map/ppermute | solution.py:293
  22.2 4.3 %shard_map.130 = (f32[4,64,256]{2,1,0:T(8,128)S(1)}, f32[4,64,256]{2,1,0:T(8,128)S(1)}) custom-call(f32[17,64,128]{2,1,0:T(8,128)S(1)} %shard_map.129.blocks, f32[16,128]{1,0:T(8,128)S(1)} %get-tuple-element.34.scale.target_scale.source_scale, s32[4,6,256]{2,1,0:T(8,128)S(1)} %pad_add_fusion.ids), custom_call_target="tpu_custom_call" | custom-call | flops 1610612736 | bytes 524288 | tf_op jit(solution)/shard_map/pallas_call | solution.py:22
  26.4 0.1 collective-permute-start.7
  26.5 1.4 %shard_map.126 = (f32[2,64,256]{2,1,0:T(8,128)S(1)}, f32[2,64,256]{2,1,0:T(8,128)S(1)}) custom-call(f32[17,64,128]{2,1,0:T(8,128)S(1)} %shard_map.125.blocks, f32[16,128]{1,0:T(8,128)S(1)} %get-tuple-element.33.scale.source_scale.target_scale, s32[2,6,256]{2,1,0:T(8,128)S(1)} %pad_add_fusion.1.ids), custom_call_target="tpu_custom_call" | custom-call | flops 805306368 | bytes 524288 | tf_op jit(solution)/shard_map/pallas_call | solution.py:22
  27.9 0.5 collective-permute-start.2
  28.4 1.0 %collective-permute-done.2.received = f32[2,64,256]{2,1,0:T(8,128)S(1)} collective-permute-done((f32[2,64,256]{2,1,0:T(8,128)S(1)}, f32[2,64,256]{2,1,0:T(8,128)S(1)}, u32[]{:S(2)}, u32[]{:S(2)}) %collective-permute-start.2) | collective-permute-done | bytes 131104 | tf_op jit(solution)/shard_map/ppermute | solution.py:293
  29.4 0.1 collective-permute-start.3
  29.5 0.0 collective-permute-done.7.received
  29.6 2.1 %collective-permute-start.8 = (f32[64,256]{1,0:T(8,128)S(1)}, f32[64,256]{1,0:T(8,128)S(1)}, u32[]{:S(2)}, u32[]{:S(2)}) collective-permute-start(f32[64,256]{1,0:T(8,128)S(1)} %get-tuple-element.46), channel_id=1, source_target_pairs={{0,4},{4,8},{8,12},{12,0},{1,5},{5,9},{9,13},{13,1},{2,6},{6,10},{... | collective-permute-start | bytes 196616 | tf_op jit(solution)/shard_map/ppermute | solution.py:293
  31.6 4.4 %collective-permute-start.9 = (f32[64,256]{1,0:T(8,128)S(1)}, f32[64,256]{1,0:T(8,128)S(1)}, u32[]{:S(2)}, u32[]{:S(2)}) collective-permute-start(f32[64,256]{1,0:T(8,128)S(1)} %get-tuple-element.47), channel_id=1, source_target_pairs={{0,8},{4,12},{8,0},{12,4},{1,9},{5,13},{9,1},{13,5},{2,10},{6,14},... | collective-permute-start | bytes 196616 | tf_op jit(solution)/shard_map/ppermute | solution.py:293
  36.1 0.0 collective-permute-start.10
  36.1 0.6 shard_map.128
  36.7 0.0 collective-permute-done.3.refs_1_
  36.7 1.8 %collective-permute-done.8.refs_4_ = f32[64,256]{1,0:T(8,128)S(1)} collective-permute-done((f32[64,256]{1,0:T(8,128)S(1)}, f32[64,256]{1,0:T(8,128)S(1)}, u32[]{:S(2)}, u32[]{:S(2)}) %collective-permute-start.8) | collective-permute-done | bytes 65568 | tf_op jit(solution)/shard_map/ppermute | solution.py:293
  38.5 2.3 %collective-permute-done.9.refs_5_ = f32[64,256]{1,0:T(8,128)S(1)} collective-permute-done((f32[64,256]{1,0:T(8,128)S(1)}, f32[64,256]{1,0:T(8,128)S(1)}, u32[]{:S(2)}, u32[]{:S(2)}) %collective-permute-start.9) | collective-permute-done | bytes 65568 | tf_op jit(solution)/shard_map/ppermute | solution.py:293
  40.7 0.5 collective-permute-done.10.refs_6_
  41.2 0.1 shard_map.132
  41.3 0.4 collective-permute-start.12
  41.7 2.2 %collective-permute-start.19 = (f32[64,256]{1,0:T(8,128)S(1)}, f32[64,256]{1,0:T(8,128)S(1)}, u32[]{:S(2)}, u32[]{:S(2)}) collective-permute-start(f32[64,256]{1,0:T(8,128)S(1)} %get-tuple-element.53.refs_0_), channel_id=1, source_target_pairs={{0,12},{4,0},{8,4},{12,8},{1,13},{5,1},{9,5},{13,9},{2,14},{6,2},{... | collective-permute-start | bytes 196616 | tf_op jit(solution)/shard_map/ppermute | solution.py:293
  43.8 0.7 collective-permute-start.17
  44.6 1.1 %collective-permute-done.12.refs_2_ = f32[64,256]{1,0:T(8,128)S(1)} collective-permute-done((f32[64,256]{1,0:T(8,128)S(1)}, f32[64,256]{1,0:T(8,128)S(1)}, u32[]{:S(2)}, u32[]{:S(2)}) %collective-permute-start.12) | collective-permute-done | bytes 65568 | tf_op jit(solution)/shard_map/ppermute | solution.py:293
  45.6 0.5 collective-permute-start.14
  46.1 0.2 collective-permute-done.19.refs_6_
  46.3 4.9 %collective-permute-done.17.refs_4_ = f32[64,256]{1,0:T(8,128)S(1)} collective-permute-done((f32[64,256]{1,0:T(8,128)S(1)}, f32[64,256]{1,0:T(8,128)S(1)}, u32[]{:S(2)}, u32[]{:S(2)}) %collective-permute-start.17) | collective-permute-done | bytes 65568 | tf_op jit(solution)/shard_map/ppermute | solution.py:293
  51.2 0.1 collective-permute-start.18
  51.3 0.4 collective-permute-start.16
  51.7 3.5 %shard_map.133 = (f32[16,64,128]{2,1,0:T(8,128)S(1)}, f32[16,32,128]{2,1,0:T(8,128)S(1)}, f32[16,32,128]{2,1,0:T(8,128)S(1)}) custom-call(s32[8,384]{1,0:T(8,128)S(1)} %get-tuple-element.32.order, s32[2,6,256]{2,1,0:T(8,128)S(1)} %pad_add_fusion.1.ids, f32[16,128]{1,0:T(8,128)S(1)} %get-tuple-element.33.scale.source_scale.target_scale, ...), custom_call_target="tpu_custom_call" | custom-call | flops 1409286144 | bytes 9437184 | tf_op jit(solution)/shard_map/pallas_call | solution.py:22
  55.3 6.7 %shard_map.134 = (f32[16,64,128]{2,1,0:T(8,128)S(1)}, f32[16,32,128]{2,1,0:T(8,128)S(1)}, f32[16,32,128]{2,1,0:T(8,128)S(1)}) custom-call(s32[8,384]{1,0:T(8,128)S(1)} %get-tuple-element.35.order, s32[4,6,256]{2,1,0:T(8,128)S(1)} %pad_add_fusion.ids, f32[16,128]{1,0:T(8,128)S(1)} %get-tuple-element.34.scale.target_scale.source_scale, ...), custom_call_target="tpu_custom_call" | custom-call | flops 2214592512 | bytes 9437184 | tf_op jit(solution)/shard_map/pallas_call | solution.py:22
  62.0 0.1 collective-permute-start.21
  62.1 0.5 collective-permute-start.25
  62.6 1.0 %collective-permute-done.21.received = f32[16,32,128]{2,1,0:T(8,128)S(1)} collective-permute-done((f32[16,32,128]{2,1,0:T(8,128)S(1)}, f32[16,32,128]{2,1,0:T(8,128)S(1)}, u32[]{:S(2)}, u32[]{:S(2)}) %collective-permute-start.21) | collective-permute-done | bytes 262176 | tf_op jit(solution)/shard_map/ppermute | solution.py:293
  63.6 3.8 %collective-permute-start.22 = (f32[16,32,128]{2,1,0:T(8,128)S(1)}, f32[16,32,128]{2,1,0:T(8,128)S(1)}, u32[]{:S(2)}, u32[]{:S(2)}) collective-permute-start(f32[16,32,128]{2,1,0:T(8,128)S(1)} %shard_map.135.refs_0_), channel_id=1, source_target_pairs={{0,2},{2,0},{1,3},{3,1},{4,6},{6,4},{5,7},{7,5},{8,10},{10,8},{9,1... | collective-permute-start | bytes 786440 | tf_op jit(solution)/shard_map/ppermute | solution.py:293
  67.5 0.1 collective-permute-start.26
  67.5 6.0 %collective-permute-start.27 = (f32[4,32,128]{2,1,0:T(8,128)S(1)}, f32[4,32,128]{2,1,0:T(8,128)S(1)}, u32[]{:S(2)}, u32[]{:S(2)}) collective-permute-start(f32[4,32,128]{2,1,0:T(8,128)S(1)} %get-tuple-element.60), channel_id=1, source_target_pairs={{0,8},{4,12},{8,0},{12,4},{1,9},{5,13},{9,1},{13,5},{2,10},{6,14},... | collective-permute-start | bytes 196616 | tf_op jit(solution)/shard_map/ppermute | solution.py:293
  73.6 0.7 collective-permute-done.22.refs_1_
  74.3 1.7 %collective-permute-done.26.refs_1_ = f32[4,32,128]{2,1,0:T(8,128)S(1)} collective-permute-done((f32[4,32,128]{2,1,0:T(8,128)S(1)}, f32[4,32,128]{2,1,0:T(8,128)S(1)}, u32[]{:S(2)}, u32[]{:S(2)}) %collective-permute-start.26) | collective-permute-done | bytes 65568 | tf_op jit(solution)/shard_map/ppermute | solution.py:293
  76.0 2.3 %collective-permute-done.27.refs_2_ = f32[4,32,128]{2,1,0:T(8,128)S(1)} collective-permute-done((f32[4,32,128]{2,1,0:T(8,128)S(1)}, f32[4,32,128]{2,1,0:T(8,128)S(1)}, u32[]{:S(2)}, u32[]{:S(2)}) %collective-permute-start.27) | collective-permute-done | bytes 65568 | tf_op jit(solution)/shard_map/ppermute | solution.py:293
  78.3 0.5 collective-permute-done.28.refs_3_
  78.8 0.1 collective-permute-start.32
  78.9 1.4 %collective-permute-start.31 = (f32[4,32,128]{2,1,0:T(8,128)S(1)}, f32[4,32,128]{2,1,0:T(8,128)S(1)}, u32[]{:S(2)}, u32[]{:S(2)}) collective-permute-start(f32[4,32,128]{2,1,0:T(8,128)S(1)} %shard_map.138.refs_0_), channel_id=1, source_target_pairs={{0,4},{4,8},{8,12},{12,0},{1,5},{5,9},{9,13},{13,1},{2,6},{6,10},{... | collective-permute-start | bytes 196616 | tf_op jit(solution)/shard_map/ppermute | solution.py:293
  80.3 1.8 %collective-permute-start.30 = (f32[4,32,128]{2,1,0:T(8,128)S(1)}, f32[4,32,128]{2,1,0:T(8,128)S(1)}, u32[]{:S(2)}, u32[]{:S(2)}) collective-permute-start(f32[4,32,128]{2,1,0:T(8,128)S(1)} %shard_map.138.refs_0_), channel_id=1, source_target_pairs={{0,8},{4,12},{8,0},{12,4},{1,9},{5,13},{9,1},{13,5},{2,10},{6,14},... | collective-permute-start | bytes 196616 | tf_op jit(solution)/shard_map/ppermute | solution.py:293
  82.2 0.6 collective-permute-start.29
  82.8 3.0 %collective-permute-done.31.refs_3_ = f32[4,32,128]{2,1,0:T(8,128)S(1)} collective-permute-done((f32[4,32,128]{2,1,0:T(8,128)S(1)}, f32[4,32,128]{2,1,0:T(8,128)S(1)}, u32[]{:S(2)}, u32[]{:S(2)}) %collective-permute-start.31) | collective-permute-done | bytes 65568 | tf_op jit(solution)/shard_map/ppermute | solution.py:293
  85.7 2.3 %collective-permute-done.30.refs_2_ = f32[4,32,128]{2,1,0:T(8,128)S(1)} collective-permute-done((f32[4,32,128]{2,1,0:T(8,128)S(1)}, f32[4,32,128]{2,1,0:T(8,128)S(1)}, u32[]{:S(2)}, u32[]{:S(2)}) %collective-permute-start.30) | collective-permute-done | bytes 65568 | tf_op jit(solution)/shard_map/ppermute | solution.py:293
  88.1 0.5 collective-permute-start.33
  88.6 0.7 collective-permute-done.34.refs_6_
  89.3 0.2 collective-permute-done.33.refs_5_
  89.5 0.9 shard_map.139
  90.4 0.9 shard_map.136
  (49 shorter events, 0.2 us)
Async XLA Ops:
  0.6 0.7 copy-start.3
  0.6 0.7 copy-start.2
  0.7 0.7 copy-start.1
  0.7 2.4 %copy-start.5 = (bf16[64,2048]{1,0:T(8,128)(2,1)S(1)}, bf16[64,2048]{1,0:T(8,128)(2,1)}, u32[]{:S(2)}) copy-start(bf16[64,2048]{1,0:T(8,128)(2,1)} %item_emb.3) | copy-start | bytes 786436
  0.7 2.4 %copy-start.4 = (bf16[64,2048]{1,0:T(8,128)(2,1)S(1)}, bf16[64,2048]{1,0:T(8,128)(2,1)}, u32[]{:S(2)}) copy-start(bf16[64,2048]{1,0:T(8,128)(2,1)} %user_emb.3) | copy-start | bytes 786436
  0.7 2.4 %copy-start.9 = (s32[288]{0:T(512)S(1)}, s32[288]{0:T(512)}, u32[]{:S(2)}) copy-start(s32[288]{0:T(512)} %columns.1) | copy-start | bytes 3460
  0.7 2.4 %copy-start.8 = (s32[288]{0:T(512)S(1)}, s32[288]{0:T(512)}, u32[]{:S(2)}) copy-start(s32[288]{0:T(512)} %rows.1) | copy-start | bytes 3460
  0.7 2.4 %copy-start.7 = (s32[2048]{0:T(1024)S(1)}, s32[2048]{0:T(1024)}, u32[]{:S(2)}) copy-start(s32[2048]{0:T(1024)} %param.14) | copy-start | bytes 24580
  0.7 2.4 %copy-start.6 = (s32[2048]{0:T(1024)S(1)}, s32[2048]{0:T(1024)}, u32[]{:S(2)}) copy-start(s32[2048]{0:T(1024)} %param.13) | copy-start | bytes 24580
  0.7 3.9 %copy-start = (bf16[288,128,128]{2,1,0:T(8,128)(2,1)S(1)}, bf16[288,128,128]{2,1,0:T(8,128)(2,1)}, u32[]{:S(2)}) copy-start(bf16[288,128,128]{2,1,0:T(8,128)(2,1)} %vals.7) | copy-start | bytes 28311556
  1.3 5.9 %collective-permute-start = (s32[3,256]{1,0:T(4,128)S(1)}, s32[3,256]{1,0:T(4,128)S(1)}, u32[]{:S(2)}, u32[]{:S(2)}) collective-permute-start(s32[3,256]{1,0:T(4,128)S(1)} %shard_map.123.after), channel_id=1, source_target_pairs={{0,1},{1,0},{2,3},{3,2},{4,5},{5,4},{6,7},{7,6},{8,9},{9,8},{10,11... | collective-permute-start | bytes 9224 | tf_op jit(solution)/shard_map/ppermute | solution.py:293
  7.3 11.9 %collective-permute-start.5 = (s32[6,256]{1,0:T(8,128)S(1)}, s32[6,256]{1,0:T(8,128)S(1)}, u32[]{:S(2)}, u32[]{:S(2)}) collective-permute-start(s32[6,256]{1,0:T(8,128)S(1)} %get-tuple-element.63), channel_id=1, source_target_pairs={{0,8},{4,12},{8,0},{12,4},{1,9},{5,13},{9,1},{13,5},{2,10},{6,14},... | collective-permute-start | bytes 18440 | tf_op jit(solution)/shard_map/ppermute | solution.py:293
  12.0 7.2 %collective-permute-start.4 = (s32[6,256]{1,0:T(8,128)S(1)}, s32[6,256]{1,0:T(8,128)S(1)}, u32[]{:S(2)}, u32[]{:S(2)}) collective-permute-start(s32[6,256]{1,0:T(8,128)S(1)} %get-tuple-element.63), channel_id=1, source_target_pairs={{0,12},{4,0},{8,4},{12,8},{1,13},{5,1},{9,5},{13,9},{2,14},{6,2},{... | collective-permute-start | bytes 18440 | tf_op jit(solution)/shard_map/ppermute | solution.py:293
  16.7 5.4 %collective-permute-start.6 = (s32[6,256]{1,0:T(8,128)S(1)}, s32[6,256]{1,0:T(8,128)S(1)}, u32[]{:S(2)}, u32[]{:S(2)}) collective-permute-start(s32[6,256]{1,0:T(8,128)S(1)} %get-tuple-element.63), channel_id=1, source_target_pairs={{0,4},{4,8},{8,12},{12,0},{1,5},{5,9},{9,13},{13,1},{2,6},{6,10},{... | collective-permute-start | bytes 18440 | tf_op jit(solution)/shard_map/ppermute | solution.py:293
  19.1 7.4 %collective-permute-start.1 = (s32[6,256]{1,0:T(8,128)S(1)}, s32[6,256]{1,0:T(8,128)S(1)}, u32[]{:S(2)}, u32[]{:S(2)}) collective-permute-start(s32[6,256]{1,0:T(8,128)S(1)} %get-tuple-element.63), channel_id=1, source_target_pairs={{0,2},{2,0},{1,3},{3,1},{4,6},{6,4},{5,7},{7,5},{8,10},{10,8},{9,1... | collective-permute-start | bytes 18440 | tf_op jit(solution)/shard_map/ppermute | solution.py:293
  26.4 3.1 %collective-permute-start.7 = (f32[4,64,256]{2,1,0:T(8,128)S(1)}, f32[4,64,256]{2,1,0:T(8,128)S(1)}, u32[]{:S(2)}, u32[]{:S(2)}) collective-permute-start(f32[4,64,256]{2,1,0:T(8,128)S(1)} %get-tuple-element.44), channel_id=1, source_target_pairs={{0,1},{1,0},{2,3},{3,2},{4,5},{5,4},{6,7},{7,6},{8,9},{9,8},{10,11... | collective-permute-start | bytes 786440 | tf_op jit(solution)/shard_map/ppermute | solution.py:293
  27.9 1.5 %collective-permute-start.2 = (f32[2,64,256]{2,1,0:T(8,128)S(1)}, f32[2,64,256]{2,1,0:T(8,128)S(1)}, u32[]{:S(2)}, u32[]{:S(2)}) collective-permute-start(f32[2,64,256]{2,1,0:T(8,128)S(1)} %get-tuple-element.38), channel_id=1, source_target_pairs={{0,1},{1,0},{2,3},{3,2},{4,5},{5,4},{6,7},{7,6},{8,9},{9,8},{10,11... | collective-permute-start | bytes 393224 | tf_op jit(solution)/shard_map/ppermute | solution.py:293
  29.4 7.3 %collective-permute-start.3 = (f32[64,256]{1,0:T(8,128)S(1)}, f32[64,256]{1,0:T(8,128)S(1)}, u32[]{:S(2)}, u32[]{:S(2)}) collective-permute-start(f32[64,256]{1,0:T(8,128)S(1)} %get-tuple-element.40), channel_id=1, source_target_pairs={{0,2},{2,0},{1,3},{3,1},{4,6},{6,4},{5,7},{7,5},{8,10},{10,8},{9,1... | collective-permute-start | bytes 196616 | tf_op jit(solution)/shard_map/ppermute | solution.py:293
  29.6 8.9 %collective-permute-start.8 = (f32[64,256]{1,0:T(8,128)S(1)}, f32[64,256]{1,0:T(8,128)S(1)}, u32[]{:S(2)}, u32[]{:S(2)}) collective-permute-start(f32[64,256]{1,0:T(8,128)S(1)} %get-tuple-element.46), channel_id=1, source_target_pairs={{0,4},{4,8},{8,12},{12,0},{1,5},{5,9},{9,13},{13,1},{2,6},{6,10},{... | collective-permute-start | bytes 196616 | tf_op jit(solution)/shard_map/ppermute | solution.py:293
  31.6 9.1 %collective-permute-start.9 = (f32[64,256]{1,0:T(8,128)S(1)}, f32[64,256]{1,0:T(8,128)S(1)}, u32[]{:S(2)}, u32[]{:S(2)}) collective-permute-start(f32[64,256]{1,0:T(8,128)S(1)} %get-tuple-element.47), channel_id=1, source_target_pairs={{0,8},{4,12},{8,0},{12,4},{1,9},{5,13},{9,1},{13,5},{2,10},{6,14},... | collective-permute-start | bytes 196616 | tf_op jit(solution)/shard_map/ppermute | solution.py:293
  36.1 5.2 %collective-permute-start.10 = (f32[64,256]{1,0:T(8,128)S(1)}, f32[64,256]{1,0:T(8,128)S(1)}, u32[]{:S(2)}, u32[]{:S(2)}) collective-permute-start(f32[64,256]{1,0:T(8,128)S(1)} %get-tuple-element.48), channel_id=1, source_target_pairs={{0,12},{4,0},{8,4},{12,8},{1,13},{5,1},{9,5},{13,9},{2,14},{6,2},{... | collective-permute-start | bytes 196616 | tf_op jit(solution)/shard_map/ppermute | solution.py:293
  41.3 4.3 %collective-permute-start.12 = (f32[64,256]{1,0:T(8,128)S(1)}, f32[64,256]{1,0:T(8,128)S(1)}, u32[]{:S(2)}, u32[]{:S(2)}) collective-permute-start(f32[64,256]{1,0:T(8,128)S(1)} %get-tuple-element.50.after.refs_0_), channel_id=1, source_target_pairs={{0,2},{2,0},{1,3},{3,1},{4,6},{6,4},{5,7},{7,5},{8,10},{10,8},{9,1... | collective-permute-start | bytes 196616 | tf_op jit(solution)/shard_map/ppermute | solution.py:293
  41.7 3.9 %collective-permute-start.11 = (f32[64,256]{1,0:T(8,128)S(1)}, f32[64,256]{1,0:T(8,128)S(1)}, u32[]{:S(2)}, u32[]{:S(2)}) collective-permute-start(f32[64,256]{1,0:T(8,128)S(1)} %get-tuple-element.50.after.refs_0_), channel_id=1, source_target_pairs={{0,1},{1,0},{2,3},{3,2},{4,5},{5,4},{6,7},{7,6},{8,9},{9,8},{10,11... | collective-permute-start | bytes 196616 | tf_op jit(solution)/shard_map/ppermute | solution.py:293
  41.7 4.6 %collective-permute-start.19 = (f32[64,256]{1,0:T(8,128)S(1)}, f32[64,256]{1,0:T(8,128)S(1)}, u32[]{:S(2)}, u32[]{:S(2)}) collective-permute-start(f32[64,256]{1,0:T(8,128)S(1)} %get-tuple-element.53.refs_0_), channel_id=1, source_target_pairs={{0,12},{4,0},{8,4},{12,8},{1,13},{5,1},{9,5},{13,9},{2,14},{6,2},{... | collective-permute-start | bytes 196616 | tf_op jit(solution)/shard_map/ppermute | solution.py:293
  43.8 7.4 %collective-permute-start.17 = (f32[64,256]{1,0:T(8,128)S(1)}, f32[64,256]{1,0:T(8,128)S(1)}, u32[]{:S(2)}, u32[]{:S(2)}) collective-permute-start(f32[64,256]{1,0:T(8,128)S(1)} %get-tuple-element.53.refs_0_), channel_id=1, source_target_pairs={{0,8},{4,12},{8,0},{12,4},{1,9},{5,13},{9,1},{13,5},{2,10},{6,14},... | collective-permute-start | bytes 196616 | tf_op jit(solution)/shard_map/ppermute | solution.py:293
  44.5 6.8 %collective-permute-start.15 = (f32[64,256]{1,0:T(8,128)S(1)}, f32[64,256]{1,0:T(8,128)S(1)}, u32[]{:S(2)}, u32[]{:S(2)}) collective-permute-start(f32[64,256]{1,0:T(8,128)S(1)} %get-tuple-element.53.refs_0_), channel_id=1, source_target_pairs={{0,4},{4,8},{8,12},{12,0},{1,5},{5,9},{9,13},{13,1},{2,6},{6,10},{... | collective-permute-start | bytes 196616 | tf_op jit(solution)/shard_map/ppermute | solution.py:293
  45.6 6.1 %collective-permute-start.13 = (f32[64,256]{1,0:T(8,128)S(1)}, f32[64,256]{1,0:T(8,128)S(1)}, u32[]{:S(2)}, u32[]{:S(2)}) collective-permute-start(f32[64,256]{1,0:T(8,128)S(1)} %collective-permute-done.12.refs_2_), channel_id=1, source_target_pairs={{0,1},{1,0},{2,3},{3,2},{4,5},{5,4},{6,7},{7,6},{8,9},{9,8},{10,11... | collective-permute-start | bytes 196616 | tf_op jit(solution)/shard_map/ppermute | solution.py:293
  45.6 9.6 %collective-permute-start.14 = (f32[64,256]{1,0:T(8,128)S(1)}, f32[64,256]{1,0:T(8,128)S(1)}, u32[]{:S(2)}, u32[]{:S(2)}) collective-permute-start(f32[64,256]{1,0:T(8,128)S(1)} %get-tuple-element.53.refs_0_), channel_id=1, source_target_pairs={{0,1},{1,0},{2,3},{3,2},{4,5},{5,4},{6,7},{7,6},{8,9},{9,8},{10,11... | collective-permute-start | bytes 196616 | tf_op jit(solution)/shard_map/ppermute | solution.py:293
  46.3 8.9 %collective-permute-start.20 = (f32[64,256]{1,0:T(8,128)S(1)}, f32[64,256]{1,0:T(8,128)S(1)}, u32[]{:S(2)}, u32[]{:S(2)}) collective-permute-start(f32[64,256]{1,0:T(8,128)S(1)} %collective-permute-done.19.refs_6_), channel_id=1, source_target_pairs={{0,1},{1,0},{2,3},{3,2},{4,5},{5,4},{6,7},{7,6},{8,9},{9,8},{10,11... | collective-permute-start | bytes 196616 | tf_op jit(solution)/shard_map/ppermute | solution.py:293
  51.2 4.0 %collective-permute-start.18 = (f32[64,256]{1,0:T(8,128)S(1)}, f32[64,256]{1,0:T(8,128)S(1)}, u32[]{:S(2)}, u32[]{:S(2)}) collective-permute-start(f32[64,256]{1,0:T(8,128)S(1)} %collective-permute-done.17.refs_4_), channel_id=1, source_target_pairs={{0,1},{1,0},{2,3},{3,2},{4,5},{5,4},{6,7},{7,6},{8,9},{9,8},{10,11... | collective-permute-start | bytes 196616 | tf_op jit(solution)/shard_map/ppermute | solution.py:293
  51.3 3.9 %collective-permute-start.16 = (f32[64,256]{1,0:T(8,128)S(1)}, f32[64,256]{1,0:T(8,128)S(1)}, u32[]{:S(2)}, u32[]{:S(2)}) collective-permute-start(f32[64,256]{1,0:T(8,128)S(1)} %collective-permute-done.15.refs_2_), channel_id=1, source_target_pairs={{0,1},{1,0},{2,3},{3,2},{4,5},{5,4},{6,7},{7,6},{8,9},{9,8},{10,11... | collective-permute-start | bytes 196616 | tf_op jit(solution)/shard_map/ppermute | solution.py:293
  62.0 1.6 %collective-permute-start.21 = (f32[16,32,128]{2,1,0:T(8,128)S(1)}, f32[16,32,128]{2,1,0:T(8,128)S(1)}, u32[]{:S(2)}, u32[]{:S(2)}) collective-permute-start(f32[16,32,128]{2,1,0:T(8,128)S(1)} %get-tuple-element.55), channel_id=1, source_target_pairs={{0,1},{1,0},{2,3},{3,2},{4,5},{5,4},{6,7},{7,6},{8,9},{9,8},{10,11... | collective-permute-start | bytes 786440 | tf_op jit(solution)/shard_map/ppermute | solution.py:293
  62.1 5.3 %collective-permute-start.25 = (f32[16,32,128]{2,1,0:T(8,128)S(1)}, f32[16,32,128]{2,1,0:T(8,128)S(1)}, u32[]{:S(2)}, u32[]{:S(2)}) collective-permute-start(f32[16,32,128]{2,1,0:T(8,128)S(1)} %get-tuple-element.52.after), channel_id=1, source_target_pairs={{0,1},{1,0},{2,3},{3,2},{4,5},{5,4},{6,7},{7,6},{8,9},{9,8},{10,11... | collective-permute-start | bytes 786440 | tf_op jit(solution)/shard_map/ppermute | solution.py:293
  63.6 10.6 %collective-permute-start.22 = (f32[16,32,128]{2,1,0:T(8,128)S(1)}, f32[16,32,128]{2,1,0:T(8,128)S(1)}, u32[]{:S(2)}, u32[]{:S(2)}) collective-permute-start(f32[16,32,128]{2,1,0:T(8,128)S(1)} %shard_map.135.refs_0_), channel_id=1, source_target_pairs={{0,2},{2,0},{1,3},{3,1},{4,6},{6,4},{5,7},{7,5},{8,10},{10,8},{9,1... | collective-permute-start | bytes 786440 | tf_op jit(solution)/shard_map/ppermute | solution.py:293
  67.5 8.5 %collective-permute-start.26 = (f32[4,32,128]{2,1,0:T(8,128)S(1)}, f32[4,32,128]{2,1,0:T(8,128)S(1)}, u32[]{:S(2)}, u32[]{:S(2)}) collective-permute-start(f32[4,32,128]{2,1,0:T(8,128)S(1)} %get-tuple-element.59), channel_id=1, source_target_pairs={{0,4},{4,8},{8,12},{12,0},{1,5},{5,9},{9,13},{13,1},{2,6},{6,10},{... | collective-permute-start | bytes 196616 | tf_op jit(solution)/shard_map/ppermute | solution.py:293
  67.5 10.8 %collective-permute-start.27 = (f32[4,32,128]{2,1,0:T(8,128)S(1)}, f32[4,32,128]{2,1,0:T(8,128)S(1)}, u32[]{:S(2)}, u32[]{:S(2)}) collective-permute-start(f32[4,32,128]{2,1,0:T(8,128)S(1)} %get-tuple-element.60), channel_id=1, source_target_pairs={{0,8},{4,12},{8,0},{12,4},{1,9},{5,13},{9,1},{13,5},{2,10},{6,14},... | collective-permute-start | bytes 196616 | tf_op jit(solution)/shard_map/ppermute | solution.py:293
  73.6 5.2 %collective-permute-start.28 = (f32[4,32,128]{2,1,0:T(8,128)S(1)}, f32[4,32,128]{2,1,0:T(8,128)S(1)}, u32[]{:S(2)}, u32[]{:S(2)}) collective-permute-start(f32[4,32,128]{2,1,0:T(8,128)S(1)} %get-tuple-element.61), channel_id=1, source_target_pairs={{0,12},{4,0},{8,4},{12,8},{1,13},{5,1},{9,5},{13,9},{2,14},{6,2},{... | collective-permute-start | bytes 196616 | tf_op jit(solution)/shard_map/ppermute | solution.py:293
  73.6 16.8 %collective-permute-start.23 = (f32[16,32,128]{2,1,0:T(8,128)S(1)}, f32[16,32,128]{2,1,0:T(8,128)S(1)}, u32[]{:S(2)}, u32[]{:S(2)}) collective-permute-start(f32[16,32,128]{2,1,0:T(8,128)S(1)} %shard_map.135.refs_0_), channel_id=1, source_target_pairs={{0,1},{1,0},{2,3},{3,2},{4,5},{5,4},{6,7},{7,6},{8,9},{9,8},{10,11... | collective-permute-start | bytes 786440 | tf_op jit(solution)/shard_map/ppermute | solution.py:293
  74.3 16.1 %collective-permute-start.24 = (f32[16,32,128]{2,1,0:T(8,128)S(1)}, f32[16,32,128]{2,1,0:T(8,128)S(1)}, u32[]{:S(2)}, u32[]{:S(2)}) collective-permute-start(f32[16,32,128]{2,1,0:T(8,128)S(1)} %collective-permute-done.22.refs_1_), channel_id=1, source_target_pairs={{0,1},{1,0},{2,3},{3,2},{4,5},{5,4},{6,7},{7,6},{8,9},{9,8},{10,11... | collective-permute-start | bytes 786440 | tf_op jit(solution)/shard_map/ppermute | solution.py:293
  78.8 3.3 %collective-permute-start.32 = (f32[4,32,128]{2,1,0:T(8,128)S(1)}, f32[4,32,128]{2,1,0:T(8,128)S(1)}, u32[]{:S(2)}, u32[]{:S(2)}) collective-permute-start(f32[4,32,128]{2,1,0:T(8,128)S(1)} %shard_map.138.refs_0_), channel_id=1, source_target_pairs={{0,1},{1,0},{2,3},{3,2},{4,5},{5,4},{6,7},{7,6},{8,9},{9,8},{10,11... | collective-permute-start | bytes 196616 | tf_op jit(solution)/shard_map/ppermute | solution.py:293
  78.9 6.8 %collective-permute-start.31 = (f32[4,32,128]{2,1,0:T(8,128)S(1)}, f32[4,32,128]{2,1,0:T(8,128)S(1)}, u32[]{:S(2)}, u32[]{:S(2)}) collective-permute-start(f32[4,32,128]{2,1,0:T(8,128)S(1)} %shard_map.138.refs_0_), channel_id=1, source_target_pairs={{0,4},{4,8},{8,12},{12,0},{1,5},{5,9},{9,13},{13,1},{2,6},{6,10},{... | collective-permute-start | bytes 196616 | tf_op jit(solution)/shard_map/ppermute | solution.py:293
  80.3 7.8 %collective-permute-start.30 = (f32[4,32,128]{2,1,0:T(8,128)S(1)}, f32[4,32,128]{2,1,0:T(8,128)S(1)}, u32[]{:S(2)}, u32[]{:S(2)}) collective-permute-start(f32[4,32,128]{2,1,0:T(8,128)S(1)} %shard_map.138.refs_0_), channel_id=1, source_target_pairs={{0,8},{4,12},{8,0},{12,4},{1,9},{5,13},{9,1},{13,5},{2,10},{6,14},... | collective-permute-start | bytes 196616 | tf_op jit(solution)/shard_map/ppermute | solution.py:293
  82.2 5.9 %collective-permute-start.29 = (f32[4,32,128]{2,1,0:T(8,128)S(1)}, f32[4,32,128]{2,1,0:T(8,128)S(1)}, u32[]{:S(2)}, u32[]{:S(2)}) collective-permute-start(f32[4,32,128]{2,1,0:T(8,128)S(1)} %shard_map.138.refs_0_), channel_id=1, source_target_pairs={{0,12},{4,0},{8,4},{12,8},{1,13},{5,1},{9,5},{13,9},{2,14},{6,2},{... | collective-permute-start | bytes 196616 | tf_op jit(solution)/shard_map/ppermute | solution.py:293
  85.7 2.8 %collective-permute-start.35 = (f32[4,32,128]{2,1,0:T(8,128)S(1)}, f32[4,32,128]{2,1,0:T(8,128)S(1)}, u32[]{:S(2)}, u32[]{:S(2)}) collective-permute-start(f32[4,32,128]{2,1,0:T(8,128)S(1)} %collective-permute-done.31.refs_3_), channel_id=1, source_target_pairs={{0,1},{1,0},{2,3},{3,2},{4,5},{5,4},{6,7},{7,6},{8,9},{9,8},{10,11... | collective-permute-start | bytes 196616 | tf_op jit(solution)/shard_map/ppermute | solution.py:293
  88.1 1.3 %collective-permute-start.34 = (f32[4,32,128]{2,1,0:T(8,128)S(1)}, f32[4,32,128]{2,1,0:T(8,128)S(1)}, u32[]{:S(2)}, u32[]{:S(2)}) collective-permute-start(f32[4,32,128]{2,1,0:T(8,128)S(1)} %collective-permute-done.30.refs_2_), channel_id=1, source_target_pairs={{0,1},{1,0},{2,3},{3,2},{4,5},{5,4},{6,7},{7,6},{8,9},{9,8},{10,11... | collective-permute-start | bytes 196616 | tf_op jit(solution)/shard_map/ppermute | solution.py:293
  88.1 1.4 %collective-permute-start.33 = (f32[4,32,128]{2,1,0:T(8,128)S(1)}, f32[4,32,128]{2,1,0:T(8,128)S(1)}, u32[]{:S(2)}, u32[]{:S(2)}) collective-permute-start(f32[4,32,128]{2,1,0:T(8,128)S(1)} %collective-permute-done.29.refs_1_), channel_id=1, source_target_pairs={{0,1},{1,0},{2,3},{3,2},{4,5},{5,4},{6,7},{7,6},{8,9},{9,8},{10,11... | collective-permute-start | bytes 196616 | tf_op jit(solution)/shard_map/ppermute | solution.py:293

commit v2 on v1

--- a/solution.py
+++ b/solution.py
@@ -42,9 +42,17 @@
     return high, middle, low
 
 
-def hot(ids, start, rows):
-    place = lax.broadcasted_iota(jnp.int32, (rows, ids.shape[1]), 0) + start
-    return jnp.where(place == ids, 1.0, 0.0)
+def hot(ids_ref, rows, start, tile):
+    ids = [ids_ref[row:row + 1, :] for row in rows]
+    if len(rows) == 2:
+        same = ids[0] == ids[1]
+        ids = [jnp.where(same, -1, each) for each in ids]
+    ids = [each.astype(jnp.int16) for each in ids]
+    place = lax.broadcasted_iota(jnp.int16, (tile, ids[0].shape[1]), 0) + jnp.int16(start)
+    chosen = jnp.zeros(place.shape, BF16)
+    for each, sign in zip(ids, (1, -1)):
+        chosen = jnp.where(place == each, jnp.asarray(sign, BF16), chosen)
+    return chosen
 
 
 def sort_slots(keys, sources, count, blocks):
@@ -79,7 +87,7 @@
     row = lax.broadcasted_iota(jnp.int32, (8, lanes), 0)
     slot = found[0:1] * 16 + found[1:2]
     source = jnp.where(valid, found[2:3], blocks)
-    target = jnp.where(valid, found[3:4], blocks)
+    target = jnp.where(valid, found[3:4], 0)
     return jnp.where(row == 0, slot, jnp.where(row == 1, source, jnp.where(
         row == 2, target, total.astype(jnp.int32))))
 
@@ -133,16 +141,8 @@
         into[blocks] = jnp.zeros(into.shape[1:], BF16)
 
 
-def first_pass(across, order, vals, source, total):
+def first_pass(across, order, vals, source, after, total):
     multiply_blocks(order, vals, source, total, across)
-
-
-def table_of(blocks, scale, table):
-    _, width, size = blocks.shape
-    for block in range(scale.shape[0]):
-        span = slice(block * size, (block + 1) * size)
-        for part, piece in enumerate(split3(scale[block:block + 1, :] * blocks[block])):
-            table[part * width:(part + 1) * width, span] = piece
 
 
 def fold(stacked, width):
@@ -151,40 +151,53 @@
     )
 
 
-def pick(table, ids_ref, peer, rows, tile):
+def pick(table, ids_ref, rows, tile):
     total = None
     for start in range(0, table.shape[1], tile):
-        chosen = hot(ids_ref[peer, pl.ds(rows[0], 1), :], start, tile)
-        if len(rows) == 2:
-            chosen = chosen - hot(ids_ref[peer, pl.ds(rows[1], 1), :], start, tile)
         term = jnp.dot(
-            table[:, start:start + tile], chosen.astype(BF16), preferred_element_type=F32
+            table[:, start:start + tile], hot(ids_ref, rows, start, tile),
+            preferred_element_type=F32,
         )
         total = term if total is None else total + term
     return total
 
 
-def gather(rows, blocks, scale, ids, keep, send, table):
-    width = blocks.shape[1]
-    tile = 2 * blocks.shape[2]
-    table_of(blocks, scale, table)
-
-    def one(peer, _):
-        keep[peer] = fold(pick(table, ids, peer, rows, tile), width)
-        send[peer] = fold(pick(table, ids, peer, [row + 3 for row in rows], tile), width)
-        return 0
-
-    lax.fori_loop(0, ids.shape[0], one, 0)
+def gather(rows, peers, mine, other, scale, *refs):
+    ids, outs, table = refs[:peers], refs[peers:2 * peers], refs[2 * peers]
+    blocks, width, size = mine.shape
+    for block in range(blocks):
+        span = slice(block * size, (block + 1) * size)
+        here = scale[block:block + 1, :] * (mine[block] + other[block])
+        for part, piece in enumerate(split3(here)):
+            table[part * width:(part + 1) * width, span] = piece
+    for peer in range(peers):
+        outs[peer][...] = fold(pick(table, ids[peer], rows, 2 * size), width)
+
+
+def scatter(rows, peers, after, *refs):
+    pieces, ids, out, table = refs[:peers], refs[peers:2 * peers], refs[2 * peers], refs[-1]
+    blocks, width, size = out.shape
+    tile = 2 * size
+    for place, piece in enumerate(pieces):
+        for part, value in enumerate(split3(piece[...])):
+            table[place, part * width:(part + 1) * width, :] = value
+    for start in range(0, blocks * size, tile):
+        total = None
+        for place in range(peers):
+            term = lax.dot_general(
+                table[place], hot(ids[place], rows, start, tile), (((1,), (1,)), ((), ())),
+                preferred_element_type=F32,
+            )
+            total = term if total is None else total + term
+        total = fold(total, width)
+        for offset in range(0, tile, size):
+            out[(start + offset) // size] = total[:, offset:offset + size]
 
 
 def gather_base(user_emb, item_emb, ids, user_out, item_out):
-    user_out[...] = pick(user_emb, ids, 0, [0], 256)
-    item_out[...] = pick(item_emb, ids, 0, [1, 2], 256)
-
-
-def add_split(peers, keep, received, *outs):
-    for peer in range(peers):
-        outs[peer][...] = keep[peer] + received[peer]
+    tile = ids.shape[1]
+    user_out[...] = pick(user_emb, ids, [0], tile)
+    item_out[...] = pick(item_emb, ids, [1, 2], tile)
 
 
 def add_all(refs):
@@ -205,30 +218,13 @@
     pushed[...] = slope * user_rows
 
 
-def second_pass(across, rows, chunks, order, ids, source_scale, target_scale, vals, after, *refs):
-    pieces = refs[:len(chunks)]
-    half_grad, keep, send, source, total, table = refs[len(chunks):]
-    blocks, width, size = half_grad.shape
-    tile = 2 * size
-    for place, piece in enumerate(pieces):
-        for part, value in enumerate(split3(piece[...])):
-            table[place, part * width:(part + 1) * width, :] = value
-    for start in range(0, blocks * size, tile):
-        total_here = jnp.zeros((3 * width, tile), F32)
-        for place, (peer, other) in enumerate(chunks):
-            chosen = hot(ids[peer, pl.ds(rows[0] + 3 * other, 1), :], start, tile)
-            if len(rows) == 2:
-                chosen = chosen - hot(ids[peer, pl.ds(rows[1] + 3 * other, 1), :], start, tile)
-            total_here = total_here + lax.dot_general(
-                table[place], chosen.astype(BF16), (((1,), (1,)), ((), ())),
-                preferred_element_type=F32,
-            )
-        grad = fold(total_here, width)
-        for offset in range(0, tile, size):
-            block = (start + offset) // size
-            mine = grad[:, offset:offset + size]
-            half_grad[block] = 0.5 * mine
-            source[block] = (source_scale[block:block + 1, :] * mine * 0.5).astype(BF16)
+def second_pass(across, order, mine, other, source_scale, target_scale, vals, after,
+                half_grad, keep, send, source, total):
+    blocks, width, size = mine.shape
+    for block in range(blocks):
+        grad = mine[block] + other[block]
+        half_grad[block] = 0.5 * grad
+        source[block] = (source_scale[block:block + 1, :] * grad * 0.5).astype(BF16)
     source[blocks] = jnp.zeros((width, size), BF16)
     multiply_blocks(order, vals, source, total, across)
     me = lax.axis_index("rep")
@@ -248,33 +244,27 @@
             outs[offset][block] = keep[there + block] + received[there + block]
 
 
-def add_two(keep, received, out):
-    out[...] = keep[...] + received[...]
-
-
 def sum_parts(*refs):
     refs[-1][...] = add_all(refs[:-1])
 
 
-def finish_users(parts, half_grad, *refs):
-    mine, other = refs[:parts], refs[parts:2 * parts]
-    out = refs[-1]
+def pack(*refs):
+    for place, ref in enumerate(refs[:-1]):
+        refs[-1][place] = ref[...]
+
+
+def finish_users(half_grad, mine, other, out):
     me = lax.axis_index("rep")
     blocks, width, size = half_grad.shape
     half = width // 2
     for block in range(blocks):
         span = slice(block * size, (block + 1) * size)
-        for rank, group in ((me, mine), (1 - me, other)):
+        for rank, part in ((me, mine), (1 - me, other)):
             rows = pl.ds(pl.multiple_of(rank * half, half), half)
-            total = half_grad[block, rows, :]
-            for ref in group:
-                total = total + ref[block]
-            out[rows, span] = total
-
-
-def finish_items(peers, half_grad, *refs):
-    mine, other = refs[:peers], refs[peers:2 * peers]
-    out = refs[-1]
+            out[rows, span] = half_grad[block, rows, :] + part[block]
+
+
+def finish_items(peers, half_grad, mine, other, out):
     me = lax.axis_index("rep")
     place = lax.axis_index("user")
     blocks, width, size = half_grad.shape
@@ -284,9 +274,9 @@
         there = lax.rem(place + offset, peers) * per
         for block in range(per):
             span = pl.ds(pl.multiple_of((there + block) * size, size), size)
-            for rank, group in ((me, mine), (1 - me, other)):
+            for rank, part in ((me, mine), (1 - me, other)):
                 rows = pl.ds(pl.multiple_of(rank * half, half), half)
-                out[rows, span] = half_grad[there + block, rows, :] + group[offset][block]
+                out[rows, span] = half_grad[there + block, rows, :] + part[offset, block]
 
 
 def shift(values, axis, count, offset):
@@ -313,10 +303,8 @@
         [each.reshape(1, trips) for each in (trip_user, trip_pos, trip_neg)] + [started],
         [VMEM, VMEM, VMEM, ANY],
     )
-    both = jnp.concatenate([ids, swap(ids)])
-    ids_user = jnp.stack([both] + [shift(both, "item", items, -o) for o in range(1, items)])
-    ids_item = jnp.stack([both] + [shift(both, "user", users, -o) for o in range(1, users)])
-
+    ids_user = [ids] + [shift(ids, "item", items, -o) for o in range(1, items)]
+    ids_item = [ids] + [shift(ids, "user", users, -o) for o in range(1, users)]
     lanes = -(-slots // size) * size
 
     order_shape = jax.ShapeDtypeStruct((8, lanes), jnp.int32)
@@ -332,44 +320,32 @@
         [pltpu.VMEM((8, lanes), jnp.int32)], product_flops, product_bytes,
     )
     item_table = call(
-        functools.partial(first_pass, False), shape(item_blocks + 1, width, size),
-        (item_order, block_vals, user_source), [SMEM, VMEM, VMEM], (),
+        functools.partial(first_pass, False), shape(item_blocks, width, size),
+        (item_order, block_vals, user_source, ids), [SMEM, VMEM, VMEM, ANY], (),
         product_flops, product_bytes,
     )
     user_table = call(
-        functools.partial(first_pass, True), shape(user_blocks + 1, width, size),
-        (user_order, block_vals, item_source), [SMEM, VMEM, VMEM], (),
+        functools.partial(first_pass, True), shape(user_blocks, width, size),
+        (user_order, block_vals, item_source, item_table), [SMEM, VMEM, VMEM, ANY], (),
         product_flops, product_bytes,
     )
 
-    def picked(rows, table, scale, peer_ids):
-        peers = peer_ids.shape[0]
-        blocks = scale.shape[0]
-        return call(
-            functools.partial(gather, rows),
-            [shape(peers, width, trips)] * 2,
-            (table, scale, peer_ids),
-            [VMEM, VMEM, VMEM],
+    hot_flops = 2 * 3 * width * trips * size
+
+    def reduced(rows, table, scale, peer_ids, axis):
+        peers, blocks = len(peer_ids), scale.shape[0]
+        dealt = call(
+            functools.partial(gather, rows, peers), [shape(width, trips)] * peers,
+            (table, swap(table), scale, *peer_ids), [VMEM] * (3 + peers),
             [pltpu.VMEM((3 * width, blocks * size), BF16)],
-            2 * peers * 2 * 3 * width * blocks * size * trips, 4 * blocks * width * size,
-        )
-
-    def reduced(rows, table, scale, peer_ids, axis):
-        peers = peer_ids.shape[0]
-        keep, send = picked(rows, table, scale, peer_ids)
-        received = swap(send)
-        dealt = call(
-            functools.partial(add_split, peers),
-            [shape(width, trips)] * peers,
-            (keep, received), [VMEM, VMEM],
-            moved=12 * peers * width * trips,
+            peers * blocks * hot_flops, 8 * blocks * width * size,
         )
         return [dealt[0]] + [shift(dealt[o], axis, peers, o) for o in range(1, peers)]
 
     item_parts = reduced([1, 2], item_table, item_scale, ids_item, "user")
     user_parts = reduced([0], user_table, user_scale, ids_user, "item")
     user_base, item_base = call(
-        gather_base, [shape(width, trips)] * 2, (user_emb, item_emb, ids_item),
+        gather_base, [shape(width, trips)] * 2, (user_emb, item_emb, ids),
         [VMEM, VMEM, VMEM], (), 4 * width * trips * size * (user_blocks + item_blocks),
         2 * width * size * (user_blocks + item_blocks),
     )
@@ -382,57 +358,59 @@
         moved=4 * width * trips * (len(user_parts) + len(item_parts) + 2),
     )
 
-    def shared(own, axis, peers):
-        arrays, chunks = [own, swap(own)], [(0, 0), (0, 1)]
-        for offset in range(1, peers):
-            come = shift(own, axis, peers, offset)
-            arrays += [come, swap(come)]
-            chunks += [(peers - offset, 0), (peers - offset, 1)]
-        return arrays, chunks
-
-    def second(across, rows, own, axis, peer_ids, order, source_scale, target_scale, after):
-        arrays, chunks = shared(own, axis, peer_ids.shape[0])
+    def added(rows, own, axis, peer_ids, blocks, after):
+        peers = len(peer_ids)
+        arrays = [own] + [shift(own, axis, peers, -o) for o in range(1, peers)]
+        return call(
+            functools.partial(scatter, rows, peers), shape(blocks, width, size),
+            (after, *arrays, *peer_ids), [ANY] + [VMEM] * (2 * peers),
+            [pltpu.VMEM((peers, 3 * width, trips), BF16)],
+            peers * blocks * hot_flops, 4 * blocks * width * size,
+        )
+
+    def second(across, grad, order, source_scale, target_scale, after):
         sources, targets = source_scale.shape[0], target_scale.shape[0]
         return call(
-            functools.partial(second_pass, across, rows, chunks),
+            functools.partial(second_pass, across),
             [shape(sources, width, size), shape(targets, half, size), shape(targets, half, size)],
-            (order, peer_ids, source_scale, target_scale, block_vals, after, *arrays),
-            [SMEM, VMEM, VMEM, VMEM, VMEM, ANY] + [VMEM] * len(arrays),
+            (order, grad, swap(grad), source_scale, target_scale, block_vals, after),
+            [SMEM, VMEM, VMEM, VMEM, VMEM, VMEM, ANY],
             [pltpu.VMEM((sources + 1, width, size), BF16),
-             pltpu.VMEM((targets + 1, width, size), F32),
-             pltpu.VMEM((len(arrays), 3 * width, trips), BF16)],
-            product_flops + 2 * len(arrays) * 3 * width * trips * sources * size, product_bytes,
+             pltpu.VMEM((targets, width, size), F32)],
+            product_flops, product_bytes,
         )
 
+    user_grad = added([0], pieces, "item", ids_user, user_blocks, pieces)
     user_half_grad, item_keep, item_send = second(
-        False, [0], pieces, "item", ids_user, item_order, user_scale, item_scale, pieces)
-    item_half_grad, user_keep, user_send = second(
-        True, [1, 2], pushed, "user", ids_item, user_order, item_scale, user_scale, item_send)
+        False, user_grad, item_order, user_scale, item_scale, pieces)
+    item_grad = added([1, 2], pushed, "user", ids_item, item_blocks, item_send)
 
     per = item_blocks // users
     dealt = call(
         functools.partial(add_deal, users), [shape(per, half, size)] * users,
         (item_keep, swap(item_send)), [VMEM, VMEM], moved=12 * item_blocks * half * size,
     )
+    item_half_grad, user_keep, user_send = second(
+        True, item_grad, user_order, item_scale, user_scale, dealt[0])
     parts = [dealt[0]] + [shift(dealt[o], "user", users, o) for o in range(1, users)]
     own = call(sum_parts, shape(per, half, size), tuple(parts), [VMEM] * users,
                moved=4 * (users + 1) * per * half * size)
-    mine = [own] + [shift(own, "user", users, -o) for o in range(1, users)]
-    other = [swap(part) for part in mine]
+    mine = call(pack, shape(users, per, half, size),
+                (own, *[shift(own, "user", users, -o) for o in range(1, users)]),
+                [VMEM] * users, moved=8 * item_blocks * half * size)
     grad_item = call(
         functools.partial(finish_items, users), shape(width, item_blocks * size),
-        (item_half_grad, *mine, *other), [VMEM] * (2 * users + 1),
-        moved=12 * item_blocks * width * size,
-    )
-
-    own = call(add_two, shape(user_blocks, half, size), (user_keep, swap(user_send)),
+        (item_half_grad, mine, swap(mine)), [VMEM] * 3, moved=12 * item_blocks * width * size,
+    )
+
+    own = call(sum_parts, shape(user_blocks, half, size), (user_keep, swap(user_send)),
                [VMEM, VMEM], moved=12 * user_blocks * half * size)
-    mine = [own] + [shift(own, "item", items, o) for o in range(1, items)]
-    other = [swap(part) for part in mine]
+    mine = call(sum_parts, shape(user_blocks, half, size),
+                (own, *[shift(own, "item", items, o) for o in range(1, items)]),
+                [VMEM] * items, moved=12 * user_blocks * half * size)
     grad_user = call(
-        functools.partial(finish_users, items), shape(width, user_blocks * size),
-        (user_half_grad, *mine, *other), [VMEM] * (2 * items + 1),
-        moved=12 * user_blocks * width * size,
+        finish_users, shape(width, user_blocks * size), (user_half_grad, mine, swap(mine)),
+        [VMEM] * 3, moved=12 * user_blocks * width * size,
     )
     return (grad_user, grad_item)
 

time: 91.9 us -> 86 us (0.936)
  Pallas kernels: 23.8 us -> 19.4 us
  starting transfers between devices: 36.9 us -> 35.8 us
    pallas_call x18 -> x20, Pallas kernels: 23.8 us -> 19.4 us  [call(): pl.pallas_call(kernel, out_shape=outs, in_specs=specs, out_specs=jax.tree...]
    ppermute x36 -> x27, starting transfers between devices: 36.9 us -> 35.8 us  [shift(): lax.ppermute(values, axis, [(i, (i + offset) % count) for i in range(coun...]
    ppermute x36 -> x27, waiting for transfers between devices: 27.1 us -> 27.2 us  [shift(): lax.ppermute(values, axis, [(i, (i + offset) % count) for i in range(coun...]
  transfers between devices with their start and end apart: 36 -> 27, of which waited for: 17 -> 15; matrix products, arithmetic and copies ran while one was open for 0% -> 0% of each run, Pallas kernels for 18% -> 7%
where the time goes in v2:
time: 86 us; the launch traced here: 86.2 us
  starting transfers between devices  35.8 us (42%)
  waiting for transfers between devices  27.2 us (32%)
  Pallas kernels  19.4 us (23%)
  local copies, waits for them, and re-layouts  2.14 us (2%)
  between operations  1.75 us (2%)
    ppermute x27, starting transfers between devices, shift(): lax.ppermute(values, axis, [(i, (i + offset) % count) for i in range(coun...  35.8 us
    ppermute x27, waiting for transfers between devices, shift(): lax.ppermute(values, axis, [(i, (i + offset) % count) for i in range(coun...  27.2 us
    pallas_call x20, Pallas kernels, call(): pl.pallas_call(kernel, out_shape=outs, in_specs=specs, out_specs=jax.tree...  19.4 us
    unnamed x20, local copies, waits for them, and re-layouts  2.14 us
  transfers between devices with their start and end apart: 27, of which 15 were waited for; matrix products, arithmetic and copies ran while one was open for 0% of the time, Pallas kernels for 7%

profile of v2, /device:TPU:0, one launch (start us, length us, event | category | flops | bytes accessed | tf_op | source)
XLA Modules:
  0.0 86.2 jit_solution(1670634816700283131)
XLA Ops:
  1.6 0.1 copy-done.4
  1.7 0.1 copy-done.5
  1.7 0.9 %shard_map.124 = (bf16[17,64,128]{2,1,0:T(8,128)(2,1)S(1)}, bf16[17,64,128]{2,1,0:T(8,128)(2,1)S(1)}, f32[16,128]{1,0:T(8,128)S(1)}, f32[16,128]{1,0:T(8,128)S(1...) custom-call(s32[1]{0:T(128)S(6)} %copy.13.count, s32[288]{0:T(512)S(1)} %copy-done.8, s32[288]{0:T(512)S(1)} %copy-done.9, ...), custom_call_target="tpu_custom_call" | custom-call | flops 603979776 | bytes 9437184 | tf_op jit(solution)/shard_map/pallas_call | solution.py:22
  2.7 2.0 %copy-done = bf16[288,128,128]{2,1,0:T(8,128)(2,1)S(1)} copy-done((bf16[288,128,128]{2,1,0:T(8,128)(2,1)S(1)}, bf16[288,128,128]{2,1,0:T(8,128)(2,1)}, u32[]{:S(2)}) %copy-start) | copy-done | bytes 9437208
  4.6 2.6 %shard_map.125.after.mine = f32[16,64,128]{2,1,0:T(8,128)S(1)} custom-call(s32[8,384]{1,0:T(8,128)S(1)} %get-tuple-element.28.order, bf16[288,128,128]{2,1,0:T(8,128)(2,1)S(1)} %copy-done, bf16[17,64,128]{2,1,0:T(8,128)(2,1)S(1)} %get-tuple-element.31.source, s32[3,256]{1,0:T(4,128)S(1)} %shard_map.123.after.refs_0_.ids.refs_2_.refs_4_), custom_call_target="tpu_custom_call" | custom-call | flops 603979776 | bytes 9437184 | tf_op jit(solution)/shard_map/pallas_call | solution.py:22
  7.3 3.2 %shard_map.126.mine = f32[16,64,128]{2,1,0:T(8,128)S(1)} custom-call(s32[8,384]{1,0:T(8,128)S(1)} %get-tuple-element.29.order, bf16[288,128,128]{2,1,0:T(8,128)(2,1)S(1)} %copy-done, bf16[17,64,128]{2,1,0:T(8,128)(2,1)S(1)} %get-tuple-element.30.source, f32[16,64,128]{2,1,0:T(8,128)S(1)} %shard_map.125.after.mine), custom_call_target="tpu_custom_call" | custom-call | flops 603979776 | bytes 9437184 | tf_op jit(solution)/shard_map/pallas_call | solution.py:22
  10.5 0.5 collective-permute-start
  11.0 0.1 collective-permute-start.3
  11.0 9.3 %collective-permute-start.1 = (s32[3,256]{1,0:T(4,128)S(1)}, s32[3,256]{1,0:T(4,128)S(1)}, u32[]{:S(2)}, u32[]{:S(2)}) collective-permute-start(s32[3,256]{1,0:T(4,128)S(1)} %shard_map.123.after.refs_0_.ids.refs_2_.refs_4_), channel_id=1, source_target_pairs={{0,2},{2,0},{1,3},{3,1},{4,6},{6,4},{5,7},{7,5},{8,10},{10,8},{9,1... | collective-permute-start | bytes 9224 | tf_op jit(solution)/shard_map/ppermute | solution.py:283
  20.4 0.0 collective-permute-start.4
  20.4 0.0 collective-permute-start.5
  20.4 1.6 %collective-permute-done.1.refs_1_.refs_3_ = s32[3,256]{1,0:T(4,128)S(1)} collective-permute-done((s32[3,256]{1,0:T(4,128)S(1)}, s32[3,256]{1,0:T(4,128)S(1)}, u32[]{:S(2)}, u32[]{:S(2)}) %collective-permute-start.1) | collective-permute-done | bytes 3104 | tf_op jit(solution)/shard_map/ppermute | solution.py:283
  22.0 0.4 collective-permute-start.6
  22.4 0.0 collective-permute-done.other
  22.4 0.6 shard_map.127
  23.0 1.6 %collective-permute-start.2 = (f32[64,256]{1,0:T(8,128)S(1)}, f32[64,256]{1,0:T(8,128)S(1)}, u32[]{:S(2)}, u32[]{:S(2)}) collective-permute-start(f32[64,256]{1,0:T(8,128)S(1)} %get-tuple-element.34), channel_id=1, source_target_pairs={{0,2},{2,0},{1,3},{3,1},{4,6},{6,4},{5,7},{7,5},{8,10},{10,8},{9,1... | collective-permute-start | bytes 196616 | tf_op jit(solution)/shard_map/ppermute | solution.py:283
  24.7 0.2 collective-permute-done.5.refs_2_.refs_6_
  24.9 2.5 %collective-permute-done.6.refs_3_.refs_7_ = s32[3,256]{1,0:T(4,128)S(1)} collective-permute-done((s32[3,256]{1,0:T(4,128)S(1)}, s32[3,256]{1,0:T(4,128)S(1)}, u32[]{:S(2)}, u32[]{:S(2)}) %collective-permute-start.6) | collective-permute-done | bytes 3104 | tf_op jit(solution)/shard_map/ppermute | solution.py:283
  27.4 1.2 %shard_map.129 = (f32[64,256]{1,0:T(8,128)S(1)}, f32[64,256]{1,0:T(8,128)S(1)}, f32[64,256]{1,0:T(8,128)S(1)}, f32[64,256]{1,0:T(8,128)S(1)}) custom-call(f32[16,64,128]{2,1,0:T(8,128)S(1)} %shard_map.125.after.mine, f32[16,64,128]{2,1,0:T(8,128)S(1)} %collective-permute-done.3.other, f32[16,128]{1,0:T(8,128)S(1)} %get-tuple-element.36.scale.target_scale.source_scale, ...), custom_call_target="tpu_custom_call" | custom-call | flops 805306368 | bytes 1048576 | tf_op jit(solution)/shard_map/pallas_call | solution.py:22
  28.6 0.1 collective-permute-start.7
  28.7 1.7 %collective-permute-start.8 = (f32[64,256]{1,0:T(8,128)S(1)}, f32[64,256]{1,0:T(8,128)S(1)}, u32[]{:S(2)}, u32[]{:S(2)}) collective-permute-start(f32[64,256]{1,0:T(8,128)S(1)} %get-tuple-element.39), channel_id=1, source_target_pairs={{0,8},{4,12},{8,0},{12,4},{1,9},{5,13},{9,1},{13,5},{2,10},{6,14},... | collective-permute-start | bytes 196616 | tf_op jit(solution)/shard_map/ppermute | solution.py:283
  30.4 2.1 %collective-permute-start.9 = (f32[64,256]{1,0:T(8,128)S(1)}, f32[64,256]{1,0:T(8,128)S(1)}, u32[]{:S(2)}, u32[]{:S(2)}) collective-permute-start(f32[64,256]{1,0:T(8,128)S(1)} %get-tuple-element.40), channel_id=1, source_target_pairs={{0,12},{4,0},{8,4},{12,8},{1,13},{5,1},{9,5},{13,9},{2,14},{6,2},{... | collective-permute-start | bytes 196616 | tf_op jit(solution)/shard_map/ppermute | solution.py:283
  32.5 0.5 shard_map.128
  33.0 1.7 %collective-permute-done.7.refs_4_ = f32[64,256]{1,0:T(8,128)S(1)} collective-permute-done((f32[64,256]{1,0:T(8,128)S(1)}, f32[64,256]{1,0:T(8,128)S(1)}, u32[]{:S(2)}, u32[]{:S(2)}) %collective-permute-start.7) | collective-permute-done | bytes 65568 | tf_op jit(solution)/shard_map/ppermute | solution.py:283
  34.7 0.0 collective-permute-done.8.refs_5_
  34.7 0.7 collective-permute-done.9.refs_6_
  35.4 0.1 shard_map.130
  35.5 2.1 %collective-permute-start.10 = (f32[64,256]{1,0:T(8,128)S(1)}, f32[64,256]{1,0:T(8,128)S(1)}, u32[]{:S(2)}, u32[]{:S(2)}) collective-permute-start(f32[64,256]{1,0:T(8,128)S(1)} %get-tuple-element.42.after.refs_0_), channel_id=1, source_target_pairs={{0,2},{2,0},{1,3},{3,1},{4,6},{6,4},{5,7},{7,5},{8,10},{10,8},{9,1... | collective-permute-start | bytes 196616 | tf_op jit(solution)/shard_map/ppermute | solution.py:283
  37.6 2.2 %collective-permute-done.10.refs_1_ = f32[64,256]{1,0:T(8,128)S(1)} collective-permute-done((f32[64,256]{1,0:T(8,128)S(1)}, f32[64,256]{1,0:T(8,128)S(1)}, u32[]{:S(2)}, u32[]{:S(2)}) %collective-permute-start.10) | collective-permute-done | bytes 65568 | tf_op jit(solution)/shard_map/ppermute | solution.py:283
  39.8 0.8 shard_map.131.mine
  40.7 0.1 collective-permute-start.11
  40.7 3.2 %collective-permute-start.12 = (f32[64,256]{1,0:T(8,128)S(1)}, f32[64,256]{1,0:T(8,128)S(1)}, u32[]{:S(2)}, u32[]{:S(2)}) collective-permute-start(f32[64,256]{1,0:T(8,128)S(1)} %get-tuple-element.45.refs_0_), channel_id=1, source_target_pairs={{0,12},{4,0},{8,4},{12,8},{1,13},{5,1},{9,5},{13,9},{2,14},{6,2},{... | collective-permute-start | bytes 196616 | tf_op jit(solution)/shard_map/ppermute | solution.py:283
  43.9 0.2 collective-permute-start.13
  44.2 0.4 collective-permute-start.14
  44.6 0.0 collective-permute-done.11.other
  44.6 2.7 %shard_map.132 = (f32[16,64,128]{2,1,0:T(8,128)S(1)}, f32[16,32,128]{2,1,0:T(8,128)S(1)}, f32[16,32,128]{2,1,0:T(8,128)S(1)}) custom-call(s32[8,384]{1,0:T(8,128)S(1)} %get-tuple-element.28.order, f32[16,64,128]{2,1,0:T(8,128)S(1)} %shard_map.131.mine, f32[16,64,128]{2,1,0:T(8,128)S(1)} %collective-permute-done.11.other, ...), custom_call_target="tpu_custom_call" | custom-call | flops 603979776 | bytes 9437184 | tf_op jit(solution)/shard_map/pallas_call | solution.py:22
  47.3 0.0 collective-permute-done.12.refs_1_
  47.3 3.5 %collective-permute-done.13.refs_2_ = f32[64,256]{1,0:T(8,128)S(1)} collective-permute-done((f32[64,256]{1,0:T(8,128)S(1)}, f32[64,256]{1,0:T(8,128)S(1)}, u32[]{:S(2)}, u32[]{:S(2)}) %collective-permute-start.13) | collective-permute-done | bytes 65568 | tf_op jit(solution)/shard_map/ppermute | solution.py:283
  50.8 0.0 collective-permute-done.14.refs_3_
  50.8 1.5 %shard_map.133.mine = f32[16,64,128]{2,1,0:T(8,128)S(1)} custom-call(f32[16,32,128]{2,1,0:T(8,128)S(1)} %get-tuple-element.44.after, f32[64,256]{1,0:T(8,128)S(1)} %get-tuple-element.45.refs_0_, f32[64,256]{1,0:T(8,128)S(1)} %collective-permute-done.12.refs_1_, f32[64,256]{1,0:T(8,128)S(1)} %collective-permute-done.13.refs_2_, ...), custom_call_target="tpu_custom_call" | custom-call | flops 805306368 | bytes 524288 | tf_op jit(solution)/shard_map/pallas_call | solution.py:22
  52.4 0.1 collective-permute-start.15
  52.5 0.5 collective-permute-start.16
  53.0 1.8 %collective-permute-done.16.received = f32[16,32,128]{2,1,0:T(8,128)S(1)} collective-permute-done((f32[16,32,128]{2,1,0:T(8,128)S(1)}, f32[16,32,128]{2,1,0:T(8,128)S(1)}, u32[]{:S(2)}, u32[]{:S(2)}) %collective-permute-start.16) | collective-permute-done | bytes 262176 | tf_op jit(solution)/shard_map/ppermute | solution.py:283
  54.8 3.4 %shard_map.135 = (f32[16,64,128]{2,1,0:T(8,128)S(1)}, f32[16,32,128]{2,1,0:T(8,128)S(1)}, f32[16,32,128]{2,1,0:T(8,128)S(1)}) custom-call(s32[8,384]{1,0:T(8,128)S(1)} %get-tuple-element.29.order, f32[16,64,128]{2,1,0:T(8,128)S(1)} %shard_map.133.mine, f32[16,64,128]{2,1,0:T(8,128)S(1)} %collective-permute-done.15.other, ...), custom_call_target="tpu_custom_call" | custom-call | flops 603979776 | bytes 9437184 | tf_op jit(solution)/shard_map/pallas_call | solution.py:22
  58.1 0.2 collective-permute-start.17
  58.3 1.4 %collective-permute-done.17.refs_1_ = f32[16,32,128]{2,1,0:T(8,128)S(1)} collective-permute-done((f32[16,32,128]{2,1,0:T(8,128)S(1)}, f32[16,32,128]{2,1,0:T(8,128)S(1)}, u32[]{:S(2)}, u32[]{:S(2)}) %collective-permute-start.17) | collective-permute-done | bytes 262176 | tf_op jit(solution)/shard_map/ppermute | solution.py:283
  59.8 5.8 %collective-permute-start.18 = (f32[16,32,128]{2,1,0:T(8,128)S(1)}, f32[16,32,128]{2,1,0:T(8,128)S(1)}, u32[]{:S(2)}, u32[]{:S(2)}) collective-permute-start(f32[16,32,128]{2,1,0:T(8,128)S(1)} %shard_map.136.refs_0_), channel_id=1, source_target_pairs={{0,2},{2,0},{1,3},{3,1},{4,6},{6,4},{5,7},{7,5},{8,10},{10,8},{9,1... | collective-permute-start | bytes 786440 | tf_op jit(solution)/shard_map/ppermute | solution.py:283
  65.5 0.0 collective-permute-start.20
  65.5 0.0 collective-permute-start.21
  65.5 3.8 %collective-permute-start.22 = (f32[4,32,128]{2,1,0:T(8,128)S(1)}, f32[4,32,128]{2,1,0:T(8,128)S(1)}, u32[]{:S(2)}, u32[]{:S(2)}) collective-permute-start(f32[4,32,128]{2,1,0:T(8,128)S(1)} %get-tuple-element.53), channel_id=1, source_target_pairs={{0,12},{4,0},{8,4},{12,8},{1,13},{5,1},{9,5},{13,9},{2,14},{6,2},{... | collective-permute-start | bytes 196616 | tf_op jit(solution)/shard_map/ppermute | solution.py:283
  69.4 2.9 %collective-permute-done.20.refs_1_ = f32[4,32,128]{2,1,0:T(8,128)S(1)} collective-permute-done((f32[4,32,128]{2,1,0:T(8,128)S(1)}, f32[4,32,128]{2,1,0:T(8,128)S(1)}, u32[]{:S(2)}, u32[]{:S(2)}) %collective-permute-start.20) | collective-permute-done | bytes 65568 | tf_op jit(solution)/shard_map/ppermute | solution.py:283
  72.3 1.6 %collective-permute-done.21.refs_2_ = f32[4,32,128]{2,1,0:T(8,128)S(1)} collective-permute-done((f32[4,32,128]{2,1,0:T(8,128)S(1)}, f32[4,32,128]{2,1,0:T(8,128)S(1)}, u32[]{:S(2)}, u32[]{:S(2)}) %collective-permute-start.21) | collective-permute-done | bytes 65568 | tf_op jit(solution)/shard_map/ppermute | solution.py:283
  73.9 1.8 %collective-permute-start.23 = (f32[4,32,128]{2,1,0:T(8,128)S(1)}, f32[4,32,128]{2,1,0:T(8,128)S(1)}, u32[]{:S(2)}, u32[]{:S(2)}) collective-permute-start(f32[4,32,128]{2,1,0:T(8,128)S(1)} %shard_map.139.refs_0_), channel_id=1, source_target_pairs={{0,12},{4,0},{8,4},{12,8},{1,13},{5,1},{9,5},{13,9},{2,14},{6,2},{... | collective-permute-start | bytes 196616 | tf_op jit(solution)/shard_map/ppermute | solution.py:283
  75.8 1.0 %collective-permute-start.24 = (f32[4,32,128]{2,1,0:T(8,128)S(1)}, f32[4,32,128]{2,1,0:T(8,128)S(1)}, u32[]{:S(2)}, u32[]{:S(2)}) collective-permute-start(f32[4,32,128]{2,1,0:T(8,128)S(1)} %shard_map.139.refs_0_), channel_id=1, source_target_pairs={{0,8},{4,12},{8,0},{12,4},{1,9},{5,13},{9,1},{13,5},{2,10},{6,14},... | collective-permute-start | bytes 196616 | tf_op jit(solution)/shard_map/ppermute | solution.py:283
  76.8 1.7 %collective-permute-done.23.refs_1_ = f32[4,32,128]{2,1,0:T(8,128)S(1)} collective-permute-done((f32[4,32,128]{2,1,0:T(8,128)S(1)}, f32[4,32,128]{2,1,0:T(8,128)S(1)}, u32[]{:S(2)}, u32[]{:S(2)}) %collective-permute-start.23) | collective-permute-done | bytes 65568 | tf_op jit(solution)/shard_map/ppermute | solution.py:283
  78.5 3.6 %collective-permute-done.24.refs_2_ = f32[4,32,128]{2,1,0:T(8,128)S(1)} collective-permute-done((f32[4,32,128]{2,1,0:T(8,128)S(1)}, f32[4,32,128]{2,1,0:T(8,128)S(1)}, u32[]{:S(2)}, u32[]{:S(2)}) %collective-permute-start.24) | collective-permute-done | bytes 65568 | tf_op jit(solution)/shard_map/ppermute | solution.py:283
  82.1 0.8 collective-permute-done.25.refs_3_
  82.9 0.1 collective-permute-start.26
  83.0 0.0 collective-permute-done.18.refs_1_
  83.0 0.5 collective-permute-start.19
  83.6 0.9 %collective-permute-done.26.other = f32[4,4,32,128]{3,2,1,0:T(8,128)S(1)} collective-permute-done((f32[4,4,32,128]{3,2,1,0:T(8,128)S(1)}, f32[4,4,32,128]{3,2,1,0:T(8,128)S(1)}, u32[]{:S(2)}, u32[]{:S(2)}) %collective-permute-start.26) | collective-permute-done | bytes 262176 | tf_op jit(solution)/shard_map/ppermute | solution.py:283
  84.5 0.9 shard_map.141
  85.3 0.0 collective-permute-done.19.other
  85.3 0.8 shard_map.138
  (30 shorter events, 0.2 us)
Async XLA Ops:
  0.6 0.9 %copy-start.1 = (s32[256]{0:T(256)S(1)}, s32[256]{0:T(256)}, u32[]{:S(2)}) copy-start(s32[256]{0:T(256)} %param.19) | copy-start | bytes 3076
  0.6 0.9 %copy-start.2 = (s32[256]{0:T(256)S(1)}, s32[256]{0:T(256)}, u32[]{:S(2)}) copy-start(s32[256]{0:T(256)} %param.20) | copy-start | bytes 3076
  0.7 0.9 %copy-start.3 = (s32[256]{0:T(256)S(1)}, s32[256]{0:T(256)}, u32[]{:S(2)}) copy-start(s32[256]{0:T(256)} %param.21) | copy-start | bytes 3076
  0.7 0.9 %copy-start.8 = (s32[288]{0:T(512)S(1)}, s32[288]{0:T(512)}, u32[]{:S(2)}) copy-start(s32[288]{0:T(512)} %rows.1) | copy-start | bytes 3460
  0.7 0.9 %copy-start.9 = (s32[288]{0:T(512)S(1)}, s32[288]{0:T(512)}, u32[]{:S(2)}) copy-start(s32[288]{0:T(512)} %columns.1) | copy-start | bytes 3460
  0.7 1.0 %copy-start.4 = (bf16[64,2048]{1,0:T(8,128)(2,1)S(1)}, bf16[64,2048]{1,0:T(8,128)(2,1)}, u32[]{:S(2)}) copy-start(bf16[64,2048]{1,0:T(8,128)(2,1)} %user_emb.3) | copy-start | bytes 786436
  0.7 1.0 %copy-start.5 = (bf16[64,2048]{1,0:T(8,128)(2,1)S(1)}, bf16[64,2048]{1,0:T(8,128)(2,1)}, u32[]{:S(2)}) copy-start(bf16[64,2048]{1,0:T(8,128)(2,1)} %item_emb.3) | copy-start | bytes 786436
  0.7 1.0 %copy-start.6 = (s32[2048]{0:T(1024)S(1)}, s32[2048]{0:T(1024)}, u32[]{:S(2)}) copy-start(s32[2048]{0:T(1024)} %param.13) | copy-start | bytes 24580
  0.7 1.0 %copy-start.7 = (s32[2048]{0:T(1024)S(1)}, s32[2048]{0:T(1024)}, u32[]{:S(2)}) copy-start(s32[2048]{0:T(1024)} %param.14) | copy-start | bytes 24580
  0.7 3.9 %copy-start = (bf16[288,128,128]{2,1,0:T(8,128)(2,1)S(1)}, bf16[288,128,128]{2,1,0:T(8,128)(2,1)}, u32[]{:S(2)}) copy-start(bf16[288,128,128]{2,1,0:T(8,128)(2,1)} %vals.7) | copy-start | bytes 28311556
  10.5 12.0 %collective-permute-start = (f32[16,64,128]{2,1,0:T(8,128)S(1)}, f32[16,64,128]{2,1,0:T(8,128)S(1)}, u32[]{:S(2)}, u32[]{:S(2)}) collective-permute-start(f32[16,64,128]{2,1,0:T(8,128)S(1)} %shard_map.126.mine), channel_id=1, source_target_pairs={{0,1},{1,0},{2,3},{3,2},{4,5},{5,4},{6,7},{7,6},{8,9},{9,8},{10,11... | collective-permute-start | bytes 1572872 | tf_op jit(solution)/shard_map/ppermute | solution.py:283
  11.0 16.4 %collective-permute-start.3 = (f32[16,64,128]{2,1,0:T(8,128)S(1)}, f32[16,64,128]{2,1,0:T(8,128)S(1)}, u32[]{:S(2)}, u32[]{:S(2)}) collective-permute-start(f32[16,64,128]{2,1,0:T(8,128)S(1)} %shard_map.125.after.mine), channel_id=1, source_target_pairs={{0,1},{1,0},{2,3},{3,2},{4,5},{5,4},{6,7},{7,6},{8,9},{9,8},{10,11... | collective-permute-start | bytes 1572872 | tf_op jit(solution)/shard_map/ppermute | solution.py:283
  11.0 10.9 %collective-permute-start.1 = (s32[3,256]{1,0:T(4,128)S(1)}, s32[3,256]{1,0:T(4,128)S(1)}, u32[]{:S(2)}, u32[]{:S(2)}) collective-permute-start(s32[3,256]{1,0:T(4,128)S(1)} %shard_map.123.after.refs_0_.ids.refs_2_.refs_4_), channel_id=1, source_target_pairs={{0,2},{2,0},{1,3},{3,1},{4,6},{6,4},{5,7},{7,5},{8,10},{10,8},{9,1... | collective-permute-start | bytes 9224 | tf_op jit(solution)/shard_map/ppermute | solution.py:283
  20.4 4.3 %collective-permute-start.4 = (s32[3,256]{1,0:T(4,128)S(1)}, s32[3,256]{1,0:T(4,128)S(1)}, u32[]{:S(2)}, u32[]{:S(2)}) collective-permute-start(s32[3,256]{1,0:T(4,128)S(1)} %shard_map.123.after.refs_0_.ids.refs_2_.refs_4_), channel_id=1, source_target_pairs={{0,12},{4,0},{8,4},{12,8},{1,13},{5,1},{9,5},{13,9},{2,14},{6,2},{... | collective-permute-start | bytes 9224 | tf_op jit(solution)/shard_map/ppermute | solution.py:283
  20.4 4.5 %collective-permute-start.5 = (s32[3,256]{1,0:T(4,128)S(1)}, s32[3,256]{1,0:T(4,128)S(1)}, u32[]{:S(2)}, u32[]{:S(2)}) collective-permute-start(s32[3,256]{1,0:T(4,128)S(1)} %shard_map.123.after.refs_0_.ids.refs_2_.refs_4_), channel_id=1, source_target_pairs={{0,8},{4,12},{8,0},{12,4},{1,9},{5,13},{9,1},{13,5},{2,10},{6,14},... | collective-permute-start | bytes 9224 | tf_op jit(solution)/shard_map/ppermute | solution.py:283
  22.0 5.4 %collective-permute-start.6 = (s32[3,256]{1,0:T(4,128)S(1)}, s32[3,256]{1,0:T(4,128)S(1)}, u32[]{:S(2)}, u32[]{:S(2)}) collective-permute-start(s32[3,256]{1,0:T(4,128)S(1)} %shard_map.123.after.refs_0_.ids.refs_2_.refs_4_), channel_id=1, source_target_pairs={{0,4},{4,8},{8,12},{12,0},{1,5},{5,9},{9,13},{13,1},{2,6},{6,10},{... | collective-permute-start | bytes 9224 | tf_op jit(solution)/shard_map/ppermute | solution.py:283
  23.0 10.0 %collective-permute-start.2 = (f32[64,256]{1,0:T(8,128)S(1)}, f32[64,256]{1,0:T(8,128)S(1)}, u32[]{:S(2)}, u32[]{:S(2)}) collective-permute-start(f32[64,256]{1,0:T(8,128)S(1)} %get-tuple-element.34), channel_id=1, source_target_pairs={{0,2},{2,0},{1,3},{3,1},{4,6},{6,4},{5,7},{7,5},{8,10},{10,8},{9,1... | collective-permute-start | bytes 196616 | tf_op jit(solution)/shard_map/ppermute | solution.py:283
  28.6 6.1 %collective-permute-start.7 = (f32[64,256]{1,0:T(8,128)S(1)}, f32[64,256]{1,0:T(8,128)S(1)}, u32[]{:S(2)}, u32[]{:S(2)}) collective-permute-start(f32[64,256]{1,0:T(8,128)S(1)} %get-tuple-element.38), channel_id=1, source_target_pairs={{0,4},{4,8},{8,12},{12,0},{1,5},{5,9},{9,13},{13,1},{2,6},{6,10},{... | collective-permute-start | bytes 196616 | tf_op jit(solution)/shard_map/ppermute | solution.py:283
  28.7 6.1 %collective-permute-start.8 = (f32[64,256]{1,0:T(8,128)S(1)}, f32[64,256]{1,0:T(8,128)S(1)}, u32[]{:S(2)}, u32[]{:S(2)}) collective-permute-start(f32[64,256]{1,0:T(8,128)S(1)} %get-tuple-element.39), channel_id=1, source_target_pairs={{0,8},{4,12},{8,0},{12,4},{1,9},{5,13},{9,1},{13,5},{2,10},{6,14},... | collective-permute-start | bytes 196616 | tf_op jit(solution)/shard_map/ppermute | solution.py:283
  30.4 5.1 %collective-permute-start.9 = (f32[64,256]{1,0:T(8,128)S(1)}, f32[64,256]{1,0:T(8,128)S(1)}, u32[]{:S(2)}, u32[]{:S(2)}) collective-permute-start(f32[64,256]{1,0:T(8,128)S(1)} %get-tuple-element.40), channel_id=1, source_target_pairs={{0,12},{4,0},{8,4},{12,8},{1,13},{5,1},{9,5},{13,9},{2,14},{6,2},{... | collective-permute-start | bytes 196616 | tf_op jit(solution)/shard_map/ppermute | solution.py:283
  35.5 4.3 %collective-permute-start.10 = (f32[64,256]{1,0:T(8,128)S(1)}, f32[64,256]{1,0:T(8,128)S(1)}, u32[]{:S(2)}, u32[]{:S(2)}) collective-permute-start(f32[64,256]{1,0:T(8,128)S(1)} %get-tuple-element.42.after.refs_0_), channel_id=1, source_target_pairs={{0,2},{2,0},{1,3},{3,1},{4,6},{6,4},{5,7},{7,5},{8,10},{10,8},{9,1... | collective-permute-start | bytes 196616 | tf_op jit(solution)/shard_map/ppermute | solution.py:283
  40.7 3.9 %collective-permute-start.11 = (f32[16,64,128]{2,1,0:T(8,128)S(1)}, f32[16,64,128]{2,1,0:T(8,128)S(1)}, u32[]{:S(2)}, u32[]{:S(2)}) collective-permute-start(f32[16,64,128]{2,1,0:T(8,128)S(1)} %shard_map.131.mine), channel_id=1, source_target_pairs={{0,1},{1,0},{2,3},{3,2},{4,5},{5,4},{6,7},{7,6},{8,9},{9,8},{10,11... | collective-permute-start | bytes 1572872 | tf_op jit(solution)/shard_map/ppermute | solution.py:283
  40.7 6.6 %collective-permute-start.12 = (f32[64,256]{1,0:T(8,128)S(1)}, f32[64,256]{1,0:T(8,128)S(1)}, u32[]{:S(2)}, u32[]{:S(2)}) collective-permute-start(f32[64,256]{1,0:T(8,128)S(1)} %get-tuple-element.45.refs_0_), channel_id=1, source_target_pairs={{0,12},{4,0},{8,4},{12,8},{1,13},{5,1},{9,5},{13,9},{2,14},{6,2},{... | collective-permute-start | bytes 196616 | tf_op jit(solution)/shard_map/ppermute | solution.py:283
  43.9 6.9 %collective-permute-start.13 = (f32[64,256]{1,0:T(8,128)S(1)}, f32[64,256]{1,0:T(8,128)S(1)}, u32[]{:S(2)}, u32[]{:S(2)}) collective-permute-start(f32[64,256]{1,0:T(8,128)S(1)} %get-tuple-element.45.refs_0_), channel_id=1, source_target_pairs={{0,8},{4,12},{8,0},{12,4},{1,9},{5,13},{9,1},{13,5},{2,10},{6,14},... | collective-permute-start | bytes 196616 | tf_op jit(solution)/shard_map/ppermute | solution.py:283
  44.2 6.7 %collective-permute-start.14 = (f32[64,256]{1,0:T(8,128)S(1)}, f32[64,256]{1,0:T(8,128)S(1)}, u32[]{:S(2)}, u32[]{:S(2)}) collective-permute-start(f32[64,256]{1,0:T(8,128)S(1)} %get-tuple-element.45.refs_0_), channel_id=1, source_target_pairs={{0,4},{4,8},{8,12},{12,0},{1,5},{5,9},{9,13},{13,1},{2,6},{6,10},{... | collective-permute-start | bytes 196616 | tf_op jit(solution)/shard_map/ppermute | solution.py:283
  52.4 2.4 %collective-permute-start.15 = (f32[16,64,128]{2,1,0:T(8,128)S(1)}, f32[16,64,128]{2,1,0:T(8,128)S(1)}, u32[]{:S(2)}, u32[]{:S(2)}) collective-permute-start(f32[16,64,128]{2,1,0:T(8,128)S(1)} %shard_map.133.mine), channel_id=1, source_target_pairs={{0,1},{1,0},{2,3},{3,2},{4,5},{5,4},{6,7},{7,6},{8,9},{9,8},{10,11... | collective-permute-start | bytes 1572872 | tf_op jit(solution)/shard_map/ppermute | solution.py:283
  52.5 2.3 %collective-permute-start.16 = (f32[16,32,128]{2,1,0:T(8,128)S(1)}, f32[16,32,128]{2,1,0:T(8,128)S(1)}, u32[]{:S(2)}, u32[]{:S(2)}) collective-permute-start(f32[16,32,128]{2,1,0:T(8,128)S(1)} %get-tuple-element.44.after), channel_id=1, source_target_pairs={{0,1},{1,0},{2,3},{3,2},{4,5},{5,4},{6,7},{7,6},{8,9},{9,8},{10,11... | collective-permute-start | bytes 786440 | tf_op jit(solution)/shard_map/ppermute | solution.py:283
  58.1 1.6 %collective-permute-start.17 = (f32[16,32,128]{2,1,0:T(8,128)S(1)}, f32[16,32,128]{2,1,0:T(8,128)S(1)}, u32[]{:S(2)}, u32[]{:S(2)}) collective-permute-start(f32[16,32,128]{2,1,0:T(8,128)S(1)} %get-tuple-element.49), channel_id=1, source_target_pairs={{0,1},{1,0},{2,3},{3,2},{4,5},{5,4},{6,7},{7,6},{8,9},{9,8},{10,11... | collective-permute-start | bytes 786440 | tf_op jit(solution)/shard_map/ppermute | solution.py:283
  59.8 23.2 %collective-permute-start.18 = (f32[16,32,128]{2,1,0:T(8,128)S(1)}, f32[16,32,128]{2,1,0:T(8,128)S(1)}, u32[]{:S(2)}, u32[]{:S(2)}) collective-permute-start(f32[16,32,128]{2,1,0:T(8,128)S(1)} %shard_map.136.refs_0_), channel_id=1, source_target_pairs={{0,2},{2,0},{1,3},{3,1},{4,6},{6,4},{5,7},{7,5},{8,10},{10,8},{9,1... | collective-permute-start | bytes 786440 | tf_op jit(solution)/shard_map/ppermute | solution.py:283
  65.5 6.8 %collective-permute-start.20 = (f32[4,32,128]{2,1,0:T(8,128)S(1)}, f32[4,32,128]{2,1,0:T(8,128)S(1)}, u32[]{:S(2)}, u32[]{:S(2)}) collective-permute-start(f32[4,32,128]{2,1,0:T(8,128)S(1)} %get-tuple-element.51), channel_id=1, source_target_pairs={{0,4},{4,8},{8,12},{12,0},{1,5},{5,9},{9,13},{13,1},{2,6},{6,10},{... | collective-permute-start | bytes 196616 | tf_op jit(solution)/shard_map/ppermute | solution.py:283
  65.5 8.4 %collective-permute-start.21 = (f32[4,32,128]{2,1,0:T(8,128)S(1)}, f32[4,32,128]{2,1,0:T(8,128)S(1)}, u32[]{:S(2)}, u32[]{:S(2)}) collective-permute-start(f32[4,32,128]{2,1,0:T(8,128)S(1)} %get-tuple-element.52), channel_id=1, source_target_pairs={{0,8},{4,12},{8,0},{12,4},{1,9},{5,13},{9,1},{13,5},{2,10},{6,14},... | collective-permute-start | bytes 196616 | tf_op jit(solution)/shard_map/ppermute | solution.py:283
  65.5 8.4 %collective-permute-start.22 = (f32[4,32,128]{2,1,0:T(8,128)S(1)}, f32[4,32,128]{2,1,0:T(8,128)S(1)}, u32[]{:S(2)}, u32[]{:S(2)}) collective-permute-start(f32[4,32,128]{2,1,0:T(8,128)S(1)} %get-tuple-element.53), channel_id=1, source_target_pairs={{0,12},{4,0},{8,4},{12,8},{1,13},{5,1},{9,5},{13,9},{2,14},{6,2},{... | collective-permute-start | bytes 196616 | tf_op jit(solution)/shard_map/ppermute | solution.py:283
  73.9 4.6 %collective-permute-start.23 = (f32[4,32,128]{2,1,0:T(8,128)S(1)}, f32[4,32,128]{2,1,0:T(8,128)S(1)}, u32[]{:S(2)}, u32[]{:S(2)}) collective-permute-start(f32[4,32,128]{2,1,0:T(8,128)S(1)} %shard_map.139.refs_0_), channel_id=1, source_target_pairs={{0,12},{4,0},{8,4},{12,8},{1,13},{5,1},{9,5},{13,9},{2,14},{6,2},{... | collective-permute-start | bytes 196616 | tf_op jit(solution)/shard_map/ppermute | solution.py:283
  75.8 6.3 %collective-permute-start.24 = (f32[4,32,128]{2,1,0:T(8,128)S(1)}, f32[4,32,128]{2,1,0:T(8,128)S(1)}, u32[]{:S(2)}, u32[]{:S(2)}) collective-permute-start(f32[4,32,128]{2,1,0:T(8,128)S(1)} %shard_map.139.refs_0_), channel_id=1, source_target_pairs={{0,8},{4,12},{8,0},{12,4},{1,9},{5,13},{9,1},{13,5},{2,10},{6,14},... | collective-permute-start | bytes 196616 | tf_op jit(solution)/shard_map/ppermute | solution.py:283
  76.8 6.1 %collective-permute-start.25 = (f32[4,32,128]{2,1,0:T(8,128)S(1)}, f32[4,32,128]{2,1,0:T(8,128)S(1)}, u32[]{:S(2)}, u32[]{:S(2)}) collective-permute-start(f32[4,32,128]{2,1,0:T(8,128)S(1)} %shard_map.139.refs_0_), channel_id=1, source_target_pairs={{0,4},{4,8},{8,12},{12,0},{1,5},{5,9},{9,13},{13,1},{2,6},{6,10},{... | collective-permute-start | bytes 196616 | tf_op jit(solution)/shard_map/ppermute | solution.py:283
  82.9 1.6 %collective-permute-start.26 = (f32[4,4,32,128]{3,2,1,0:T(8,128)S(1)}, f32[4,4,32,128]{3,2,1,0:T(8,128)S(1)}, u32[]{:S(2)}, u32[]{:S(2)}) collective-permute-start(f32[4,4,32,128]{3,2,1,0:T(8,128)S(1)} %shard_map.140.mine), channel_id=1, source_target_pairs={{0,1},{1,0},{2,3},{3,2},{4,5},{5,4},{6,7},{7,6},{8,9},{9,8},{10,11... | collective-permute-start | bytes 786440 | tf_op jit(solution)/shard_map/ppermute | solution.py:283
  83.0 2.3 %collective-permute-start.19 = (f32[16,32,128]{2,1,0:T(8,128)S(1)}, f32[16,32,128]{2,1,0:T(8,128)S(1)}, u32[]{:S(2)}, u32[]{:S(2)}) collective-permute-start(f32[16,32,128]{2,1,0:T(8,128)S(1)} %shard_map.137.mine), channel_id=1, source_target_pairs={{0,1},{1,0},{2,3},{3,2},{4,5},{5,4},{6,7},{7,6},{8,9},{9,8},{10,11... | collective-permute-start | bytes 786440 | tf_op jit(solution)/shard_map/ppermute | solution.py:283

commit v3 on v2

--- a/solution.py
+++ b/solution.py
@@ -116,9 +116,11 @@
     out[...] = jnp.zeros_like(out)
 
 
-def stack_ids(user, positive, negative, after, out):
-    for row, ids in enumerate((user, positive, negative)):
-        out[row:row + 1, :] = ids[...]
+def stack_ids(user, positive, negative, after, *outs):
+    for out in outs:
+        for place in range(out.shape[0]):
+            for row, ids in enumerate((user, positive, negative)):
+                out[place, row:row + 1, :] = ids[...]
 
 
 def prepare(count, rows, columns, user_emb, item_emb, user_deg, item_deg, after,
@@ -162,8 +164,7 @@
     return total
 
 
-def gather(rows, peers, mine, other, scale, *refs):
-    ids, outs, table = refs[:peers], refs[peers:2 * peers], refs[2 * peers]
+def gather(rows, peers, mine, other, scale, ids, after, out, table):
     blocks, width, size = mine.shape
     for block in range(blocks):
         span = slice(block * size, (block + 1) * size)
@@ -171,21 +172,20 @@
         for part, piece in enumerate(split3(here)):
             table[part * width:(part + 1) * width, span] = piece
     for peer in range(peers):
-        outs[peer][...] = fold(pick(table, ids[peer], rows, 2 * size), width)
-
-
-def scatter(rows, peers, after, *refs):
-    pieces, ids, out, table = refs[:peers], refs[peers:2 * peers], refs[2 * peers], refs[-1]
+        out[peer] = fold(pick(table, ids.at[peer], rows, 2 * size), width)
+
+
+def scatter(rows, peers, pieces, ids, after, out, table):
     blocks, width, size = out.shape
     tile = 2 * size
-    for place, piece in enumerate(pieces):
-        for part, value in enumerate(split3(piece[...])):
+    for place in range(peers):
+        for part, value in enumerate(split3(pieces[place])):
             table[place, part * width:(part + 1) * width, :] = value
     for start in range(0, blocks * size, tile):
         total = None
         for place in range(peers):
             term = lax.dot_general(
-                table[place], hot(ids[place], rows, start, tile), (((1,), (1,)), ((), ())),
+                table[place], hot(ids.at[place], rows, start, tile), (((1,), (1,)), ((), ())),
                 preferred_element_type=F32,
             )
             total = term if total is None else total + term
@@ -195,27 +195,26 @@
 
 
 def gather_base(user_emb, item_emb, ids, user_out, item_out):
-    tile = ids.shape[1]
-    user_out[...] = pick(user_emb, ids, [0], tile)
-    item_out[...] = pick(item_emb, ids, [1, 2], tile)
-
-
-def add_all(refs):
-    total = refs[0][...]
-    for ref in refs[1:]:
-        total = total + ref[...]
+    tile = ids.shape[2]
+    user_out[...] = pick(user_emb, ids.at[0], [0], tile)
+    item_out[...] = pick(item_emb, ids.at[0], [1, 2], tile)
+
+
+def add_parts(parts, start, peers):
+    total = parts[start]
+    for place in range(start + 1, start + peers):
+        total = total + parts[place]
     return total
 
 
-def slopes(user_parts, item_parts, *refs):
-    users, items = refs[:user_parts], refs[user_parts:user_parts + item_parts]
-    pieces, pushed = refs[user_parts + item_parts:]
-    user_rows = 0.5 * add_all(users)
-    difference = 0.5 * add_all(items)
+def slopes(users, items, user_base, item_base, pieces, pushed):
+    user_rows = 0.5 * (add_parts(users, 0, users.shape[0]) + user_base[...])
+    difference = 0.5 * (add_parts(items, 0, items.shape[0]) + item_base[...])
     margin = jnp.sum(user_rows * difference, axis=0, keepdims=True)
     slope = -jax.nn.sigmoid(-margin)
-    pieces[...] = slope * difference
-    pushed[...] = slope * user_rows
+    for out, value in ((pieces, slope * difference), (pushed, slope * user_rows)):
+        for place in range(out.shape[0]):
+            out[place] = value
 
 
 def second_pass(across, order, mine, other, source_scale, target_scale, vals, after,
@@ -235,25 +234,28 @@
         send[block] = scale * total[block, pl.ds(pl.multiple_of((1 - me) * half, half), half), :]
 
 
-def add_deal(peers, keep, received, *outs):
-    me = lax.axis_index("user")
-    per = outs[0].shape[0]
-    for offset in range(peers):
-        there = lax.rem(me + offset, peers) * per
-        for block in range(per):
-            outs[offset][block] = keep[there + block] + received[there + block]
-
-
-def sum_parts(*refs):
-    refs[-1][...] = add_all(refs[:-1])
-
-
-def pack(*refs):
-    for place, ref in enumerate(refs[:-1]):
-        refs[-1][place] = ref[...]
-
-
-def finish_users(half_grad, mine, other, out):
+def add_two(mine, other, after, out):
+    out[...] = mine[...] + other[...]
+
+
+def add_copies(peers, parts, out):
+    per = parts.shape[0] // peers
+    for block in range(per):
+        total = parts[block]
+        for peer in range(1, peers):
+            total = total + parts[peer * per + block]
+        for peer in range(peers):
+            out[peer * per + block] = total
+
+
+def add_list(*refs):
+    total = refs[0][...]
+    for ref in refs[1:-1]:
+        total = total + ref[...]
+    refs[-1][...] = total
+
+
+def finish(half_grad, mine, other, out):
     me = lax.axis_index("rep")
     blocks, width, size = half_grad.shape
     half = width // 2
@@ -264,23 +266,12 @@
             out[rows, span] = half_grad[block, rows, :] + part[block]
 
 
-def finish_items(peers, half_grad, mine, other, out):
-    me = lax.axis_index("rep")
-    place = lax.axis_index("user")
-    blocks, width, size = half_grad.shape
-    half = width // 2
-    per = blocks // peers
-    for offset in range(peers):
-        there = lax.rem(place + offset, peers) * per
-        for block in range(per):
-            span = pl.ds(pl.multiple_of((there + block) * size, size), size)
-            for rank, part in ((me, mine), (1 - me, other)):
-                rows = pl.ds(pl.multiple_of(rank * half, half), half)
-                out[rows, span] = half_grad[there + block, rows, :] + part[offset, block]
-
-
-def shift(values, axis, count, offset):
-    return lax.ppermute(values, axis, [(i, (i + offset) % count) for i in range(count)])
+def swap(values):
+    return lax.ppermute(values, "rep", [(0, 1), (1, 0)])
+
+
+def exchange(values, axis):
+    return lax.all_to_all(values, axis, 0, 0, tiled=True)
 
 
 def on_device(users, items, user_emb, item_emb, user_deg, item_deg, block_vals, block_row,
@@ -291,20 +282,19 @@
     item_blocks = item_emb.shape[1] // size
     trips = trip_user.shape[0]
     half = width // 2
-    swap = functools.partial(shift, axis="rep", count=2, offset=1)
     user_deg = user_deg.reshape(user_blocks, size)
     item_deg = item_deg.reshape(item_blocks, size)
 
     product_flops = 2 * slots * size * size * width
     product_bytes = slots * size * size * 2
     started = call(begin, shape(8, size), (), [], (), 16 * product_flops, product_bytes)
-    ids = call(
-        stack_ids, jax.ShapeDtypeStruct((3, trips), jnp.int32),
+    ids_item, ids_user = call(
+        stack_ids, [jax.ShapeDtypeStruct((peers, 3, trips), jnp.int32) for peers in (users, items)],
         [each.reshape(1, trips) for each in (trip_user, trip_pos, trip_neg)] + [started],
         [VMEM, VMEM, VMEM, ANY],
     )
-    ids_user = [ids] + [shift(ids, "item", items, -o) for o in range(1, items)]
-    ids_item = [ids] + [shift(ids, "user", users, -o) for o in range(1, users)]
+    ids = ids_user
+    ids_item, ids_user = exchange(ids_item, "user"), exchange(ids_user, "item")
     lanes = -(-slots // size) * size
 
     order_shape = jax.ShapeDtypeStruct((8, lanes), jnp.int32)
@@ -332,38 +322,33 @@
 
     hot_flops = 2 * 3 * width * trips * size
 
-    def reduced(rows, table, scale, peer_ids, axis):
-        peers, blocks = len(peer_ids), scale.shape[0]
-        dealt = call(
-            functools.partial(gather, rows, peers), [shape(width, trips)] * peers,
-            (table, swap(table), scale, *peer_ids), [VMEM] * (3 + peers),
+    def reduced(rows, table, scale, peer_ids, axis, after):
+        peers, blocks = peer_ids.shape[0], scale.shape[0]
+        return call(
+            functools.partial(gather, rows, peers), shape(peers, width, trips),
+            (table, swap(table), scale, peer_ids, after), [VMEM] * 4 + [ANY],
             [pltpu.VMEM((3 * width, blocks * size), BF16)],
             peers * blocks * hot_flops, 8 * blocks * width * size,
         )
-        return [dealt[0]] + [shift(dealt[o], axis, peers, o) for o in range(1, peers)]
-
-    item_parts = reduced([1, 2], item_table, item_scale, ids_item, "user")
-    user_parts = reduced([0], user_table, user_scale, ids_user, "item")
+
+    item_parts = reduced([1, 2], item_table, item_scale, ids_item, "user", ids)
+    user_parts = reduced([0], user_table, user_scale, ids_user, "item", item_parts)
     user_base, item_base = call(
         gather_base, [shape(width, trips)] * 2, (user_emb, item_emb, ids),
         [VMEM, VMEM, VMEM], (), 4 * width * trips * size * (user_blocks + item_blocks),
         2 * width * size * (user_blocks + item_blocks),
     )
-    user_parts.append(user_base)
-    item_parts.append(item_base)
     pieces, pushed = call(
-        functools.partial(slopes, len(user_parts), len(item_parts)),
-        [shape(width, trips)] * 2,
-        (*user_parts, *item_parts), [VMEM] * (len(user_parts) + len(item_parts)),
-        moved=4 * width * trips * (len(user_parts) + len(item_parts) + 2),
+        slopes, [shape(items, width, trips), shape(users, width, trips)],
+        (exchange(user_parts, "item"), exchange(item_parts, "user"), user_base, item_base),
+        [VMEM] * 4, moved=8 * width * trips * (users + items + 1),
     )
 
     def added(rows, own, axis, peer_ids, blocks, after):
-        peers = len(peer_ids)
-        arrays = [own] + [shift(own, axis, peers, -o) for o in range(1, peers)]
+        peers = peer_ids.shape[0]
         return call(
             functools.partial(scatter, rows, peers), shape(blocks, width, size),
-            (after, *arrays, *peer_ids), [ANY] + [VMEM] * (2 * peers),
+            (exchange(own, axis), peer_ids, after), [VMEM, VMEM, ANY],
             [pltpu.VMEM((peers, 3 * width, trips), BF16)],
             peers * blocks * hot_flops, 4 * blocks * width * size,
         )
@@ -385,31 +370,27 @@
         False, user_grad, item_order, user_scale, item_scale, pieces)
     item_grad = added([1, 2], pushed, "user", ids_item, item_blocks, item_send)
 
-    per = item_blocks // users
-    dealt = call(
-        functools.partial(add_deal, users), [shape(per, half, size)] * users,
-        (item_keep, swap(item_send)), [VMEM, VMEM], moved=12 * item_blocks * half * size,
-    )
+    dealt = call(add_two, shape(item_blocks, half, size), (item_keep, swap(item_send), item_grad),
+                 [VMEM, VMEM, ANY], moved=12 * item_blocks * half * size)
     item_half_grad, user_keep, user_send = second(
-        True, item_grad, user_order, item_scale, user_scale, dealt[0])
-    parts = [dealt[0]] + [shift(dealt[o], "user", users, o) for o in range(1, users)]
-    own = call(sum_parts, shape(per, half, size), tuple(parts), [VMEM] * users,
-               moved=4 * (users + 1) * per * half * size)
-    mine = call(pack, shape(users, per, half, size),
-                (own, *[shift(own, "user", users, -o) for o in range(1, users)]),
-                [VMEM] * users, moved=8 * item_blocks * half * size)
+        True, item_grad, user_order, item_scale, user_scale, dealt)
+    copies = call(
+        functools.partial(add_copies, users), shape(item_blocks, half, size),
+        (exchange(dealt, "user"),), [VMEM], moved=8 * item_blocks * half * size,
+    )
+    own = call(add_two, shape(user_blocks, half, size), (user_keep, swap(user_send), copies),
+               [VMEM, VMEM, ANY], moved=12 * user_blocks * half * size)
+    mine = exchange(copies, "user")
     grad_item = call(
-        functools.partial(finish_items, users), shape(width, item_blocks * size),
-        (item_half_grad, mine, swap(mine)), [VMEM] * 3, moved=12 * item_blocks * width * size,
-    )
-
-    own = call(sum_parts, shape(user_blocks, half, size), (user_keep, swap(user_send)),
-               [VMEM, VMEM], moved=12 * user_blocks * half * size)
-    mine = call(sum_parts, shape(user_blocks, half, size),
-                (own, *[shift(own, "item", items, o) for o in range(1, items)]),
-                [VMEM] * items, moved=12 * user_blocks * half * size)
+        finish, shape(width, item_blocks * size), (item_half_grad, mine, swap(mine)),
+        [VMEM] * 3, moved=12 * item_blocks * width * size,
+    )
+    come = [lax.ppermute(own, "item", [(i, (i + o) % items) for i in range(items)])
+            for o in range(1, items)]
+    mine = call(add_list, shape(user_blocks, half, size), (own, *come), [VMEM] * items,
+                moved=12 * user_blocks * half * size)
     grad_user = call(
-        finish_users, shape(width, user_blocks * size), (user_half_grad, mine, swap(mine)),
+        finish, shape(width, user_blocks * size), (user_half_grad, mine, swap(mine)),
         [VMEM] * 3, moved=12 * user_blocks * width * size,
     )
     return (grad_user, grad_item)

time: 86 us -> 108 us (1.26); the launches traced: 86.2 us -> 107 us
  blocking collectives: 0 us -> 21.6 us
  starting transfers between devices: 35.8 us -> 27 us
  local copies, waits for them, and re-layouts: 2.14 us -> 8.9 us
  Pallas kernels: 19.4 us -> 25.7 us
  waiting for transfers between devices: 27.2 us -> 21.8 us
    ppermute x27 -> x9, starting transfers between devices: 35.8 us -> 10.1 us  [the longest x8 10 us: swap(): return lax.ppermute(values, 'rep', [(0, 1), (1, 0)])]
    all_to_all x0 -> x3, blocking collectives: none -> 21.6 us  [exchange(): return lax.all_to_all(values, axis, 0, 0, tiled=True)]
    all_to_all x0 -> x5, starting transfers between devices: none -> 16.9 us  [exchange(): return lax.all_to_all(values, axis, 0, 0, tiled=True)]
    ppermute x27 -> x9, waiting for transfers between devices: 27.2 us -> 10.7 us  [the longest x1 8.22 us: on_device(): lax.ppermute(own, 'item', [(i, (i + o) % items) for i in range(items)])]
    all_to_all x0 -> x5, waiting for transfers between devices: none -> 11.1 us  [exchange(): return lax.all_to_all(values, axis, 0, 0, tiled=True)]
    unnamed x20 -> x24, local copies, waits for them, and re-layouts: 2.14 us -> 8.9 us
    pallas_call x20 -> x19, Pallas kernels: 19.4 us -> 25.7 us  [call(): pl.pallas_call(kernel, out_shape=outs, in_specs=specs, out_specs=jax.tree...]
  transfers between devices with their start and end apart: 27 -> 14, of which waited for: 15 -> 7; matrix products, arithmetic and copies ran while one was open for 0% -> 0% of each run, Pallas kernels for 7% -> 15%
where the time goes in v3:
time: 108 us; the launch traced here: 107 us
  starting transfers between devices  27 us (25%)
  Pallas kernels  25.7 us (24%)
  waiting for transfers between devices  21.8 us (20%)
  blocking collectives  21.6 us (20%)
  local copies, waits for them, and re-layouts  8.9 us (8%)
  between operations  1.74 us (2%)
    pallas_call x19, Pallas kernels, call(): pl.pallas_call(kernel, out_shape=outs, in_specs=specs, out_specs=jax.tree...  25.7 us
    all_to_all x3, blocking collectives, exchange(): return lax.all_to_all(values, axis, 0, 0, tiled=True)  21.6 us
    all_to_all x5, starting transfers between devices, exchange(): return lax.all_to_all(values, axis, 0, 0, tiled=True)  16.9 us
    all_to_all x5, waiting for transfers between devices, exchange(): return lax.all_to_all(values, axis, 0, 0, tiled=True)  11.1 us
    ppermute x8, starting transfers between devices, swap(): return lax.ppermute(values, 'rep', [(0, 1), (1, 0)])  10 us
    unnamed x24, local copies, waits for them, and re-layouts  8.9 us
    ppermute x1, waiting for transfers between devices, on_device(): lax.ppermute(own, 'item', [(i, (i + o) % items) for i in range(items)])  8.22 us
    ppermute x8, waiting for transfers between devices, swap(): return lax.ppermute(values, 'rep', [(0, 1), (1, 0)])  2.47 us
  transfers between devices with their start and end apart: 14, of which 7 were waited for; matrix products, arithmetic and copies ran while one was open for 0% of the time, Pallas kernels for 15%

profile of v3, /device:TPU:0, one launch (start us, length us, event | category | flops | bytes accessed | tf_op | source)
XLA Modules:
  0.0 106.8 jit_solution(1570261616497904585)
XLA Ops:
  0.6 0.0 copy-start.3
  0.6 0.0 copy-start.4
  0.7 0.0 copy-start.5
  0.7 0.0 copy-start.10
  0.7 0.0 copy-start.11
  0.7 0.0 copy-start.6
  0.7 0.0 copy-start.7
  0.7 0.0 copy-start.8
  0.7 0.0 copy-start.9
  0.7 0.0 copy-start
  1.5 0.0 copy-done.3
  1.6 0.6 shard_map.123
  2.2 0.0 copy-done.11
  2.2 0.0 copy-done.7
  2.2 0.9 shard_map.124
  3.1 1.5 %copy-done = bf16[288,128,128]{2,1,0:T(8,128)(2,1)S(1)} copy-done((bf16[288,128,128]{2,1,0:T(8,128)(2,1)S(1)}, bf16[288,128,128]{2,1,0:T(8,128)(2,1)}, u32[]{:S(2)}) %copy-start) | copy-done | bytes 9437208
  4.6 3.1 %shard_map.125.after.mine = f32[16,64,128]{2,1,0:T(8,128)S(1)} custom-call(s32[8,384]{1,0:T(8,128)S(1)} %get-tuple-element.21.order, bf16[288,128,128]{2,1,0:T(8,128)(2,1)S(1)} %copy-done, bf16[17,64,128]{2,1,0:T(8,128)(2,1)S(1)} %get-tuple-element.24.source, s32[2,3,256]{2,1,0:T(4,128)} %get-tuple-element.20.after.ids), custom_call_target="tpu_custom_call" | custom-call | flops 603979776 | bytes 9437184 | tf_op jit(solution)/shard_map/pallas_call | solution.py:22
  7.8 2.9 %collective-permute-start.1 = (f32[16,64,128]{2,1,0:T(8,128)S(1)}, f32[16,64,128]{2,1,0:T(8,128)S(1)}, u32[]{:S(2)}, u32[]{:S(2)}) collective-permute-start(f32[16,64,128]{2,1,0:T(8,128)S(1)} %shard_map.125.after.mine), channel_id=1, source_target_pairs={{0,1},{1,0},{2,3},{3,2},{4,5},{5,4},{6,7},{7,6},{8,9},{9,8},{10,11... | collective-permute-start | bytes 1572872 | tf_op jit(solution)/shard_map/ppermute | solution.py:270
  10.6 3.8 %shard_map.126.mine = f32[16,64,128]{2,1,0:T(8,128)S(1)} custom-call(s32[8,384]{1,0:T(8,128)S(1)} %get-tuple-element.22.order, bf16[288,128,128]{2,1,0:T(8,128)(2,1)S(1)} %copy-done, bf16[17,64,128]{2,1,0:T(8,128)(2,1)S(1)} %get-tuple-element.23.source, f32[16,64,128]{2,1,0:T(8,128)S(1)} %shard_map.125.after.mine), custom_call_target="tpu_custom_call" | custom-call | flops 603979776 | bytes 9437184 | tf_op jit(solution)/shard_map/pallas_call | solution.py:22
  14.5 3.2 %collective-permute-start = (f32[16,64,128]{2,1,0:T(8,128)S(1)}, f32[16,64,128]{2,1,0:T(8,128)S(1)}, u32[]{:S(2)}, u32[]{:S(2)}) collective-permute-start(f32[16,64,128]{2,1,0:T(8,128)S(1)} %shard_map.126.mine), channel_id=1, source_target_pairs={{0,1},{1,0},{2,3},{3,2},{4,5},{5,4},{6,7},{7,6},{8,9},{9,8},{10,11... | collective-permute-start | bytes 1572872 | tf_op jit(solution)/shard_map/ppermute | solution.py:270
  17.6 8.0 %all_to_all.40.ids = s32[4,3,256]{2,1,0:T(4,128)S(1)} all-to-all(s32[4,3,256]{2,1,0:T(4,128)S(1)} %get-tuple-element.27), channel_id=1, replica_groups=mesh['groups'=2,'user'=4,'item'=2,'rep'=2] {'user'}, dimensions={0} | all-to-all | bytes 24576 | tf_op jit(solution)/shard_map/all_to_all | solution.py:274
  25.6 3.2 %all-to-all-start = ((s32[2,3,256]{2,1,0:T(4,128)}), s32[2,3,256]{2,1,0:T(4,128)S(1)}, u32[]{:S(2)}, u32[]{:S(2)}) async-start(s32[2,3,256]{2,1,0:T(4,128)} %get-tuple-element.20.after.ids), calls=%async_computation | async-start | bytes 16384 | tf_op jit(solution)/shard_map/all_to_all | solution.py:274
  28.8 0.0 collective-permute-done.1.other
  28.8 1.9 %shard_map.127.after = f32[4,64,256]{2,1,0:T(8,128)} custom-call(f32[16,64,128]{2,1,0:T(8,128)S(1)} %shard_map.125.after.mine, f32[16,64,128]{2,1,0:T(8,128)S(1)} %collective-permute-done.1.other, f32[16,128]{1,0:T(8,128)S(1)} %get-tuple-element.26.scale.target_scale.source_scale, s32[4,3,256]{2,1,0:T(4,128)S(1)} %all_to_all.40.ids, ...), custom_call_target="tpu_custom_call" | custom-call | flops 805306368 | bytes 1048576 | tf_op jit(solution)/shard_map/pallas_call | solution.py:22
  30.8 1.8 %all-to-all-done.ids = s32[2,3,256]{2,1,0:T(4,128)S(1)} async-done(((s32[2,3,256]{2,1,0:T(4,128)}), s32[2,3,256]{2,1,0:T(4,128)S(1)}, u32[]{:S(2)}, u32[]{:S(2)}) %all-to-all-start) | async-done | bytes 6176 | tf_op jit(solution)/shard_map/all_to_all | solution.py:274
  32.6 0.0 collective-permute-done.other
  32.6 0.6 shard_map.128
  33.2 6.8 %all_to_all.41.users = f32[2,64,256]{2,1,0:T(8,128)S(1)} all-to-all(f32[2,64,256]{2,1,0:T(8,128)S(1)} %shard_map.128), channel_id=1, replica_groups=mesh['groups'=2,'user'=4,'item'=2,'rep'=2] {'item'}, dimensions={0} | all-to-all | bytes 262144 | tf_op jit(solution)/shard_map/all_to_all | solution.py:274
  40.1 3.4 %all-to-all-start.3 = ((f32[4,64,256]{2,1,0:T(8,128)}), f32[4,64,256]{2,1,0:T(8,128)S(1)}, u32[]{:S(2)}, u32[]{:S(2)}) async-start(f32[4,64,256]{2,1,0:T(8,128)} %shard_map.127.after), calls=%async_computation.3 | async-start | bytes 524288 | tf_op jit(solution)/shard_map/all_to_all | solution.py:274
  43.5 1.2 %shard_map.129 = (f32[64,256]{1,0:T(8,128)S(1)}, f32[64,256]{1,0:T(8,128)S(1)}) custom-call(bf16[64,2048]{1,0:T(8,128)(2,1)S(1)} %copy-done.6, bf16[64,2048]{1,0:T(8,128)(2,1)S(1)} %copy-done.7, s32[2,3,256]{2,1,0:T(4,128)} %get-tuple-element.20.after.ids), custom_call_target="tpu_custom_call" | custom-call | flops 268435456 | bytes 524288 | tf_op jit(solution)/shard_map/pallas_call | solution.py:22
  44.7 5.6 %all-to-all-done.3.items = f32[4,64,256]{2,1,0:T(8,128)S(1)} async-done(((f32[4,64,256]{2,1,0:T(8,128)}), f32[4,64,256]{2,1,0:T(8,128)S(1)}, u32[]{:S(2)}, u32[]{:S(2)}) %all-to-all-start.3) | async-done | bytes 262176 | tf_op jit(solution)/shard_map/all_to_all | solution.py:274
  50.2 0.8 shard_map.130
  51.0 6.8 %all_to_all.42.pieces = f32[2,64,256]{2,1,0:T(8,128)S(1)} all-to-all(f32[2,64,256]{2,1,0:T(8,128)S(1)} %get-tuple-element.30.after), channel_id=1, replica_groups=mesh['groups'=2,'user'=4,'item'=2,'rep'=2] {'item'}, dimensions={0} | all-to-all | bytes 262144 | tf_op jit(solution)/shard_map/all_to_all | solution.py:274
  57.8 0.8 shard_map.131.mine
  58.7 0.1 collective-permute-start.2
  58.8 3.4 %all-to-all-start.5 = ((f32[4,64,256]{2,1,0:T(8,128)}), f32[4,64,256]{2,1,0:T(8,128)S(1)}, u32[]{:S(2)}, u32[]{:S(2)}) async-start(f32[4,64,256]{2,1,0:T(8,128)} %get-tuple-element.32), calls=%async_computation.5 | async-start | bytes 524288 | tf_op jit(solution)/shard_map/all_to_all | solution.py:274
  62.2 0.0 collective-permute-done.2.other
  62.2 3.7 %copy-done.1 = bf16[288,128,128]{2,1,0:T(8,128)(2,1)S(1)} copy-done((bf16[288,128,128]{2,1,0:T(8,128)(2,1)S(1)}, bf16[288,128,128]{2,1,0:T(8,128)(2,1)}, u32[]{:S(2)}) %copy-start.1) | copy-done | bytes 9437208
  65.9 3.2 %shard_map.132 = (f32[16,64,128]{2,1,0:T(8,128)S(1)}, f32[16,32,128]{2,1,0:T(8,128)S(1)}, f32[16,32,128]{2,1,0:T(8,128)S(1)}) custom-call(s32[8,384]{1,0:T(8,128)S(1)} %get-tuple-element.21.order, f32[16,64,128]{2,1,0:T(8,128)S(1)} %shard_map.131.mine, f32[16,64,128]{2,1,0:T(8,128)S(1)} %collective-permute-done.2.other, ...), custom_call_target="tpu_custom_call" | custom-call | flops 603979776 | bytes 9437184 | tf_op jit(solution)/shard_map/pallas_call | solution.py:22
  69.1 2.9 %all-to-all-done.5.pieces = f32[4,64,256]{2,1,0:T(8,128)S(1)} async-done(((f32[4,64,256]{2,1,0:T(8,128)}), f32[4,64,256]{2,1,0:T(8,128)S(1)}, u32[]{:S(2)}, u32[]{:S(2)}) %all-to-all-start.5) | async-done | bytes 262176 | tf_op jit(solution)/shard_map/all_to_all | solution.py:274
  72.0 1.5 %shard_map.133.after.mine = f32[16,64,128]{2,1,0:T(8,128)S(1)} custom-call(f32[4,64,256]{2,1,0:T(8,128)S(1)} %all-to-all-done.5.pieces, s32[4,3,256]{2,1,0:T(4,128)S(1)} %all_to_all.40.ids, f32[16,32,128]{2,1,0:T(8,128)S(1)} %get-tuple-element.33.after), custom_call_target="tpu_custom_call" | custom-call | flops 805306368 | bytes 524288 | tf_op jit(solution)/shard_map/pallas_call | solution.py:22
  73.5 0.1 collective-permute-start.3
  73.6 0.5 collective-permute-start.4
  74.1 1.8 %collective-permute-done.4.other = f32[16,32,128]{2,1,0:T(8,128)S(1)} collective-permute-done((f32[16,32,128]{2,1,0:T(8,128)S(1)}, f32[16,32,128]{2,1,0:T(8,128)S(1)}, u32[]{:S(2)}, u32[]{:S(2)}) %collective-permute-start.4) | collective-permute-done | bytes 262176 | tf_op jit(solution)/shard_map/ppermute | solution.py:270
  75.8 0.7 shard_map.134.after
  76.6 3.4 %all-to-all-start.6 = ((f32[16,32,128]{2,1,0:T(8,128)}), f32[16,32,128]{2,1,0:T(8,128)S(1)}, u32[]{:S(2)}, u32[]{:S(2)}) async-start(f32[16,32,128]{2,1,0:T(8,128)} %shard_map.134.after), calls=%async_computation.6 | async-start | bytes 524288 | tf_op jit(solution)/shard_map/all_to_all | solution.py:274
  80.0 0.0 collective-permute-done.3.other
  80.0 0.0 copy-start.2
  80.0 3.7 %copy-done.2 = bf16[288,128,128]{2,1,0:T(8,128)(2,1)S(1)} copy-done((bf16[288,128,128]{2,1,0:T(8,128)(2,1)S(1)}, bf16[288,128,128]{2,1,0:T(8,128)(2,1)}, u32[]{:S(2)}) %copy-start.2) | copy-done | bytes 9437208
  83.7 4.0 %shard_map.135 = (f32[16,64,128]{2,1,0:T(8,128)S(1)}, f32[16,32,128]{2,1,0:T(8,128)S(1)}, f32[16,32,128]{2,1,0:T(8,128)S(1)}) custom-call(s32[8,384]{1,0:T(8,128)S(1)} %get-tuple-element.22.order, f32[16,64,128]{2,1,0:T(8,128)S(1)} %shard_map.133.after.mine, f32[16,64,128]{2,1,0:T(8,128)S(1)} %collective-permute-done.3.other, ...), custom_call_target="tpu_custom_call" | custom-call | flops 603979776 | bytes 9437184 | tf_op jit(solution)/shard_map/pallas_call | solution.py:22
  87.7 3.3 %collective-permute-start.5 = (f32[16,32,128]{2,1,0:T(8,128)S(1)}, f32[16,32,128]{2,1,0:T(8,128)S(1)}, u32[]{:S(2)}, u32[]{:S(2)}) collective-permute-start(f32[16,32,128]{2,1,0:T(8,128)S(1)} %get-tuple-element.36), channel_id=1, source_target_pairs={{0,1},{1,0},{2,3},{3,2},{4,5},{5,4},{6,7},{7,6},{8,9},{9,8},{10,11... | collective-permute-start | bytes 786440 | tf_op jit(solution)/shard_map/ppermute | solution.py:270
  90.9 0.0 all-to-all-done.6.parts
  90.9 0.7 shard_map.136.after
  91.7 3.4 %all-to-all-start.7 = ((f32[16,32,128]{2,1,0:T(8,128)}), f32[16,32,128]{2,1,0:T(8,128)S(1)}, u32[]{:S(2)}, u32[]{:S(2)}) async-start(f32[16,32,128]{2,1,0:T(8,128)} %shard_map.136.after), calls=%async_computation.7 | async-start | bytes 524288 | tf_op jit(solution)/shard_map/all_to_all | solution.py:274
  95.1 0.0 collective-permute-done.5.other
  95.1 0.1 collective-permute-start.6
  95.2 8.2 %collective-permute-done.6.refs_1_ = f32[16,32,128]{2,1,0:T(8,128)S(1)} collective-permute-done((f32[16,32,128]{2,1,0:T(8,128)S(1)}, f32[16,32,128]{2,1,0:T(8,128)S(1)}, u32[]{:S(2)}, u32[]{:S(2)}) %collective-permute-start.6) | collective-permute-done | bytes 262176 | tf_op jit(solution)/shard_map/ppermute | solution.py:388
  103.5 0.1 collective-permute-start.7
  103.5 0.8 all-to-all-done.7.mine
  104.4 0.0 collective-permute-start.8
  104.4 0.7 collective-permute-done.7.other
  105.1 0.8 shard_map.139
  105.9 0.0 collective-permute-done.8.other
  105.9 0.8 shard_map.140
  (10 shorter events, 0.1 us)
Async XLA Ops:
  0.6 0.9 copy-start.3
  0.6 0.9 copy-start.4
  0.7 0.9 copy-start.5
  0.7 1.5 %copy-start.10 = (s32[288]{0:T(512)S(1)}, s32[288]{0:T(512)}, u32[]{:S(2)}) copy-start(s32[288]{0:T(512)} %rows.1) | copy-start | bytes 3460
  0.7 1.5 %copy-start.11 = (s32[288]{0:T(512)S(1)}, s32[288]{0:T(512)}, u32[]{:S(2)}) copy-start(s32[288]{0:T(512)} %columns.1) | copy-start | bytes 3460
  0.7 1.5 %copy-start.6 = (bf16[64,2048]{1,0:T(8,128)(2,1)S(1)}, bf16[64,2048]{1,0:T(8,128)(2,1)}, u32[]{:S(2)}) copy-start(bf16[64,2048]{1,0:T(8,128)(2,1)} %user_emb.3) | copy-start | bytes 786436
  0.7 1.5 %copy-start.7 = (bf16[64,2048]{1,0:T(8,128)(2,1)S(1)}, bf16[64,2048]{1,0:T(8,128)(2,1)}, u32[]{:S(2)}) copy-start(bf16[64,2048]{1,0:T(8,128)(2,1)} %item_emb.3) | copy-start | bytes 786436
  0.7 1.5 %copy-start.8 = (s32[2048]{0:T(1024)S(1)}, s32[2048]{0:T(1024)}, u32[]{:S(2)}) copy-start(s32[2048]{0:T(1024)} %param.13) | copy-start | bytes 24580
  0.7 1.5 %copy-start.9 = (s32[2048]{0:T(1024)S(1)}, s32[2048]{0:T(1024)}, u32[]{:S(2)}) copy-start(s32[2048]{0:T(1024)} %param.14) | copy-start | bytes 24580
  0.7 3.9 %copy-start = (bf16[288,128,128]{2,1,0:T(8,128)(2,1)S(1)}, bf16[288,128,128]{2,1,0:T(8,128)(2,1)}, u32[]{:S(2)}) copy-start(bf16[288,128,128]{2,1,0:T(8,128)(2,1)} %vals.7) | copy-start | bytes 28311556
  7.8 21.1 %collective-permute-start.1 = (f32[16,64,128]{2,1,0:T(8,128)S(1)}, f32[16,64,128]{2,1,0:T(8,128)S(1)}, u32[]{:S(2)}, u32[]{:S(2)}) collective-permute-start(f32[16,64,128]{2,1,0:T(8,128)S(1)} %shard_map.125.after.mine), channel_id=1, source_target_pairs={{0,1},{1,0},{2,3},{3,2},{4,5},{5,4},{6,7},{7,6},{8,9},{9,8},{10,11... | collective-permute-start | bytes 1572872 | tf_op jit(solution)/shard_map/ppermute | solution.py:270
  14.5 18.1 %collective-permute-start = (f32[16,64,128]{2,1,0:T(8,128)S(1)}, f32[16,64,128]{2,1,0:T(8,128)S(1)}, u32[]{:S(2)}, u32[]{:S(2)}) collective-permute-start(f32[16,64,128]{2,1,0:T(8,128)S(1)} %shard_map.126.mine), channel_id=1, source_target_pairs={{0,1},{1,0},{2,3},{3,2},{4,5},{5,4},{6,7},{7,6},{8,9},{9,8},{10,11... | collective-permute-start | bytes 1572872 | tf_op jit(solution)/shard_map/ppermute | solution.py:270
  25.6 7.0 %all-to-all-start = ((s32[2,3,256]{2,1,0:T(4,128)}), s32[2,3,256]{2,1,0:T(4,128)S(1)}, u32[]{:S(2)}, u32[]{:S(2)}) async-start(s32[2,3,256]{2,1,0:T(4,128)} %get-tuple-element.20.after.ids), calls=%async_computation | async-start | bytes 16384 | tf_op jit(solution)/shard_map/all_to_all | solution.py:274
  40.1 10.2 %all-to-all-start.3 = ((f32[4,64,256]{2,1,0:T(8,128)}), f32[4,64,256]{2,1,0:T(8,128)S(1)}, u32[]{:S(2)}, u32[]{:S(2)}) async-start(f32[4,64,256]{2,1,0:T(8,128)} %shard_map.127.after), calls=%async_computation.3 | async-start | bytes 524288 | tf_op jit(solution)/shard_map/all_to_all | solution.py:274
  58.7 3.5 %collective-permute-start.2 = (f32[16,64,128]{2,1,0:T(8,128)S(1)}, f32[16,64,128]{2,1,0:T(8,128)S(1)}, u32[]{:S(2)}, u32[]{:S(2)}) collective-permute-start(f32[16,64,128]{2,1,0:T(8,128)S(1)} %shard_map.131.mine), channel_id=1, source_target_pairs={{0,1},{1,0},{2,3},{3,2},{4,5},{5,4},{6,7},{7,6},{8,9},{9,8},{10,11... | collective-permute-start | bytes 1572872 | tf_op jit(solution)/shard_map/ppermute | solution.py:270
  58.8 13.2 %all-to-all-start.5 = ((f32[4,64,256]{2,1,0:T(8,128)}), f32[4,64,256]{2,1,0:T(8,128)S(1)}, u32[]{:S(2)}, u32[]{:S(2)}) async-start(f32[4,64,256]{2,1,0:T(8,128)} %get-tuple-element.32), calls=%async_computation.5 | async-start | bytes 524288 | tf_op jit(solution)/shard_map/all_to_all | solution.py:274
  62.2 3.7 %copy-start.1 = (bf16[288,128,128]{2,1,0:T(8,128)(2,1)S(1)}, bf16[288,128,128]{2,1,0:T(8,128)(2,1)}, u32[]{:S(2)}) copy-start(bf16[288,128,128]{2,1,0:T(8,128)(2,1)} %vals.7) | copy-start | bytes 28311556
  73.5 6.5 %collective-permute-start.3 = (f32[16,64,128]{2,1,0:T(8,128)S(1)}, f32[16,64,128]{2,1,0:T(8,128)S(1)}, u32[]{:S(2)}, u32[]{:S(2)}) collective-permute-start(f32[16,64,128]{2,1,0:T(8,128)S(1)} %shard_map.133.after.mine), channel_id=1, source_target_pairs={{0,1},{1,0},{2,3},{3,2},{4,5},{5,4},{6,7},{7,6},{8,9},{9,8},{10,11... | collective-permute-start | bytes 1572872 | tf_op jit(solution)/shard_map/ppermute | solution.py:270
  73.6 2.3 %collective-permute-start.4 = (f32[16,32,128]{2,1,0:T(8,128)S(1)}, f32[16,32,128]{2,1,0:T(8,128)S(1)}, u32[]{:S(2)}, u32[]{:S(2)}) collective-permute-start(f32[16,32,128]{2,1,0:T(8,128)S(1)} %get-tuple-element.33.after), channel_id=1, source_target_pairs={{0,1},{1,0},{2,3},{3,2},{4,5},{5,4},{6,7},{7,6},{8,9},{9,8},{10,11... | collective-permute-start | bytes 786440 | tf_op jit(solution)/shard_map/ppermute | solution.py:270
  76.6 14.4 %all-to-all-start.6 = ((f32[16,32,128]{2,1,0:T(8,128)}), f32[16,32,128]{2,1,0:T(8,128)S(1)}, u32[]{:S(2)}, u32[]{:S(2)}) async-start(f32[16,32,128]{2,1,0:T(8,128)} %shard_map.134.after), calls=%async_computation.6 | async-start | bytes 524288 | tf_op jit(solution)/shard_map/all_to_all | solution.py:274
  80.0 3.7 %copy-start.2 = (bf16[288,128,128]{2,1,0:T(8,128)(2,1)S(1)}, bf16[288,128,128]{2,1,0:T(8,128)(2,1)}, u32[]{:S(2)}) copy-start(bf16[288,128,128]{2,1,0:T(8,128)(2,1)} %vals.7) | copy-start | bytes 28311556
  87.7 7.4 %collective-permute-start.5 = (f32[16,32,128]{2,1,0:T(8,128)S(1)}, f32[16,32,128]{2,1,0:T(8,128)S(1)}, u32[]{:S(2)}, u32[]{:S(2)}) collective-permute-start(f32[16,32,128]{2,1,0:T(8,128)S(1)} %get-tuple-element.36), channel_id=1, source_target_pairs={{0,1},{1,0},{2,3},{3,2},{4,5},{5,4},{6,7},{7,6},{8,9},{9,8},{10,11... | collective-permute-start | bytes 786440 | tf_op jit(solution)/shard_map/ppermute | solution.py:270
  91.7 12.7 %all-to-all-start.7 = ((f32[16,32,128]{2,1,0:T(8,128)}), f32[16,32,128]{2,1,0:T(8,128)S(1)}, u32[]{:S(2)}, u32[]{:S(2)}) async-start(f32[16,32,128]{2,1,0:T(8,128)} %shard_map.136.after), calls=%async_computation.7 | async-start | bytes 524288 | tf_op jit(solution)/shard_map/all_to_all | solution.py:274
  95.1 8.3 %collective-permute-start.6 = (f32[16,32,128]{2,1,0:T(8,128)S(1)}, f32[16,32,128]{2,1,0:T(8,128)S(1)}, u32[]{:S(2)}, u32[]{:S(2)}) collective-permute-start(f32[16,32,128]{2,1,0:T(8,128)S(1)} %shard_map.137.refs_0_), channel_id=1, source_target_pairs={{0,2},{2,0},{1,3},{3,1},{4,6},{6,4},{5,7},{7,5},{8,10},{10,8},{9,1... | collective-permute-start | bytes 786440 | tf_op jit(solution)/shard_map/ppermute | solution.py:388
  103.5 1.6 %collective-permute-start.7 = (f32[16,32,128]{2,1,0:T(8,128)S(1)}, f32[16,32,128]{2,1,0:T(8,128)S(1)}, u32[]{:S(2)}, u32[]{:S(2)}) collective-permute-start(f32[16,32,128]{2,1,0:T(8,128)S(1)} %shard_map.138.mine), channel_id=1, source_target_pairs={{0,1},{1,0},{2,3},{3,2},{4,5},{5,4},{6,7},{7,6},{8,9},{9,8},{10,11... | collective-permute-start | bytes 786440 | tf_op jit(solution)/shard_map/ppermute | solution.py:270
  104.4 1.5 %collective-permute-start.8 = (f32[16,32,128]{2,1,0:T(8,128)S(1)}, f32[16,32,128]{2,1,0:T(8,128)S(1)}, u32[]{:S(2)}, u32[]{:S(2)}) collective-permute-start(f32[16,32,128]{2,1,0:T(8,128)S(1)} %all-to-all-done.7.mine), channel_id=1, source_target_pairs={{0,1},{1,0},{2,3},{3,2},{4,5},{5,4},{6,7},{7,6},{8,9},{9,8},{10,11... | collective-permute-start | bytes 786440 | tf_op jit(solution)/shard_map/ppermute | solution.py:270

commit v4 on v2

--- a/solution.py
+++ b/solution.py
@@ -93,23 +93,31 @@
 
 
 def multiply_blocks(order, vals, source, total, across):
+    _, width, size = source.shape
     total[...] = jnp.zeros_like(total)
     contract = (((1,), (1,)), ((), ())) if across else (((1,), (0,)), ((), ()))
 
     def group(index, _):
         targets, terms = [], []
         for step in range(GROUP):
-            places = [(index * GROUP + step) * PACK + each for each in range(PACK)]
-            left = jnp.concatenate([source[order[1, place]] for place in places], axis=1)
-            right = jnp.concatenate([vals[order[0, place]] for place in places],
-                                    axis=1 if across else 0)
-            targets.append(order[2, places[0]])
-            terms.append(lax.dot_general(left, right, contract, preferred_element_type=F32))
+            left, right = [], []
+            for half in range(2):
+                first = ((index * GROUP + step) * 2 + half) * PACK
+                places = [first + each for each in range(PACK)]
+                left.append(jnp.concatenate([source[order[1, each]] for each in places], axis=1))
+                right.append(jnp.concatenate([vals[order[0, each]] for each in places],
+                                             axis=1 if across else 0))
+                targets.append(order[2, first])
+            both = lax.dot_general(
+                jnp.concatenate(left, axis=0), jnp.concatenate(right, axis=0 if across else 1),
+                contract, preferred_element_type=F32,
+            )
+            terms += [both[:width, :size], both[width:, size:]]
         for target, term in zip(targets, terms):
             total[target] += term
         return 0
 
-    lax.fori_loop(0, (order[3, 0] + GROUP - 1) // GROUP, group, 0)
+    lax.fori_loop(0, (order[3, 0] + 2 * GROUP - 1) // (2 * GROUP), group, 0)
 
 
 def begin(out):
@@ -141,8 +149,8 @@
         into[blocks] = jnp.zeros(into.shape[1:], BF16)
 
 
-def first_pass(across, order, vals, source, after, total):
-    multiply_blocks(order, vals, source, total, across)
+def first_pass(across, order, vals, source, *refs):
+    multiply_blocks(order, vals, source, refs[-1], across)
 
 
 def fold(stacked, width):
@@ -162,7 +170,7 @@
     return total
 
 
-def gather(rows, peers, mine, other, scale, *refs):
+def gather(rows, peers, mine, other, scale, after, *refs):
     ids, outs, table = refs[:peers], refs[peers:2 * peers], refs[2 * peers]
     blocks, width, size = mine.shape
     for block in range(blocks):
@@ -218,8 +226,17 @@
     pushed[...] = slope * user_rows
 
 
+def halves(total, keep, send):
+    me = lax.axis_index("rep")
+    half = keep.shape[1]
+    for block in range(keep.shape[0]):
+        keep[block] = total[block, pl.ds(pl.multiple_of(me * half, half), half), :]
+        send[block] = total[block, pl.ds(pl.multiple_of((1 - me) * half, half), half), :]
+
+
 def second_pass(across, order, mine, other, source_scale, target_scale, vals, after,
-                half_grad, keep, send, source, total):
+                half_grad, *refs):
+    outs, (source, total) = refs[:-2], refs[-2:]
     blocks, width, size = mine.shape
     for block in range(blocks):
         grad = mine[block] + other[block]
@@ -227,15 +244,18 @@
         source[block] = (source_scale[block:block + 1, :] * grad * 0.5).astype(BF16)
     source[blocks] = jnp.zeros((width, size), BF16)
     multiply_blocks(order, vals, source, total, across)
-    me = lax.axis_index("rep")
-    half = keep.shape[1]
-    for block in range(keep.shape[0]):
-        scale = target_scale[block:block + 1, :]
-        keep[block] = scale * total[block, pl.ds(pl.multiple_of(me * half, half), half), :]
-        send[block] = scale * total[block, pl.ds(pl.multiple_of((1 - me) * half, half), half), :]
-
-
-def add_deal(peers, keep, received, *outs):
+    scaled = outs[0] if len(outs) == 1 else total
+    for block in range(total.shape[0]):
+        scaled[block] = target_scale[block:block + 1, :] * total[block]
+    if len(outs) == 2:
+        halves(total, *outs)
+
+
+def halves_after(total, after, keep, send):
+    halves(total, keep, send)
+
+
+def add_deal(peers, keep, received, after, *outs):
     me = lax.axis_index("user")
     per = outs[0].shape[0]
     for offset in range(peers):
@@ -246,6 +266,10 @@
 
 def sum_parts(*refs):
     refs[-1][...] = add_all(refs[:-1])
+
+
+def sum_after(after, *refs):
+    sum_parts(*refs)
 
 
 def pack(*refs):
@@ -324,26 +348,28 @@
         (item_order, block_vals, user_source, ids), [SMEM, VMEM, VMEM, ANY], (),
         product_flops, product_bytes,
     )
+    ids_here = [*ids_item[1:], *ids_user[1:]]
     user_table = call(
         functools.partial(first_pass, True), shape(user_blocks, width, size),
-        (user_order, block_vals, item_source, item_table), [SMEM, VMEM, VMEM, ANY], (),
+        (user_order, block_vals, item_source, item_table, *ids_here),
+        [SMEM, VMEM, VMEM] + [ANY] * (1 + len(ids_here)), (),
         product_flops, product_bytes,
     )
 
     hot_flops = 2 * 3 * width * trips * size
 
-    def reduced(rows, table, scale, peer_ids, axis):
+    def reduced(rows, table, scale, peer_ids, axis, after):
         peers, blocks = len(peer_ids), scale.shape[0]
         dealt = call(
             functools.partial(gather, rows, peers), [shape(width, trips)] * peers,
-            (table, swap(table), scale, *peer_ids), [VMEM] * (3 + peers),
+            (table, swap(table), scale, after, *peer_ids), [VMEM] * 3 + [ANY] + [VMEM] * peers,
             [pltpu.VMEM((3 * width, blocks * size), BF16)],
             peers * blocks * hot_flops, 8 * blocks * width * size,
         )
         return [dealt[0]] + [shift(dealt[o], axis, peers, o) for o in range(1, peers)]
 
-    item_parts = reduced([1, 2], item_table, item_scale, ids_item, "user")
-    user_parts = reduced([0], user_table, user_scale, ids_user, "item")
+    item_parts = reduced([1, 2], item_table, item_scale, ids_item, "user", ids)
+    user_parts = reduced([0], user_table, user_scale, ids_user, "item", item_parts[0])
     user_base, item_base = call(
         gather_base, [shape(width, trips)] * 2, (user_emb, item_emb, ids),
         [VMEM, VMEM, VMEM], (), 4 * width * trips * size * (user_blocks + item_blocks),
@@ -368,11 +394,12 @@
             peers * blocks * hot_flops, 4 * blocks * width * size,
         )
 
-    def second(across, grad, order, source_scale, target_scale, after):
+    def second(across, grad, order, source_scale, target_scale, after, divided):
         sources, targets = source_scale.shape[0], target_scale.shape[0]
         return call(
             functools.partial(second_pass, across),
-            [shape(sources, width, size), shape(targets, half, size), shape(targets, half, size)],
+            [shape(sources, width, size)]
+            + ([shape(targets, half, size)] * 2 if divided else [shape(targets, width, size)]),
             (order, grad, swap(grad), source_scale, target_scale, block_vals, after),
             [SMEM, VMEM, VMEM, VMEM, VMEM, VMEM, ANY],
             [pltpu.VMEM((sources + 1, width, size), BF16),
@@ -381,28 +408,41 @@
         )
 
     user_grad = added([0], pieces, "item", ids_user, user_blocks, pieces)
+    user_grad = added([0], pieces, "item", ids_user, user_blocks, pieces)
+    def divided(total, after):
+        blocks = total.shape[0]
+        return call(halves, [shape(blocks, half, size)] * 2, (total, after), [VMEM, ANY],
+                    moved=8 * blocks * width * size)
+
+    user_grad = added([0], pieces, "item", ids_user, user_blocks, pieces)
     user_half_grad, item_keep, item_send = second(
-        False, user_grad, item_order, user_scale, item_scale, pieces)
+        False, user_grad, item_order, user_scale, item_scale, pieces, True)
     item_grad = added([1, 2], pushed, "user", ids_item, item_blocks, item_send)
 
     per = item_blocks // users
     dealt = call(
         functools.partial(add_deal, users), [shape(per, half, size)] * users,
-        (item_keep, swap(item_send)), [VMEM, VMEM], moved=12 * item_blocks * half * size,
-    )
-    item_half_grad, user_keep, user_send = second(
-        True, item_grad, user_order, item_scale, user_scale, dealt[0])
+        (item_keep, swap(item_send), item_grad), [VMEM, VMEM, ANY],
+        moved=12 * item_blocks * half * size,
+    )
+    item_half_grad, user_back = second(
+        True, item_grad, user_order, item_scale, user_scale, dealt[0], False)
     parts = [dealt[0]] + [shift(dealt[o], "user", users, o) for o in range(1, users)]
-    own = call(sum_parts, shape(per, half, size), tuple(parts), [VMEM] * users,
+    item_own = call(sum_after, shape(per, half, size), (user_back, *parts),
+                    [ANY] + [VMEM] * users,
                moved=4 * (users + 1) * per * half * size)
     mine = call(pack, shape(users, per, half, size),
-                (own, *[shift(own, "user", users, -o) for o in range(1, users)]),
+                (item_own, *[shift(item_own, "user", users, -o) for o in range(1, users)]),
                 [VMEM] * users, moved=8 * item_blocks * half * size)
     grad_item = call(
         functools.partial(finish_items, users), shape(width, item_blocks * size),
         (item_half_grad, mine, swap(mine)), [VMEM] * 3, moved=12 * item_blocks * width * size,
     )
 
+    user_keep, user_send = call(
+        halves_after, [shape(user_blocks, half, size)] * 2, (user_back, item_own), [VMEM, ANY],
+        moved=8 * user_blocks * width * size,
+    )
     own = call(sum_parts, shape(user_blocks, half, size), (user_keep, swap(user_send)),
                [VMEM, VMEM], moved=12 * user_blocks * half * size)
     mine = call(sum_parts, shape(user_blocks, half, size),

time: 86 us -> 77.1 us (0.90)
  starting transfers between devices: 35.8 us -> 29.3 us
  waiting for transfers between devices: 27.2 us -> 24.4 us
    ppermute x27, starting transfers between devices: 35.8 us -> 29.3 us  [shift(): lax.ppermute(values, axis, [(i, (i + offset) % count) for i in range(coun...]
    ppermute x27, waiting for transfers between devices: 27.2 us -> 24.4 us  [shift(): lax.ppermute(values, axis, [(i, (i + offset) % count) for i in range(coun...]
    pallas_call x20 -> x21, Pallas kernels: 19.4 us -> 19.1 us  [call(): pl.pallas_call(kernel, out_shape=outs, in_specs=specs, out_specs=jax.tree...]
  transfers between devices with their start and end apart: 27 -> 27, of which waited for: 15 -> 15; matrix products, arithmetic and copies ran while one was open for 0% -> 0% of each run, Pallas kernels for 7% -> 16%
where the time goes in v4:
time: 77.1 us; the launch traced here: 76.8 us
  starting transfers between devices  29.3 us (38%)
  waiting for transfers between devices  24.4 us (32%)
  Pallas kernels  19.1 us (25%)
  local copies, waits for them, and re-layouts  2.16 us (3%)
  between operations  1.77 us (2%)
    ppermute x27, starting transfers between devices, shift(): lax.ppermute(values, axis, [(i, (i + offset) % count) for i in range(coun...  29.3 us
    ppermute x27, waiting for transfers between devices, shift(): lax.ppermute(values, axis, [(i, (i + offset) % count) for i in range(coun...  24.4 us
    pallas_call x21, Pallas kernels, call(): pl.pallas_call(kernel, out_shape=outs, in_specs=specs, out_specs=jax.tree...  19.1 us
    unnamed x20, local copies, waits for them, and re-layouts  2.16 us
  transfers between devices with their start and end apart: 27, of which 15 were waited for; matrix products, arithmetic and copies ran while one was open for 0% of the time, Pallas kernels for 16%

profile of v4, /device:TPU:0, one launch (start us, length us, event | category | flops | bytes accessed | tf_op | source)
XLA Modules:
  0.0 76.8 jit_solution(13379557137012515117)
XLA Ops:
  1.6 0.0 copy-done.5
  1.6 0.1 copy-done.4
  1.7 0.9 %shard_map.124 = (bf16[17,64,128]{2,1,0:T(8,128)(2,1)S(1)}, bf16[17,64,128]{2,1,0:T(8,128)(2,1)S(1)}, f32[16,128]{1,0:T(8,128)S(1)}, f32[16,128]{1,0:T(8,128)S(1...) custom-call(s32[1]{0:T(128)S(6)} %copy.13.count, s32[288]{0:T(512)S(1)} %copy-done.8, s32[288]{0:T(512)S(1)} %copy-done.9, ...), custom_call_target="tpu_custom_call" | custom-call | flops 603979776 | bytes 9437184 | tf_op jit(solution)/shard_map/pallas_call | solution.py:22
  2.6 2.0 %copy-done = bf16[288,128,128]{2,1,0:T(8,128)(2,1)S(1)} copy-done((bf16[288,128,128]{2,1,0:T(8,128)(2,1)S(1)}, bf16[288,128,128]{2,1,0:T(8,128)(2,1)}, u32[]{:S(2)}) %copy-start) | copy-done | bytes 9437208
  4.6 2.5 %shard_map.125.refs_0_.mine = f32[16,64,128]{2,1,0:T(8,128)S(1)} custom-call(s32[8,384]{1,0:T(8,128)S(1)} %get-tuple-element.29.order, bf16[288,128,128]{2,1,0:T(8,128)(2,1)S(1)} %copy-done, bf16[17,64,128]{2,1,0:T(8,128)(2,1)S(1)} %get-tuple-element.32.source, s32[3,256]{1,0:T(4,128)S(1)} %shard_map.123.after.refs_0_.ids.refs_2_.refs_4_), custom_call_target="tpu_custom_call" | custom-call | flops 603979776 | bytes 9437184 | tf_op jit(solution)/shard_map/pallas_call | solution.py:22
  7.1 0.5 collective-permute-start.5
  7.6 2.6 %collective-permute-start.3 = (s32[3,256]{1,0:T(4,128)S(1)}, s32[3,256]{1,0:T(4,128)S(1)}, u32[]{:S(2)}, u32[]{:S(2)}) collective-permute-start(s32[3,256]{1,0:T(4,128)S(1)} %shard_map.123.after.refs_0_.ids.refs_2_.refs_4_), channel_id=1, source_target_pairs={{0,2},{2,0},{1,3},{3,1},{4,6},{6,4},{5,7},{7,5},{8,10},{10,8},{9,1... | collective-permute-start | bytes 9224 | tf_op jit(solution)/shard_map/ppermute | solution.py:307
  10.2 1.3 %collective-permute-start.2 = (s32[3,256]{1,0:T(4,128)S(1)}, s32[3,256]{1,0:T(4,128)S(1)}, u32[]{:S(2)}, u32[]{:S(2)}) collective-permute-start(s32[3,256]{1,0:T(4,128)S(1)} %shard_map.123.after.refs_0_.ids.refs_2_.refs_4_), channel_id=1, source_target_pairs={{0,4},{4,8},{8,12},{12,0},{1,5},{5,9},{9,13},{13,1},{2,6},{6,10},{... | collective-permute-start | bytes 9224 | tf_op jit(solution)/shard_map/ppermute | solution.py:307
  11.5 3.1 %collective-permute-start.1 = (s32[3,256]{1,0:T(4,128)S(1)}, s32[3,256]{1,0:T(4,128)S(1)}, u32[]{:S(2)}, u32[]{:S(2)}) collective-permute-start(s32[3,256]{1,0:T(4,128)S(1)} %shard_map.123.after.refs_0_.ids.refs_2_.refs_4_), channel_id=1, source_target_pairs={{0,8},{4,12},{8,0},{12,4},{1,9},{5,13},{9,1},{13,5},{2,10},{6,14},... | collective-permute-start | bytes 9224 | tf_op jit(solution)/shard_map/ppermute | solution.py:307
  14.7 1.0 %collective-permute-start = (s32[3,256]{1,0:T(4,128)S(1)}, s32[3,256]{1,0:T(4,128)S(1)}, u32[]{:S(2)}, u32[]{:S(2)}) collective-permute-start(s32[3,256]{1,0:T(4,128)S(1)} %shard_map.123.after.refs_0_.ids.refs_2_.refs_4_), channel_id=1, source_target_pairs={{0,12},{4,0},{8,4},{12,8},{1,13},{5,1},{9,5},{13,9},{2,14},{6,2},{... | collective-permute-start | bytes 9224 | tf_op jit(solution)/shard_map/ppermute | solution.py:307
  15.7 0.0 collective-permute-done.3.refs_4_.refs_1_.refs_3_
  15.7 0.0 collective-permute-done.2.refs_3_.refs_7_
  15.7 0.5 collective-permute-done.1.refs_2_.refs_6_
  16.3 2.0 %collective-permute-done.refs_1_.refs_5_ = s32[3,256]{1,0:T(4,128)S(1)} collective-permute-done((s32[3,256]{1,0:T(4,128)S(1)}, s32[3,256]{1,0:T(4,128)S(1)}, u32[]{:S(2)}, u32[]{:S(2)}) %collective-permute-start) | collective-permute-done | bytes 3104 | tf_op jit(solution)/shard_map/ppermute | solution.py:307
  18.3 3.2 %shard_map.126.mine = f32[16,64,128]{2,1,0:T(8,128)S(1)} custom-call(s32[8,384]{1,0:T(8,128)S(1)} %get-tuple-element.30.order, bf16[288,128,128]{2,1,0:T(8,128)(2,1)S(1)} %copy-done, bf16[17,64,128]{2,1,0:T(8,128)(2,1)S(1)} %get-tuple-element.31.source, f32[16,64,128]{2,1,0:T(8,128)S(1)} %shard_map.125.refs_0_.mine, ...), custom_call_target="tpu_custom_call" | custom-call | flops 603979776 | bytes 9437184 | tf_op jit(solution)/shard_map/pallas_call | solution.py:22
  21.5 0.1 collective-permute-start.4
  21.6 0.0 collective-permute-done.5.other
  21.6 1.2 %shard_map.127 = (f32[64,256]{1,0:T(8,128)S(1)}, f32[64,256]{1,0:T(8,128)S(1)}, f32[64,256]{1,0:T(8,128)S(1)}, f32[64,256]{1,0:T(8,128)S(1)}) custom-call(f32[16,64,128]{2,1,0:T(8,128)S(1)} %shard_map.125.refs_0_.mine, f32[16,64,128]{2,1,0:T(8,128)S(1)} %collective-permute-done.5.other, f32[16,128]{1,0:T(8,128)S(1)} %get-tuple-element.34.scale.target_scale.source_scale, ...), custom_call_target="tpu_custom_call" | custom-call | flops 805306368 | bytes 1048576 | tf_op jit(solution)/shard_map/pallas_call | solution.py:22
  22.8 0.1 collective-permute-start.7
  22.9 6.3 %collective-permute-start.8 = (f32[64,256]{1,0:T(8,128)S(1)}, f32[64,256]{1,0:T(8,128)S(1)}, u32[]{:S(2)}, u32[]{:S(2)}) collective-permute-start(f32[64,256]{1,0:T(8,128)S(1)} %get-tuple-element.40), channel_id=1, source_target_pairs={{0,8},{4,12},{8,0},{12,4},{1,9},{5,13},{9,1},{13,5},{2,10},{6,14},... | collective-permute-start | bytes 196616 | tf_op jit(solution)/shard_map/ppermute | solution.py:307
  29.2 0.6 shard_map.128
  29.8 0.1 collective-permute-start.6
  29.9 0.5 shard_map.129
  30.4 1.3 %collective-permute-done.7.refs_4_ = f32[64,256]{1,0:T(8,128)S(1)} collective-permute-done((f32[64,256]{1,0:T(8,128)S(1)}, f32[64,256]{1,0:T(8,128)S(1)}, u32[]{:S(2)}, u32[]{:S(2)}) %collective-permute-start.7) | collective-permute-done | bytes 65568 | tf_op jit(solution)/shard_map/ppermute | solution.py:307
  31.7 2.6 %collective-permute-done.8.refs_5_ = f32[64,256]{1,0:T(8,128)S(1)} collective-permute-done((f32[64,256]{1,0:T(8,128)S(1)}, f32[64,256]{1,0:T(8,128)S(1)}, u32[]{:S(2)}, u32[]{:S(2)}) %collective-permute-start.8) | collective-permute-done | bytes 65568 | tf_op jit(solution)/shard_map/ppermute | solution.py:307
  34.3 0.5 collective-permute-done.9.refs_6_
  34.8 0.0 collective-permute-done.6.refs_1_
  34.8 0.1 shard_map.130
  34.9 0.1 collective-permute-start.10
  34.9 4.3 %collective-permute-done.10.refs_1_ = f32[64,256]{1,0:T(8,128)S(1)} collective-permute-done((f32[64,256]{1,0:T(8,128)S(1)}, f32[64,256]{1,0:T(8,128)S(1)}, u32[]{:S(2)}, u32[]{:S(2)}) %collective-permute-start.10) | collective-permute-done | bytes 65568 | tf_op jit(solution)/shard_map/ppermute | solution.py:307
  39.2 0.8 %shard_map.131.mine = f32[16,64,128]{2,1,0:T(8,128)S(1)} custom-call(f32[64,256]{1,0:T(8,128)S(1)} %get-tuple-element.43.after.refs_0_, f32[64,256]{1,0:T(8,128)S(1)} %get-tuple-element.43.after.refs_0_, f32[64,256]{1,0:T(8,128)S(1)} %collective-permute-done.10.refs_1_, s32[3,256]{1,0:T(4,128)S(1)} %shard_map.123.after.refs_0_.ids.refs_2_.refs_4_, ...), custom_call_target="tpu_custom_call" | custom-call | flops 402653184 | bytes 524288 | tf_op jit(solution)/shard_map/pallas_call | solution.py:22
  40.0 0.1 collective-permute-start.11
  40.1 1.5 %collective-permute-start.14 = (f32[64,256]{1,0:T(8,128)S(1)}, f32[64,256]{1,0:T(8,128)S(1)}, u32[]{:S(2)}, u32[]{:S(2)}) collective-permute-start(f32[64,256]{1,0:T(8,128)S(1)} %get-tuple-element.46.refs_0_), channel_id=1, source_target_pairs={{0,4},{4,8},{8,12},{12,0},{1,5},{5,9},{9,13},{13,1},{2,6},{6,10},{... | collective-permute-start | bytes 196616 | tf_op jit(solution)/shard_map/ppermute | solution.py:307
  41.6 1.3 %collective-permute-start.13 = (f32[64,256]{1,0:T(8,128)S(1)}, f32[64,256]{1,0:T(8,128)S(1)}, u32[]{:S(2)}, u32[]{:S(2)}) collective-permute-start(f32[64,256]{1,0:T(8,128)S(1)} %get-tuple-element.46.refs_0_), channel_id=1, source_target_pairs={{0,8},{4,12},{8,0},{12,4},{1,9},{5,13},{9,1},{13,5},{2,10},{6,14},... | collective-permute-start | bytes 196616 | tf_op jit(solution)/shard_map/ppermute | solution.py:307
  42.9 1.1 %collective-permute-start.12 = (f32[64,256]{1,0:T(8,128)S(1)}, f32[64,256]{1,0:T(8,128)S(1)}, u32[]{:S(2)}, u32[]{:S(2)}) collective-permute-start(f32[64,256]{1,0:T(8,128)S(1)} %get-tuple-element.46.refs_0_), channel_id=1, source_target_pairs={{0,12},{4,0},{8,4},{12,8},{1,13},{5,1},{9,5},{13,9},{2,14},{6,2},{... | collective-permute-start | bytes 196616 | tf_op jit(solution)/shard_map/ppermute | solution.py:307
  44.1 0.0 collective-permute-done.11.other
  44.1 2.6 %shard_map.132 = (f32[16,64,128]{2,1,0:T(8,128)S(1)}, f32[16,32,128]{2,1,0:T(8,128)S(1)}, f32[16,32,128]{2,1,0:T(8,128)S(1)}) custom-call(s32[8,384]{1,0:T(8,128)S(1)} %get-tuple-element.29.order, f32[16,64,128]{2,1,0:T(8,128)S(1)} %shard_map.131.mine, f32[16,64,128]{2,1,0:T(8,128)S(1)} %collective-permute-done.11.other, ...), custom_call_target="tpu_custom_call" | custom-call | flops 603979776 | bytes 9437184 | tf_op jit(solution)/shard_map/pallas_call | solution.py:22
  46.6 0.3 collective-permute-done.14.refs_3_
  46.9 2.3 %collective-permute-done.13.refs_2_ = f32[64,256]{1,0:T(8,128)S(1)} collective-permute-done((f32[64,256]{1,0:T(8,128)S(1)}, f32[64,256]{1,0:T(8,128)S(1)}, u32[]{:S(2)}, u32[]{:S(2)}) %collective-permute-start.13) | collective-permute-done | bytes 65568 | tf_op jit(solution)/shard_map/ppermute | solution.py:307
  49.3 0.0 collective-permute-done.12.refs_1_
  49.3 1.5 %shard_map.133.after.mine = f32[16,64,128]{2,1,0:T(8,128)S(1)} custom-call(f32[16,32,128]{2,1,0:T(8,128)S(1)} %get-tuple-element.45.after, f32[64,256]{1,0:T(8,128)S(1)} %get-tuple-element.46.refs_0_, f32[64,256]{1,0:T(8,128)S(1)} %collective-permute-done.12.refs_1_, f32[64,256]{1,0:T(8,128)S(1)} %collective-permute-done.13.refs_2_, ...), custom_call_target="tpu_custom_call" | custom-call | flops 805306368 | bytes 524288 | tf_op jit(solution)/shard_map/pallas_call | solution.py:22
  50.8 0.1 collective-permute-start.15
  50.9 0.5 collective-permute-start.16
  51.4 1.8 %collective-permute-done.16.received = f32[16,32,128]{2,1,0:T(8,128)S(1)} collective-permute-done((f32[16,32,128]{2,1,0:T(8,128)S(1)}, f32[16,32,128]{2,1,0:T(8,128)S(1)}, u32[]{:S(2)}, u32[]{:S(2)}) %collective-permute-start.16) | collective-permute-done | bytes 262176 | tf_op jit(solution)/shard_map/ppermute | solution.py:307
  53.2 1.9 %collective-permute-start.17 = (f32[4,32,128]{2,1,0:T(8,128)S(1)}, f32[4,32,128]{2,1,0:T(8,128)S(1)}, u32[]{:S(2)}, u32[]{:S(2)}) collective-permute-start(f32[4,32,128]{2,1,0:T(8,128)S(1)} %get-tuple-element.50), channel_id=1, source_target_pairs={{0,4},{4,8},{8,12},{12,0},{1,5},{5,9},{9,13},{13,1},{2,6},{6,10},{... | collective-permute-start | bytes 196616 | tf_op jit(solution)/shard_map/ppermute | solution.py:307
  55.1 1.2 %collective-permute-start.18 = (f32[4,32,128]{2,1,0:T(8,128)S(1)}, f32[4,32,128]{2,1,0:T(8,128)S(1)}, u32[]{:S(2)}, u32[]{:S(2)}) collective-permute-start(f32[4,32,128]{2,1,0:T(8,128)S(1)} %get-tuple-element.51), channel_id=1, source_target_pairs={{0,8},{4,12},{8,0},{12,4},{1,9},{5,13},{9,1},{13,5},{2,10},{6,14},... | collective-permute-start | bytes 196616 | tf_op jit(solution)/shard_map/ppermute | solution.py:307
  56.3 1.3 %collective-permute-start.19 = (f32[4,32,128]{2,1,0:T(8,128)S(1)}, f32[4,32,128]{2,1,0:T(8,128)S(1)}, u32[]{:S(2)}, u32[]{:S(2)}) collective-permute-start(f32[4,32,128]{2,1,0:T(8,128)S(1)} %get-tuple-element.52), channel_id=1, source_target_pairs={{0,12},{4,0},{8,4},{12,8},{1,13},{5,1},{9,5},{13,9},{2,14},{6,2},{... | collective-permute-start | bytes 196616 | tf_op jit(solution)/shard_map/ppermute | solution.py:307
  57.6 3.3 %shard_map.135 = (f32[16,64,128]{2,1,0:T(8,128)S(1)}, f32[16,64,128]{2,1,0:T(8,128)S(1)}) custom-call(s32[8,384]{1,0:T(8,128)S(1)} %get-tuple-element.30.order, f32[16,64,128]{2,1,0:T(8,128)S(1)} %shard_map.133.after.mine, f32[16,64,128]{2,1,0:T(8,128)S(1)} %collective-permute-done.15.other, f32[16,128]{1,0:T(8,128)S(1)} %get-tuple-element.34.scale.target_scale.source_scale, ...), custom_call_target="tpu_custom_call" | custom-call | flops 603979776 | bytes 9437184 | tf_op jit(solution)/shard_map/pallas_call | solution.py:22
  60.9 0.0 collective-permute-done.17.refs_1_
  60.9 1.1 %collective-permute-done.18.refs_2_ = f32[4,32,128]{2,1,0:T(8,128)S(1)} collective-permute-done((f32[4,32,128]{2,1,0:T(8,128)S(1)}, f32[4,32,128]{2,1,0:T(8,128)S(1)}, u32[]{:S(2)}, u32[]{:S(2)}) %collective-permute-start.18) | collective-permute-done | bytes 65568 | tf_op jit(solution)/shard_map/ppermute | solution.py:307
  62.2 0.1 collective-permute-start.20
  62.2 1.5 %collective-permute-done.20.refs_1_ = f32[16,32,128]{2,1,0:T(8,128)S(1)} collective-permute-done((f32[16,32,128]{2,1,0:T(8,128)S(1)}, f32[16,32,128]{2,1,0:T(8,128)S(1)}, u32[]{:S(2)}, u32[]{:S(2)}) %collective-permute-start.20) | collective-permute-done | bytes 262176 | tf_op jit(solution)/shard_map/ppermute | solution.py:307
  63.8 0.1 collective-permute-start.21
  63.9 1.9 %collective-permute-start.25 = (f32[4,32,128]{2,1,0:T(8,128)S(1)}, f32[4,32,128]{2,1,0:T(8,128)S(1)}, u32[]{:S(2)}, u32[]{:S(2)}) collective-permute-start(f32[4,32,128]{2,1,0:T(8,128)S(1)} %shard_map.136.after.refs_0_), channel_id=1, source_target_pairs={{0,4},{4,8},{8,12},{12,0},{1,5},{5,9},{9,13},{13,1},{2,6},{6,10},{... | collective-permute-start | bytes 196616 | tf_op jit(solution)/shard_map/ppermute | solution.py:307
  65.8 2.5 %collective-permute-start.24 = (f32[4,32,128]{2,1,0:T(8,128)S(1)}, f32[4,32,128]{2,1,0:T(8,128)S(1)}, u32[]{:S(2)}, u32[]{:S(2)}) collective-permute-start(f32[4,32,128]{2,1,0:T(8,128)S(1)} %shard_map.136.after.refs_0_), channel_id=1, source_target_pairs={{0,8},{4,12},{8,0},{12,4},{1,9},{5,13},{9,1},{13,5},{2,10},{6,14},... | collective-permute-start | bytes 196616 | tf_op jit(solution)/shard_map/ppermute | solution.py:307
  68.3 2.5 %collective-permute-done.25.refs_3_ = f32[4,32,128]{2,1,0:T(8,128)S(1)} collective-permute-done((f32[4,32,128]{2,1,0:T(8,128)S(1)}, f32[4,32,128]{2,1,0:T(8,128)S(1)}, u32[]{:S(2)}, u32[]{:S(2)}) %collective-permute-start.25) | collective-permute-done | bytes 65568 | tf_op jit(solution)/shard_map/ppermute | solution.py:307
  70.7 2.3 %collective-permute-done.24.refs_2_ = f32[4,32,128]{2,1,0:T(8,128)S(1)} collective-permute-done((f32[4,32,128]{2,1,0:T(8,128)S(1)}, f32[4,32,128]{2,1,0:T(8,128)S(1)}, u32[]{:S(2)}, u32[]{:S(2)}) %collective-permute-start.24) | collective-permute-done | bytes 65568 | tf_op jit(solution)/shard_map/ppermute | solution.py:307
  73.0 0.5 collective-permute-done.23.refs_1_
  73.5 0.1 collective-permute-start.26
  73.6 0.5 collective-permute-start.22
  74.2 0.9 %collective-permute-done.26.other = f32[4,4,32,128]{3,2,1,0:T(8,128)S(1)} collective-permute-done((f32[4,4,32,128]{3,2,1,0:T(8,128)S(1)}, f32[4,4,32,128]{3,2,1,0:T(8,128)S(1)}, u32[]{:S(2)}, u32[]{:S(2)}) %collective-permute-start.26) | collective-permute-done | bytes 262176 | tf_op jit(solution)/shard_map/ppermute | solution.py:307
  75.1 0.9 %shard_map.142 = f32[64,2048]{1,0:T(8,128)} custom-call(f32[16,64,128]{2,1,0:T(8,128)S(1)} %get-tuple-element.55.half_grad, f32[4,4,32,128]{3,2,1,0:T(8,128)S(1)} %shard_map.141.mine, f32[4,4,32,128]{3,2,1,0:T(8,128)S(1)} %collective-permute-done.26.other), custom_call_target="tpu_custom_call" | custom-call | bytes 1572864 | tf_op jit(solution)/shard_map/pallas_call | solution.py:22
  75.9 0.0 collective-permute-done.22.other
  75.9 0.8 %shard_map.140 = f32[64,2048]{1,0:T(8,128)} custom-call(f32[16,64,128]{2,1,0:T(8,128)S(1)} %get-tuple-element.44.half_grad, f32[16,32,128]{2,1,0:T(8,128)S(1)} %shard_map.139.mine, f32[16,32,128]{2,1,0:T(8,128)S(1)} %collective-permute-done.22.other), custom_call_target="tpu_custom_call" | custom-call | bytes 1572864 | tf_op jit(solution)/shard_map/pallas_call | solution.py:22
  (31 shorter events, 0.2 us)
Async XLA Ops:
  0.6 0.9 %copy-start.3 = (s32[256]{0:T(256)S(1)}, s32[256]{0:T(256)}, u32[]{:S(2)}) copy-start(s32[256]{0:T(256)} %param.21) | copy-start | bytes 3076
  0.6 0.9 %copy-start.2 = (s32[256]{0:T(256)S(1)}, s32[256]{0:T(256)}, u32[]{:S(2)}) copy-start(s32[256]{0:T(256)} %param.20) | copy-start | bytes 3076
  0.7 0.9 %copy-start.1 = (s32[256]{0:T(256)S(1)}, s32[256]{0:T(256)}, u32[]{:S(2)}) copy-start(s32[256]{0:T(256)} %param.19) | copy-start | bytes 3076
  0.7 1.0 %copy-start.5 = (bf16[64,2048]{1,0:T(8,128)(2,1)S(1)}, bf16[64,2048]{1,0:T(8,128)(2,1)}, u32[]{:S(2)}) copy-start(bf16[64,2048]{1,0:T(8,128)(2,1)} %item_emb.3) | copy-start | bytes 786436
  0.7 1.0 %copy-start.4 = (bf16[64,2048]{1,0:T(8,128)(2,1)S(1)}, bf16[64,2048]{1,0:T(8,128)(2,1)}, u32[]{:S(2)}) copy-start(bf16[64,2048]{1,0:T(8,128)(2,1)} %user_emb.3) | copy-start | bytes 786436
  0.7 1.0 %copy-start.9 = (s32[288]{0:T(512)S(1)}, s32[288]{0:T(512)}, u32[]{:S(2)}) copy-start(s32[288]{0:T(512)} %columns.1) | copy-start | bytes 3460
  0.7 1.0 %copy-start.8 = (s32[288]{0:T(512)S(1)}, s32[288]{0:T(512)}, u32[]{:S(2)}) copy-start(s32[288]{0:T(512)} %rows.1) | copy-start | bytes 3460
  0.7 1.0 %copy-start.7 = (s32[2048]{0:T(1024)S(1)}, s32[2048]{0:T(1024)}, u32[]{:S(2)}) copy-start(s32[2048]{0:T(1024)} %param.14) | copy-start | bytes 24580
  0.7 1.0 %copy-start.6 = (s32[2048]{0:T(1024)S(1)}, s32[2048]{0:T(1024)}, u32[]{:S(2)}) copy-start(s32[2048]{0:T(1024)} %param.13) | copy-start | bytes 24580
  0.7 3.9 %copy-start = (bf16[288,128,128]{2,1,0:T(8,128)(2,1)S(1)}, bf16[288,128,128]{2,1,0:T(8,128)(2,1)}, u32[]{:S(2)}) copy-start(bf16[288,128,128]{2,1,0:T(8,128)(2,1)} %vals.7) | copy-start | bytes 28311556
  7.1 14.5 %collective-permute-start.5 = (f32[16,64,128]{2,1,0:T(8,128)S(1)}, f32[16,64,128]{2,1,0:T(8,128)S(1)}, u32[]{:S(2)}, u32[]{:S(2)}) collective-permute-start(f32[16,64,128]{2,1,0:T(8,128)S(1)} %shard_map.125.refs_0_.mine), channel_id=1, source_target_pairs={{0,1},{1,0},{2,3},{3,2},{4,5},{5,4},{6,7},{7,6},{8,9},{9,8},{10,11... | collective-permute-start | bytes 1572872 | tf_op jit(solution)/shard_map/ppermute | solution.py:307
  7.6 8.1 %collective-permute-start.3 = (s32[3,256]{1,0:T(4,128)S(1)}, s32[3,256]{1,0:T(4,128)S(1)}, u32[]{:S(2)}, u32[]{:S(2)}) collective-permute-start(s32[3,256]{1,0:T(4,128)S(1)} %shard_map.123.after.refs_0_.ids.refs_2_.refs_4_), channel_id=1, source_target_pairs={{0,2},{2,0},{1,3},{3,1},{4,6},{6,4},{5,7},{7,5},{8,10},{10,8},{9,1... | collective-permute-start | bytes 9224 | tf_op jit(solution)/shard_map/ppermute | solution.py:307
  10.2 5.5 %collective-permute-start.2 = (s32[3,256]{1,0:T(4,128)S(1)}, s32[3,256]{1,0:T(4,128)S(1)}, u32[]{:S(2)}, u32[]{:S(2)}) collective-permute-start(s32[3,256]{1,0:T(4,128)S(1)} %shard_map.123.after.refs_0_.ids.refs_2_.refs_4_), channel_id=1, source_target_pairs={{0,4},{4,8},{8,12},{12,0},{1,5},{5,9},{9,13},{13,1},{2,6},{6,10},{... | collective-permute-start | bytes 9224 | tf_op jit(solution)/shard_map/ppermute | solution.py:307
  11.5 4.7 %collective-permute-start.1 = (s32[3,256]{1,0:T(4,128)S(1)}, s32[3,256]{1,0:T(4,128)S(1)}, u32[]{:S(2)}, u32[]{:S(2)}) collective-permute-start(s32[3,256]{1,0:T(4,128)S(1)} %shard_map.123.after.refs_0_.ids.refs_2_.refs_4_), channel_id=1, source_target_pairs={{0,8},{4,12},{8,0},{12,4},{1,9},{5,13},{9,1},{13,5},{2,10},{6,14},... | collective-permute-start | bytes 9224 | tf_op jit(solution)/shard_map/ppermute | solution.py:307
  14.7 3.6 %collective-permute-start = (s32[3,256]{1,0:T(4,128)S(1)}, s32[3,256]{1,0:T(4,128)S(1)}, u32[]{:S(2)}, u32[]{:S(2)}) collective-permute-start(s32[3,256]{1,0:T(4,128)S(1)} %shard_map.123.after.refs_0_.ids.refs_2_.refs_4_), channel_id=1, source_target_pairs={{0,12},{4,0},{8,4},{12,8},{1,13},{5,1},{9,5},{13,9},{2,14},{6,2},{... | collective-permute-start | bytes 9224 | tf_op jit(solution)/shard_map/ppermute | solution.py:307
  21.5 7.7 %collective-permute-start.4 = (f32[16,64,128]{2,1,0:T(8,128)S(1)}, f32[16,64,128]{2,1,0:T(8,128)S(1)}, u32[]{:S(2)}, u32[]{:S(2)}) collective-permute-start(f32[16,64,128]{2,1,0:T(8,128)S(1)} %shard_map.126.mine), channel_id=1, source_target_pairs={{0,1},{1,0},{2,3},{3,2},{4,5},{5,4},{6,7},{7,6},{8,9},{9,8},{10,11... | collective-permute-start | bytes 1572872 | tf_op jit(solution)/shard_map/ppermute | solution.py:307
  22.8 8.9 %collective-permute-start.7 = (f32[64,256]{1,0:T(8,128)S(1)}, f32[64,256]{1,0:T(8,128)S(1)}, u32[]{:S(2)}, u32[]{:S(2)}) collective-permute-start(f32[64,256]{1,0:T(8,128)S(1)} %get-tuple-element.39), channel_id=1, source_target_pairs={{0,4},{4,8},{8,12},{12,0},{1,5},{5,9},{9,13},{13,1},{2,6},{6,10},{... | collective-permute-start | bytes 196616 | tf_op jit(solution)/shard_map/ppermute | solution.py:307
  22.9 11.4 %collective-permute-start.8 = (f32[64,256]{1,0:T(8,128)S(1)}, f32[64,256]{1,0:T(8,128)S(1)}, u32[]{:S(2)}, u32[]{:S(2)}) collective-permute-start(f32[64,256]{1,0:T(8,128)S(1)} %get-tuple-element.40), channel_id=1, source_target_pairs={{0,8},{4,12},{8,0},{12,4},{1,9},{5,13},{9,1},{13,5},{2,10},{6,14},... | collective-permute-start | bytes 196616 | tf_op jit(solution)/shard_map/ppermute | solution.py:307
  29.2 5.6 %collective-permute-start.9 = (f32[64,256]{1,0:T(8,128)S(1)}, f32[64,256]{1,0:T(8,128)S(1)}, u32[]{:S(2)}, u32[]{:S(2)}) collective-permute-start(f32[64,256]{1,0:T(8,128)S(1)} %get-tuple-element.41), channel_id=1, source_target_pairs={{0,12},{4,0},{8,4},{12,8},{1,13},{5,1},{9,5},{13,9},{2,14},{6,2},{... | collective-permute-start | bytes 196616 | tf_op jit(solution)/shard_map/ppermute | solution.py:307
  29.8 4.9 %collective-permute-start.6 = (f32[64,256]{1,0:T(8,128)S(1)}, f32[64,256]{1,0:T(8,128)S(1)}, u32[]{:S(2)}, u32[]{:S(2)}) collective-permute-start(f32[64,256]{1,0:T(8,128)S(1)} %get-tuple-element.37), channel_id=1, source_target_pairs={{0,2},{2,0},{1,3},{3,1},{4,6},{6,4},{5,7},{7,5},{8,10},{10,8},{9,1... | collective-permute-start | bytes 196616 | tf_op jit(solution)/shard_map/ppermute | solution.py:307
  34.9 4.3 %collective-permute-start.10 = (f32[64,256]{1,0:T(8,128)S(1)}, f32[64,256]{1,0:T(8,128)S(1)}, u32[]{:S(2)}, u32[]{:S(2)}) collective-permute-start(f32[64,256]{1,0:T(8,128)S(1)} %get-tuple-element.43.after.refs_0_), channel_id=1, source_target_pairs={{0,2},{2,0},{1,3},{3,1},{4,6},{6,4},{5,7},{7,5},{8,10},{10,8},{9,1... | collective-permute-start | bytes 196616 | tf_op jit(solution)/shard_map/ppermute | solution.py:307
  40.0 4.0 %collective-permute-start.11 = (f32[16,64,128]{2,1,0:T(8,128)S(1)}, f32[16,64,128]{2,1,0:T(8,128)S(1)}, u32[]{:S(2)}, u32[]{:S(2)}) collective-permute-start(f32[16,64,128]{2,1,0:T(8,128)S(1)} %shard_map.131.mine), channel_id=1, source_target_pairs={{0,1},{1,0},{2,3},{3,2},{4,5},{5,4},{6,7},{7,6},{8,9},{9,8},{10,11... | collective-permute-start | bytes 1572872 | tf_op jit(solution)/shard_map/ppermute | solution.py:307
  40.1 6.8 %collective-permute-start.14 = (f32[64,256]{1,0:T(8,128)S(1)}, f32[64,256]{1,0:T(8,128)S(1)}, u32[]{:S(2)}, u32[]{:S(2)}) collective-permute-start(f32[64,256]{1,0:T(8,128)S(1)} %get-tuple-element.46.refs_0_), channel_id=1, source_target_pairs={{0,4},{4,8},{8,12},{12,0},{1,5},{5,9},{9,13},{13,1},{2,6},{6,10},{... | collective-permute-start | bytes 196616 | tf_op jit(solution)/shard_map/ppermute | solution.py:307
  41.6 7.7 %collective-permute-start.13 = (f32[64,256]{1,0:T(8,128)S(1)}, f32[64,256]{1,0:T(8,128)S(1)}, u32[]{:S(2)}, u32[]{:S(2)}) collective-permute-start(f32[64,256]{1,0:T(8,128)S(1)} %get-tuple-element.46.refs_0_), channel_id=1, source_target_pairs={{0,8},{4,12},{8,0},{12,4},{1,9},{5,13},{9,1},{13,5},{2,10},{6,14},... | collective-permute-start | bytes 196616 | tf_op jit(solution)/shard_map/ppermute | solution.py:307
  42.9 6.4 %collective-permute-start.12 = (f32[64,256]{1,0:T(8,128)S(1)}, f32[64,256]{1,0:T(8,128)S(1)}, u32[]{:S(2)}, u32[]{:S(2)}) collective-permute-start(f32[64,256]{1,0:T(8,128)S(1)} %get-tuple-element.46.refs_0_), channel_id=1, source_target_pairs={{0,12},{4,0},{8,4},{12,8},{1,13},{5,1},{9,5},{13,9},{2,14},{6,2},{... | collective-permute-start | bytes 196616 | tf_op jit(solution)/shard_map/ppermute | solution.py:307
  50.8 6.8 %collective-permute-start.15 = (f32[16,64,128]{2,1,0:T(8,128)S(1)}, f32[16,64,128]{2,1,0:T(8,128)S(1)}, u32[]{:S(2)}, u32[]{:S(2)}) collective-permute-start(f32[16,64,128]{2,1,0:T(8,128)S(1)} %shard_map.133.after.mine), channel_id=1, source_target_pairs={{0,1},{1,0},{2,3},{3,2},{4,5},{5,4},{6,7},{7,6},{8,9},{9,8},{10,11... | collective-permute-start | bytes 1572872 | tf_op jit(solution)/shard_map/ppermute | solution.py:307
  50.9 2.3 %collective-permute-start.16 = (f32[16,32,128]{2,1,0:T(8,128)S(1)}, f32[16,32,128]{2,1,0:T(8,128)S(1)}, u32[]{:S(2)}, u32[]{:S(2)}) collective-permute-start(f32[16,32,128]{2,1,0:T(8,128)S(1)} %get-tuple-element.45.after), channel_id=1, source_target_pairs={{0,1},{1,0},{2,3},{3,2},{4,5},{5,4},{6,7},{7,6},{8,9},{9,8},{10,11... | collective-permute-start | bytes 786440 | tf_op jit(solution)/shard_map/ppermute | solution.py:307
  53.2 7.7 %collective-permute-start.17 = (f32[4,32,128]{2,1,0:T(8,128)S(1)}, f32[4,32,128]{2,1,0:T(8,128)S(1)}, u32[]{:S(2)}, u32[]{:S(2)}) collective-permute-start(f32[4,32,128]{2,1,0:T(8,128)S(1)} %get-tuple-element.50), channel_id=1, source_target_pairs={{0,4},{4,8},{8,12},{12,0},{1,5},{5,9},{9,13},{13,1},{2,6},{6,10},{... | collective-permute-start | bytes 196616 | tf_op jit(solution)/shard_map/ppermute | solution.py:307
  55.1 6.9 %collective-permute-start.18 = (f32[4,32,128]{2,1,0:T(8,128)S(1)}, f32[4,32,128]{2,1,0:T(8,128)S(1)}, u32[]{:S(2)}, u32[]{:S(2)}) collective-permute-start(f32[4,32,128]{2,1,0:T(8,128)S(1)} %get-tuple-element.51), channel_id=1, source_target_pairs={{0,8},{4,12},{8,0},{12,4},{1,9},{5,13},{9,1},{13,5},{2,10},{6,14},... | collective-permute-start | bytes 196616 | tf_op jit(solution)/shard_map/ppermute | solution.py:307
  56.3 5.8 %collective-permute-start.19 = (f32[4,32,128]{2,1,0:T(8,128)S(1)}, f32[4,32,128]{2,1,0:T(8,128)S(1)}, u32[]{:S(2)}, u32[]{:S(2)}) collective-permute-start(f32[4,32,128]{2,1,0:T(8,128)S(1)} %get-tuple-element.52), channel_id=1, source_target_pairs={{0,12},{4,0},{8,4},{12,8},{1,13},{5,1},{9,5},{13,9},{2,14},{6,2},{... | collective-permute-start | bytes 196616 | tf_op jit(solution)/shard_map/ppermute | solution.py:307
  62.2 1.6 %collective-permute-start.20 = (f32[16,32,128]{2,1,0:T(8,128)S(1)}, f32[16,32,128]{2,1,0:T(8,128)S(1)}, u32[]{:S(2)}, u32[]{:S(2)}) collective-permute-start(f32[16,32,128]{2,1,0:T(8,128)S(1)} %get-tuple-element.54), channel_id=1, source_target_pairs={{0,1},{1,0},{2,3},{3,2},{4,5},{5,4},{6,7},{7,6},{8,9},{9,8},{10,11... | collective-permute-start | bytes 786440 | tf_op jit(solution)/shard_map/ppermute | solution.py:307
  63.8 9.8 %collective-permute-start.21 = (f32[16,32,128]{2,1,0:T(8,128)S(1)}, f32[16,32,128]{2,1,0:T(8,128)S(1)}, u32[]{:S(2)}, u32[]{:S(2)}) collective-permute-start(f32[16,32,128]{2,1,0:T(8,128)S(1)} %shard_map.138.refs_0_), channel_id=1, source_target_pairs={{0,2},{2,0},{1,3},{3,1},{4,6},{6,4},{5,7},{7,5},{8,10},{10,8},{9,1... | collective-permute-start | bytes 786440 | tf_op jit(solution)/shard_map/ppermute | solution.py:307
  63.9 6.9 %collective-permute-start.25 = (f32[4,32,128]{2,1,0:T(8,128)S(1)}, f32[4,32,128]{2,1,0:T(8,128)S(1)}, u32[]{:S(2)}, u32[]{:S(2)}) collective-permute-start(f32[4,32,128]{2,1,0:T(8,128)S(1)} %shard_map.136.after.refs_0_), channel_id=1, source_target_pairs={{0,4},{4,8},{8,12},{12,0},{1,5},{5,9},{9,13},{13,1},{2,6},{6,10},{... | collective-permute-start | bytes 196616 | tf_op jit(solution)/shard_map/ppermute | solution.py:307
  65.8 7.2 %collective-permute-start.24 = (f32[4,32,128]{2,1,0:T(8,128)S(1)}, f32[4,32,128]{2,1,0:T(8,128)S(1)}, u32[]{:S(2)}, u32[]{:S(2)}) collective-permute-start(f32[4,32,128]{2,1,0:T(8,128)S(1)} %shard_map.136.after.refs_0_), channel_id=1, source_target_pairs={{0,8},{4,12},{8,0},{12,4},{1,9},{5,13},{9,1},{13,5},{2,10},{6,14},... | collective-permute-start | bytes 196616 | tf_op jit(solution)/shard_map/ppermute | solution.py:307
  68.2 5.2 %collective-permute-start.23 = (f32[4,32,128]{2,1,0:T(8,128)S(1)}, f32[4,32,128]{2,1,0:T(8,128)S(1)}, u32[]{:S(2)}, u32[]{:S(2)}) collective-permute-start(f32[4,32,128]{2,1,0:T(8,128)S(1)} %shard_map.136.after.refs_0_), channel_id=1, source_target_pairs={{0,12},{4,0},{8,4},{12,8},{1,13},{5,1},{9,5},{13,9},{2,14},{6,2},{... | collective-permute-start | bytes 196616 | tf_op jit(solution)/shard_map/ppermute | solution.py:307
  73.5 1.6 %collective-permute-start.26 = (f32[4,4,32,128]{3,2,1,0:T(8,128)S(1)}, f32[4,4,32,128]{3,2,1,0:T(8,128)S(1)}, u32[]{:S(2)}, u32[]{:S(2)}) collective-permute-start(f32[4,4,32,128]{3,2,1,0:T(8,128)S(1)} %shard_map.141.mine), channel_id=1, source_target_pairs={{0,1},{1,0},{2,3},{3,2},{4,5},{5,4},{6,7},{7,6},{8,9},{9,8},{10,11... | collective-permute-start | bytes 786440 | tf_op jit(solution)/shard_map/ppermute | solution.py:307
  73.6 2.3 %collective-permute-start.22 = (f32[16,32,128]{2,1,0:T(8,128)S(1)}, f32[16,32,128]{2,1,0:T(8,128)S(1)}, u32[]{:S(2)}, u32[]{:S(2)}) collective-permute-start(f32[16,32,128]{2,1,0:T(8,128)S(1)} %shard_map.139.mine), channel_id=1, source_target_pairs={{0,1},{1,0},{2,3},{3,2},{4,5},{5,4},{6,7},{7,6},{8,9},{9,8},{10,11... | collective-permute-start | bytes 786440 | tf_op jit(solution)/shard_map/ppermute | solution.py:307

commit v5 on v4

--- a/solution.py
+++ b/solution.py
@@ -11,6 +11,7 @@
 BF16 = jnp.bfloat16
 PACK = 4
 GROUP = 4
+ID_ROWS = 64
 
 VMEM = pl.BlockSpec(memory_space=pltpu.VMEM)
 SMEM = pl.BlockSpec(memory_space=pltpu.SMEM)
@@ -125,6 +126,7 @@
 
 
 def stack_ids(user, positive, negative, after, out):
+    out[...] = jnp.zeros_like(out)
     for row, ids in enumerate((user, positive, negative)):
         out[row:row + 1, :] = ids[...]
 
@@ -259,7 +261,7 @@
     me = lax.axis_index("user")
     per = outs[0].shape[0]
     for offset in range(peers):
-        there = lax.rem(me + offset, peers) * per
+        there = (me ^ offset) * per
         for block in range(per):
             outs[offset][block] = keep[there + block] + received[there + block]
 
@@ -275,6 +277,12 @@
 def pack(*refs):
     for place, ref in enumerate(refs[:-1]):
         refs[-1][place] = ref[...]
+
+
+def finish(peers, user_half_grad, user_mine, user_other, item_half_grad, item_mine, item_other,
+           user_out, item_out):
+    finish_users(user_half_grad, user_mine, user_other, user_out)
+    finish_items(peers, item_half_grad, item_mine, item_other, item_out)
 
 
 def finish_users(half_grad, mine, other, out):
@@ -295,7 +303,7 @@
     half = width // 2
     per = blocks // peers
     for offset in range(peers):
-        there = lax.rem(place + offset, peers) * per
+        there = (place ^ offset) * per
         for block in range(per):
             span = pl.ds(pl.multiple_of((there + block) * size, size), size)
             for rank, part in ((me, mine), (1 - me, other)):
@@ -303,8 +311,8 @@
                 out[rows, span] = half_grad[there + block, rows, :] + part[offset, block]
 
 
-def shift(values, axis, count, offset):
-    return lax.ppermute(values, axis, [(i, (i + offset) % count) for i in range(count)])
+def swap(values, axis="rep", peers=2, offset=1):
+    return lax.ppermute(values, axis, [(i, i ^ offset) for i in range(peers)])
 
 
 def on_device(users, items, user_emb, item_emb, user_deg, item_deg, block_vals, block_row,
@@ -315,7 +323,6 @@
     item_blocks = item_emb.shape[1] // size
     trips = trip_user.shape[0]
     half = width // 2
-    swap = functools.partial(shift, axis="rep", count=2, offset=1)
     user_deg = user_deg.reshape(user_blocks, size)
     item_deg = item_deg.reshape(item_blocks, size)
 
@@ -323,12 +330,12 @@
     product_bytes = slots * size * size * 2
     started = call(begin, shape(8, size), (), [], (), 16 * product_flops, product_bytes)
     ids = call(
-        stack_ids, jax.ShapeDtypeStruct((3, trips), jnp.int32),
+        stack_ids, jax.ShapeDtypeStruct((ID_ROWS, trips), jnp.int32),
         [each.reshape(1, trips) for each in (trip_user, trip_pos, trip_neg)] + [started],
         [VMEM, VMEM, VMEM, ANY],
     )
-    ids_user = [ids] + [shift(ids, "item", items, -o) for o in range(1, items)]
-    ids_item = [ids] + [shift(ids, "user", users, -o) for o in range(1, users)]
+    ids_user = [ids] + [swap(ids, "item", items, o) for o in range(1, items)]
+    ids_item = [ids] + [swap(ids, "user", users, o) for o in range(1, users)]
     lanes = -(-slots // size) * size
 
     order_shape = jax.ShapeDtypeStruct((8, lanes), jnp.int32)
@@ -366,7 +373,7 @@
             [pltpu.VMEM((3 * width, blocks * size), BF16)],
             peers * blocks * hot_flops, 8 * blocks * width * size,
         )
-        return [dealt[0]] + [shift(dealt[o], axis, peers, o) for o in range(1, peers)]
+        return [dealt[0]] + [swap(dealt[o], axis, peers, o) for o in range(1, peers)]
 
     item_parts = reduced([1, 2], item_table, item_scale, ids_item, "user", ids)
     user_parts = reduced([0], user_table, user_scale, ids_user, "item", item_parts[0])
@@ -386,7 +393,7 @@
 
     def added(rows, own, axis, peer_ids, blocks, after):
         peers = len(peer_ids)
-        arrays = [own] + [shift(own, axis, peers, -o) for o in range(1, peers)]
+        arrays = [own] + [swap(own, axis, peers, o) for o in range(1, peers)]
         return call(
             functools.partial(scatter, rows, peers), shape(blocks, width, size),
             (after, *arrays, *peer_ids), [ANY] + [VMEM] * (2 * peers),
@@ -427,17 +434,14 @@
     )
     item_half_grad, user_back = second(
         True, item_grad, user_order, item_scale, user_scale, dealt[0], False)
-    parts = [dealt[0]] + [shift(dealt[o], "user", users, o) for o in range(1, users)]
+    parts = [dealt[0]] + [swap(dealt[o], "user", users, o) for o in range(1, users)]
     item_own = call(sum_after, shape(per, half, size), (user_back, *parts),
                     [ANY] + [VMEM] * users,
                moved=4 * (users + 1) * per * half * size)
-    mine = call(pack, shape(users, per, half, size),
-                (item_own, *[shift(item_own, "user", users, -o) for o in range(1, users)]),
-                [VMEM] * users, moved=8 * item_blocks * half * size)
-    grad_item = call(
-        functools.partial(finish_items, users), shape(width, item_blocks * size),
-        (item_half_grad, mine, swap(mine)), [VMEM] * 3, moved=12 * item_blocks * width * size,
-    )
+    item_mine = call(pack, shape(users, per, half, size),
+                     (item_own, *[swap(item_own, "user", users, o) for o in range(1, users)]),
+                     [VMEM] * users, moved=8 * item_blocks * half * size)
+    item_other = swap(item_mine)
 
     user_keep, user_send = call(
         halves_after, [shape(user_blocks, half, size)] * 2, (user_back, item_own), [VMEM, ANY],
@@ -446,13 +450,14 @@
     own = call(sum_parts, shape(user_blocks, half, size), (user_keep, swap(user_send)),
                [VMEM, VMEM], moved=12 * user_blocks * half * size)
     mine = call(sum_parts, shape(user_blocks, half, size),
-                (own, *[shift(own, "item", items, o) for o in range(1, items)]),
+                (own, *[swap(own, "item", items, o) for o in range(1, items)]),
                 [VMEM] * items, moved=12 * user_blocks * half * size)
-    grad_user = call(
-        finish_users, shape(width, user_blocks * size), (user_half_grad, mine, swap(mine)),
-        [VMEM] * 3, moved=12 * user_blocks * width * size,
-    )
-    return (grad_user, grad_item)
+    return call(
+        functools.partial(finish, users),
+        (shape(width, user_blocks * size), shape(width, item_blocks * size)),
+        (user_half_grad, mine, swap(mine), item_half_grad, item_mine, item_other),
+        [VMEM] * 6, moved=12 * (user_blocks + item_blocks) * width * size,
+    )
 
 
 def solution(mesh):

time: 77.1 us -> 73.2 us (0.949)
  Pallas kernels: 19.1 us -> 15.3 us
  local copies, waits for them, and re-layouts: 2.16 us -> 0.65 us
  starting transfers between devices: 29.3 us -> 30.2 us
    pallas_call x21 -> x20, Pallas kernels: 19.1 us -> 15.3 us  [call(): pl.pallas_call(kernel, out_shape=outs, in_specs=specs, out_specs=jax.tree...]
    unnamed x20, local copies, waits for them, and re-layouts: 2.16 us -> 0.65 us
    ppermute x27, starting transfers between devices: 29.3 us -> 30.2 us  [swap(): return lax.ppermute(values, axis, [(i, i ^ offset) for i in range(peers)])]
where the time goes in v5:
time: 73.2 us; the launch traced here: 72.6 us
  starting transfers between devices  30.2 us (41%)
  waiting for transfers between devices  24.8 us (34%)
  Pallas kernels  15.3 us (21%)
  between operations  1.64 us (2%)
    ppermute x27, starting transfers between devices, swap(): return lax.ppermute(values, axis, [(i, i ^ offset) for i in range(peers)])  30.2 us
    ppermute x27, waiting for transfers between devices, swap(): return lax.ppermute(values, axis, [(i, i ^ offset) for i in range(peers)])  24.8 us
    pallas_call x20, Pallas kernels, call(): pl.pallas_call(kernel, out_shape=outs, in_specs=specs, out_specs=jax.tree...  15.3 us
  transfers between devices with their start and end apart: 27, of which 15 were waited for; matrix products, arithmetic and copies ran while one was open for 0% of the time, Pallas kernels for 16%

profile of v5, /device:TPU:0, one launch (start us, length us, event | category | flops | bytes accessed | tf_op | source)
XLA Modules:
  0.0 72.6 jit_solution(9695311154190402937)
XLA Ops:
  0.7 0.6 copy-done.3
  1.3 0.0 copy-done.2
  1.3 0.0 copy-done.1
  1.4 3.0 %collective-permute-start.3 = (s32[64,256]{1,0:T(8,128)S(1)}, s32[64,256]{1,0:T(8,128)S(1)}, u32[]{:S(2)}, u32[]{:S(2)}) collective-permute-start(s32[64,256]{1,0:T(8,128)S(1)} %shard_map.123.after.refs_0_.ids.refs_2_.refs_4_), channel_id=1, source_target_pairs={{0,2},{2,0},{1,3},{3,1},{4,6},{6,4},{5,7},{7,5},{8,10},{10,8},{9,1... | collective-permute-start | bytes 196616 | tf_op jit(solution)/shard_map/ppermute | solution.py:315
  4.3 3.6 %collective-permute-start.2 = (s32[64,256]{1,0:T(8,128)S(1)}, s32[64,256]{1,0:T(8,128)S(1)}, u32[]{:S(2)}, u32[]{:S(2)}) collective-permute-start(s32[64,256]{1,0:T(8,128)S(1)} %shard_map.123.after.refs_0_.ids.refs_2_.refs_4_), channel_id=1, source_target_pairs={{0,12},{4,8},{8,4},{12,0},{1,13},{5,9},{9,5},{13,1},{2,14},{6,10},... | collective-permute-start | bytes 196616 | tf_op jit(solution)/shard_map/ppermute | solution.py:315
  7.9 0.0 collective-permute-start.1
  8.0 0.8 %collective-permute-start = (s32[64,256]{1,0:T(8,128)S(1)}, s32[64,256]{1,0:T(8,128)S(1)}, u32[]{:S(2)}, u32[]{:S(2)}) collective-permute-start(s32[64,256]{1,0:T(8,128)S(1)} %shard_map.123.after.refs_0_.ids.refs_2_.refs_4_), channel_id=1, source_target_pairs={{0,4},{4,0},{8,12},{12,8},{1,5},{5,1},{9,13},{13,9},{2,6},{6,2},{1... | collective-permute-start | bytes 196616 | tf_op jit(solution)/shard_map/ppermute | solution.py:315
  9.4 0.9 %shard_map.124 = (bf16[17,64,128]{2,1,0:T(8,128)(2,1)S(1)}, bf16[17,64,128]{2,1,0:T(8,128)(2,1)S(1)}, f32[16,128]{1,0:T(8,128)S(1)}, f32[16,128]{1,0:T(8,128)S(1...) custom-call(s32[1]{0:T(128)S(6)} %copy.13.count, s32[288]{0:T(512)S(1)} %copy-done.8, s32[288]{0:T(512)S(1)} %copy-done.9, ...), custom_call_target="tpu_custom_call" | custom-call | flops 603979776 | bytes 9437184 | tf_op jit(solution)/shard_map/pallas_call | solution.py:23
  10.4 0.0 copy-done
  10.4 1.8 %shard_map.125.refs_0_.mine = f32[16,64,128]{2,1,0:T(8,128)S(1)} custom-call(s32[8,384]{1,0:T(8,128)S(1)} %get-tuple-element.29.order, bf16[288,128,128]{2,1,0:T(8,128)(2,1)S(1)} %copy-done, bf16[17,64,128]{2,1,0:T(8,128)(2,1)S(1)} %get-tuple-element.32.source, s32[64,256]{1,0:T(8,128)S(1)} %shard_map.123.after.refs_0_.ids.refs_2_.refs_4_), custom_call_target="tpu_custom_call" | custom-call | flops 603979776 | bytes 9437184 | tf_op jit(solution)/shard_map/pallas_call | solution.py:23
  12.2 0.1 collective-permute-start.5
  12.3 0.0 collective-permute-done.3.refs_4_.refs_1_.refs_3_
  12.3 0.0 collective-permute-done.2.refs_3_.refs_7_
  12.3 1.0 %collective-permute-done.1.refs_2_.refs_6_ = s32[64,256]{1,0:T(8,128)S(1)} collective-permute-done((s32[64,256]{1,0:T(8,128)S(1)}, s32[64,256]{1,0:T(8,128)S(1)}, u32[]{:S(2)}, u32[]{:S(2)}) %collective-permute-start.1) | collective-permute-done | bytes 65568 | tf_op jit(solution)/shard_map/ppermute | solution.py:315
  13.3 0.1 collective-permute-done.refs_1_.refs_5_
  13.4 2.2 %shard_map.126.mine = f32[16,64,128]{2,1,0:T(8,128)S(1)} custom-call(s32[8,384]{1,0:T(8,128)S(1)} %get-tuple-element.30.order, bf16[288,128,128]{2,1,0:T(8,128)(2,1)S(1)} %copy-done, bf16[17,64,128]{2,1,0:T(8,128)(2,1)S(1)} %get-tuple-element.31.source, f32[16,64,128]{2,1,0:T(8,128)S(1)} %shard_map.125.refs_0_.mine, ...), custom_call_target="tpu_custom_call" | custom-call | flops 603979776 | bytes 9437184 | tf_op jit(solution)/shard_map/pallas_call | solution.py:23
  15.6 0.5 collective-permute-start.4
  16.1 0.0 collective-permute-done.5.other
  16.1 1.2 %shard_map.127 = (f32[64,256]{1,0:T(8,128)S(1)}, f32[64,256]{1,0:T(8,128)S(1)}, f32[64,256]{1,0:T(8,128)S(1)}, f32[64,256]{1,0:T(8,128)S(1)}) custom-call(f32[16,64,128]{2,1,0:T(8,128)S(1)} %shard_map.125.refs_0_.mine, f32[16,64,128]{2,1,0:T(8,128)S(1)} %collective-permute-done.5.other, f32[16,128]{1,0:T(8,128)S(1)} %get-tuple-element.34.scale.target_scale.source_scale, ...), custom_call_target="tpu_custom_call" | custom-call | flops 805306368 | bytes 1048576 | tf_op jit(solution)/shard_map/pallas_call | solution.py:23
  17.4 1.1 %collective-permute-start.7 = (f32[64,256]{1,0:T(8,128)S(1)}, f32[64,256]{1,0:T(8,128)S(1)}, u32[]{:S(2)}, u32[]{:S(2)}) collective-permute-start(f32[64,256]{1,0:T(8,128)S(1)} %get-tuple-element.39), channel_id=1, source_target_pairs={{0,4},{4,0},{8,12},{12,8},{1,5},{5,1},{9,13},{13,9},{2,6},{6,2},{1... | collective-permute-start | bytes 196616 | tf_op jit(solution)/shard_map/ppermute | solution.py:315
  18.5 6.2 %collective-permute-start.8 = (f32[64,256]{1,0:T(8,128)S(1)}, f32[64,256]{1,0:T(8,128)S(1)}, u32[]{:S(2)}, u32[]{:S(2)}) collective-permute-start(f32[64,256]{1,0:T(8,128)S(1)} %get-tuple-element.40), channel_id=1, source_target_pairs={{0,8},{4,12},{8,0},{12,4},{1,9},{5,13},{9,1},{13,5},{2,10},{6,14},... | collective-permute-start | bytes 196616 | tf_op jit(solution)/shard_map/ppermute | solution.py:315
  24.7 0.0 collective-permute-start.9
  24.7 0.0 collective-permute-done.4.other
  24.7 0.6 shard_map.128
  25.3 0.1 collective-permute-start.6
  25.4 0.5 shard_map.129
  25.9 3.5 %collective-permute-done.8.refs_5_ = f32[64,256]{1,0:T(8,128)S(1)} collective-permute-done((f32[64,256]{1,0:T(8,128)S(1)}, f32[64,256]{1,0:T(8,128)S(1)}, u32[]{:S(2)}, u32[]{:S(2)}) %collective-permute-start.8) | collective-permute-done | bytes 65568 | tf_op jit(solution)/shard_map/ppermute | solution.py:315
  29.4 1.5 %collective-permute-done.9.refs_6_ = f32[64,256]{1,0:T(8,128)S(1)} collective-permute-done((f32[64,256]{1,0:T(8,128)S(1)}, f32[64,256]{1,0:T(8,128)S(1)}, u32[]{:S(2)}, u32[]{:S(2)}) %collective-permute-start.9) | collective-permute-done | bytes 65568 | tf_op jit(solution)/shard_map/ppermute | solution.py:315
  30.9 0.1 shard_map.130
  30.9 0.1 collective-permute-start.10
  31.0 4.3 %collective-permute-done.10.refs_1_ = f32[64,256]{1,0:T(8,128)S(1)} collective-permute-done((f32[64,256]{1,0:T(8,128)S(1)}, f32[64,256]{1,0:T(8,128)S(1)}, u32[]{:S(2)}, u32[]{:S(2)}) %collective-permute-start.10) | collective-permute-done | bytes 65568 | tf_op jit(solution)/shard_map/ppermute | solution.py:315
  35.3 0.8 %shard_map.131.mine = f32[16,64,128]{2,1,0:T(8,128)S(1)} custom-call(f32[64,256]{1,0:T(8,128)S(1)} %get-tuple-element.43.after.refs_0_, f32[64,256]{1,0:T(8,128)S(1)} %get-tuple-element.43.after.refs_0_, f32[64,256]{1,0:T(8,128)S(1)} %collective-permute-done.10.refs_1_, s32[64,256]{1,0:T(8,128)S(1)} %shard_map.123.after.refs_0_.ids.refs_2_.refs_4_, ...), custom_call_target="tpu_custom_call" | custom-call | flops 402653184 | bytes 524288 | tf_op jit(solution)/shard_map/pallas_call | solution.py:23
  36.1 0.1 collective-permute-start.11
  36.2 2.6 %collective-permute-start.14 = (f32[64,256]{1,0:T(8,128)S(1)}, f32[64,256]{1,0:T(8,128)S(1)}, u32[]{:S(2)}, u32[]{:S(2)}) collective-permute-start(f32[64,256]{1,0:T(8,128)S(1)} %get-tuple-element.46.refs_0_), channel_id=1, source_target_pairs={{0,12},{4,8},{8,4},{12,0},{1,13},{5,9},{9,5},{13,1},{2,14},{6,10},... | collective-permute-start | bytes 196616 | tf_op jit(solution)/shard_map/ppermute | solution.py:315
  38.8 0.0 collective-permute-start.13
  38.8 1.8 %collective-permute-start.12 = (f32[64,256]{1,0:T(8,128)S(1)}, f32[64,256]{1,0:T(8,128)S(1)}, u32[]{:S(2)}, u32[]{:S(2)}) collective-permute-start(f32[64,256]{1,0:T(8,128)S(1)} %get-tuple-element.46.refs_0_), channel_id=1, source_target_pairs={{0,4},{4,0},{8,12},{12,8},{1,5},{5,1},{9,13},{13,9},{2,6},{6,2},{1... | collective-permute-start | bytes 196616 | tf_op jit(solution)/shard_map/ppermute | solution.py:315
  40.7 1.9 %shard_map.132 = (f32[16,64,128]{2,1,0:T(8,128)S(1)}, f32[16,32,128]{2,1,0:T(8,128)S(1)}, f32[16,32,128]{2,1,0:T(8,128)S(1)}) custom-call(s32[8,384]{1,0:T(8,128)S(1)} %get-tuple-element.29.order, f32[16,64,128]{2,1,0:T(8,128)S(1)} %shard_map.131.mine, f32[16,64,128]{2,1,0:T(8,128)S(1)} %collective-permute-done.11.other, ...), custom_call_target="tpu_custom_call" | custom-call | flops 603979776 | bytes 9437184 | tf_op jit(solution)/shard_map/pallas_call | solution.py:23
  42.6 0.4 collective-permute-done.14.refs_3_
  43.0 2.3 %collective-permute-done.13.refs_2_ = f32[64,256]{1,0:T(8,128)S(1)} collective-permute-done((f32[64,256]{1,0:T(8,128)S(1)}, f32[64,256]{1,0:T(8,128)S(1)}, u32[]{:S(2)}, u32[]{:S(2)}) %collective-permute-start.13) | collective-permute-done | bytes 65568 | tf_op jit(solution)/shard_map/ppermute | solution.py:315
  45.3 0.0 collective-permute-done.12.refs_1_
  45.3 1.5 %shard_map.133.after.mine = f32[16,64,128]{2,1,0:T(8,128)S(1)} custom-call(f32[16,32,128]{2,1,0:T(8,128)S(1)} %get-tuple-element.45.after, f32[64,256]{1,0:T(8,128)S(1)} %get-tuple-element.46.refs_0_, f32[64,256]{1,0:T(8,128)S(1)} %collective-permute-done.12.refs_1_, f32[64,256]{1,0:T(8,128)S(1)} %collective-permute-done.13.refs_2_, ...), custom_call_target="tpu_custom_call" | custom-call | flops 805306368 | bytes 524288 | tf_op jit(solution)/shard_map/pallas_call | solution.py:23
  46.8 0.1 collective-permute-start.15
  46.9 0.5 collective-permute-start.16
  47.4 1.8 %collective-permute-done.16.received = f32[16,32,128]{2,1,0:T(8,128)S(1)} collective-permute-done((f32[16,32,128]{2,1,0:T(8,128)S(1)}, f32[16,32,128]{2,1,0:T(8,128)S(1)}, u32[]{:S(2)}, u32[]{:S(2)}) %collective-permute-start.16) | collective-permute-done | bytes 262176 | tf_op jit(solution)/shard_map/ppermute | solution.py:315
  49.2 0.9 %collective-permute-start.17 = (f32[4,32,128]{2,1,0:T(8,128)S(1)}, f32[4,32,128]{2,1,0:T(8,128)S(1)}, u32[]{:S(2)}, u32[]{:S(2)}) collective-permute-start(f32[4,32,128]{2,1,0:T(8,128)S(1)} %get-tuple-element.50), channel_id=1, source_target_pairs={{0,4},{4,0},{8,12},{12,8},{1,5},{5,1},{9,13},{13,9},{2,6},{6,2},{1... | collective-permute-start | bytes 196616 | tf_op jit(solution)/shard_map/ppermute | solution.py:315
  50.1 2.3 %collective-permute-start.18 = (f32[4,32,128]{2,1,0:T(8,128)S(1)}, f32[4,32,128]{2,1,0:T(8,128)S(1)}, u32[]{:S(2)}, u32[]{:S(2)}) collective-permute-start(f32[4,32,128]{2,1,0:T(8,128)S(1)} %get-tuple-element.51), channel_id=1, source_target_pairs={{0,8},{4,12},{8,0},{12,4},{1,9},{5,13},{9,1},{13,5},{2,10},{6,14},... | collective-permute-start | bytes 196616 | tf_op jit(solution)/shard_map/ppermute | solution.py:315
  52.4 1.2 %collective-permute-start.19 = (f32[4,32,128]{2,1,0:T(8,128)S(1)}, f32[4,32,128]{2,1,0:T(8,128)S(1)}, u32[]{:S(2)}, u32[]{:S(2)}) collective-permute-start(f32[4,32,128]{2,1,0:T(8,128)S(1)} %get-tuple-element.52), channel_id=1, source_target_pairs={{0,12},{4,8},{8,4},{12,0},{1,13},{5,9},{9,5},{13,1},{2,14},{6,10},... | collective-permute-start | bytes 196616 | tf_op jit(solution)/shard_map/ppermute | solution.py:315
  53.7 0.0 collective-permute-done.15.other
  53.7 2.4 %shard_map.135 = (f32[16,64,128]{2,1,0:T(8,128)S(1)}, f32[16,64,128]{2,1,0:T(8,128)S(1)}) custom-call(s32[8,384]{1,0:T(8,128)S(1)} %get-tuple-element.30.order, f32[16,64,128]{2,1,0:T(8,128)S(1)} %shard_map.133.after.mine, f32[16,64,128]{2,1,0:T(8,128)S(1)} %collective-permute-done.15.other, f32[16,128]{1,0:T(8,128)S(1)} %get-tuple-element.34.scale.target_scale.source_scale, ...), custom_call_target="tpu_custom_call" | custom-call | flops 603979776 | bytes 9437184 | tf_op jit(solution)/shard_map/pallas_call | solution.py:23
  56.1 1.7 %collective-permute-done.18.refs_2_ = f32[4,32,128]{2,1,0:T(8,128)S(1)} collective-permute-done((f32[4,32,128]{2,1,0:T(8,128)S(1)}, f32[4,32,128]{2,1,0:T(8,128)S(1)}, u32[]{:S(2)}, u32[]{:S(2)}) %collective-permute-start.18) | collective-permute-done | bytes 65568 | tf_op jit(solution)/shard_map/ppermute | solution.py:315
  57.7 0.9 %collective-permute-done.19.refs_3_ = f32[4,32,128]{2,1,0:T(8,128)S(1)} collective-permute-done((f32[4,32,128]{2,1,0:T(8,128)S(1)}, f32[4,32,128]{2,1,0:T(8,128)S(1)}, u32[]{:S(2)}, u32[]{:S(2)}) %collective-permute-start.19) | collective-permute-done | bytes 65568 | tf_op jit(solution)/shard_map/ppermute | solution.py:315
  58.7 0.1 collective-permute-start.20
  58.8 1.5 %collective-permute-done.20.refs_1_ = f32[16,32,128]{2,1,0:T(8,128)S(1)} collective-permute-done((f32[16,32,128]{2,1,0:T(8,128)S(1)}, f32[16,32,128]{2,1,0:T(8,128)S(1)}, u32[]{:S(2)}, u32[]{:S(2)}) %collective-permute-start.20) | collective-permute-done | bytes 262176 | tf_op jit(solution)/shard_map/ppermute | solution.py:315
  60.3 0.1 collective-permute-start.21
  60.4 2.5 %collective-permute-start.25 = (f32[4,32,128]{2,1,0:T(8,128)S(1)}, f32[4,32,128]{2,1,0:T(8,128)S(1)}, u32[]{:S(2)}, u32[]{:S(2)}) collective-permute-start(f32[4,32,128]{2,1,0:T(8,128)S(1)} %shard_map.136.after.refs_0_), channel_id=1, source_target_pairs={{0,12},{4,8},{8,4},{12,0},{1,13},{5,9},{9,5},{13,1},{2,14},{6,10},... | collective-permute-start | bytes 196616 | tf_op jit(solution)/shard_map/ppermute | solution.py:315
  62.9 0.1 collective-permute-start.24
  63.0 1.8 %collective-permute-start.23 = (f32[4,32,128]{2,1,0:T(8,128)S(1)}, f32[4,32,128]{2,1,0:T(8,128)S(1)}, u32[]{:S(2)}, u32[]{:S(2)}) collective-permute-start(f32[4,32,128]{2,1,0:T(8,128)S(1)} %shard_map.136.after.refs_0_), channel_id=1, source_target_pairs={{0,4},{4,0},{8,12},{12,8},{1,5},{5,1},{9,13},{13,9},{2,6},{6,2},{1... | collective-permute-start | bytes 196616 | tf_op jit(solution)/shard_map/ppermute | solution.py:315
  64.9 2.4 %collective-permute-done.25.refs_3_ = f32[4,32,128]{2,1,0:T(8,128)S(1)} collective-permute-done((f32[4,32,128]{2,1,0:T(8,128)S(1)}, f32[4,32,128]{2,1,0:T(8,128)S(1)}, u32[]{:S(2)}, u32[]{:S(2)}) %collective-permute-start.25) | collective-permute-done | bytes 65568 | tf_op jit(solution)/shard_map/ppermute | solution.py:315
  67.2 2.3 %collective-permute-done.24.refs_2_ = f32[4,32,128]{2,1,0:T(8,128)S(1)} collective-permute-done((f32[4,32,128]{2,1,0:T(8,128)S(1)}, f32[4,32,128]{2,1,0:T(8,128)S(1)}, u32[]{:S(2)}, u32[]{:S(2)}) %collective-permute-start.24) | collective-permute-done | bytes 65568 | tf_op jit(solution)/shard_map/ppermute | solution.py:315
  69.5 0.1 collective-permute-start.26
  69.6 0.5 collective-permute-start.22
  70.2 0.9 %collective-permute-done.26.item_other = f32[4,4,32,128]{3,2,1,0:T(8,128)S(1)} collective-permute-done((f32[4,4,32,128]{3,2,1,0:T(8,128)S(1)}, f32[4,4,32,128]{3,2,1,0:T(8,128)S(1)}, u32[]{:S(2)}, u32[]{:S(2)}) %collective-permute-start.26) | collective-permute-done | bytes 262176 | tf_op jit(solution)/shard_map/ppermute | solution.py:315
  71.1 0.4 collective-permute-done.22.user_other
  71.5 1.1 %shard_map.141 = (f32[64,2048]{1,0:T(8,128)}, f32[64,2048]{1,0:T(8,128)}) custom-call(f32[16,64,128]{2,1,0:T(8,128)S(1)} %get-tuple-element.44.user_half_grad, f32[16,32,128]{2,1,0:T(8,128)S(1)} %shard_map.139.user_mine, f32[16,32,128]{2,1,0:T(8,128)S(1)} %collective-permute-done.22.user_other, f32[16,64,128]{2,1,0:T(8,128)S(1)} %get-tuple-element.55.item_half_grad, ...), custom_call_target="tpu_custom_call" | custom-call | bytes 3145728 | tf_op jit(solution)/shard_map/pallas_call | solution.py:23
  (30 shorter events, 0.2 us)
Async XLA Ops:
  0.6 0.7 copy-start.3
  0.6 0.7 copy-start.2
  0.7 0.7 copy-start.1
  0.7 8.7 %copy-start.5 = (bf16[64,2048]{1,0:T(8,128)(2,1)S(1)}, bf16[64,2048]{1,0:T(8,128)(2,1)}, u32[]{:S(2)}) copy-start(bf16[64,2048]{1,0:T(8,128)(2,1)} %item_emb.3) | copy-start | bytes 786436
  0.7 8.7 %copy-start.4 = (bf16[64,2048]{1,0:T(8,128)(2,1)S(1)}, bf16[64,2048]{1,0:T(8,128)(2,1)}, u32[]{:S(2)}) copy-start(bf16[64,2048]{1,0:T(8,128)(2,1)} %user_emb.3) | copy-start | bytes 786436
  0.7 8.7 %copy-start.9 = (s32[288]{0:T(512)S(1)}, s32[288]{0:T(512)}, u32[]{:S(2)}) copy-start(s32[288]{0:T(512)} %columns.1) | copy-start | bytes 3460
  0.7 8.7 %copy-start.8 = (s32[288]{0:T(512)S(1)}, s32[288]{0:T(512)}, u32[]{:S(2)}) copy-start(s32[288]{0:T(512)} %rows.1) | copy-start | bytes 3460
  0.7 8.7 %copy-start.7 = (s32[2048]{0:T(1024)S(1)}, s32[2048]{0:T(1024)}, u32[]{:S(2)}) copy-start(s32[2048]{0:T(1024)} %param.14) | copy-start | bytes 24580
  0.7 8.7 %copy-start.6 = (s32[2048]{0:T(1024)S(1)}, s32[2048]{0:T(1024)}, u32[]{:S(2)}) copy-start(s32[2048]{0:T(1024)} %param.13) | copy-start | bytes 24580
  0.7 9.7 %copy-start = (bf16[288,128,128]{2,1,0:T(8,128)(2,1)S(1)}, bf16[288,128,128]{2,1,0:T(8,128)(2,1)}, u32[]{:S(2)}) copy-start(bf16[288,128,128]{2,1,0:T(8,128)(2,1)} %vals.7) | copy-start | bytes 28311556
  1.4 10.9 %collective-permute-start.3 = (s32[64,256]{1,0:T(8,128)S(1)}, s32[64,256]{1,0:T(8,128)S(1)}, u32[]{:S(2)}, u32[]{:S(2)}) collective-permute-start(s32[64,256]{1,0:T(8,128)S(1)} %shard_map.123.after.refs_0_.ids.refs_2_.refs_4_), channel_id=1, source_target_pairs={{0,2},{2,0},{1,3},{3,1},{4,6},{6,4},{5,7},{7,5},{8,10},{10,8},{9,1... | collective-permute-start | bytes 196616 | tf_op jit(solution)/shard_map/ppermute | solution.py:315
  4.3 8.0 %collective-permute-start.2 = (s32[64,256]{1,0:T(8,128)S(1)}, s32[64,256]{1,0:T(8,128)S(1)}, u32[]{:S(2)}, u32[]{:S(2)}) collective-permute-start(s32[64,256]{1,0:T(8,128)S(1)} %shard_map.123.after.refs_0_.ids.refs_2_.refs_4_), channel_id=1, source_target_pairs={{0,12},{4,8},{8,4},{12,0},{1,13},{5,9},{9,5},{13,1},{2,14},{6,10},... | collective-permute-start | bytes 196616 | tf_op jit(solution)/shard_map/ppermute | solution.py:315
  7.9 5.4 %collective-permute-start.1 = (s32[64,256]{1,0:T(8,128)S(1)}, s32[64,256]{1,0:T(8,128)S(1)}, u32[]{:S(2)}, u32[]{:S(2)}) collective-permute-start(s32[64,256]{1,0:T(8,128)S(1)} %shard_map.123.after.refs_0_.ids.refs_2_.refs_4_), channel_id=1, source_target_pairs={{0,8},{4,12},{8,0},{12,4},{1,9},{5,13},{9,1},{13,5},{2,10},{6,14},... | collective-permute-start | bytes 196616 | tf_op jit(solution)/shard_map/ppermute | solution.py:315
  8.0 5.4 %collective-permute-start = (s32[64,256]{1,0:T(8,128)S(1)}, s32[64,256]{1,0:T(8,128)S(1)}, u32[]{:S(2)}, u32[]{:S(2)}) collective-permute-start(s32[64,256]{1,0:T(8,128)S(1)} %shard_map.123.after.refs_0_.ids.refs_2_.refs_4_), channel_id=1, source_target_pairs={{0,4},{4,0},{8,12},{12,8},{1,5},{5,1},{9,13},{13,9},{2,6},{6,2},{1... | collective-permute-start | bytes 196616 | tf_op jit(solution)/shard_map/ppermute | solution.py:315
  12.2 3.9 %collective-permute-start.5 = (f32[16,64,128]{2,1,0:T(8,128)S(1)}, f32[16,64,128]{2,1,0:T(8,128)S(1)}, u32[]{:S(2)}, u32[]{:S(2)}) collective-permute-start(f32[16,64,128]{2,1,0:T(8,128)S(1)} %shard_map.125.refs_0_.mine), channel_id=1, source_target_pairs={{0,1},{1,0},{2,3},{3,2},{4,5},{5,4},{6,7},{7,6},{8,9},{9,8},{10,11... | collective-permute-start | bytes 1572872 | tf_op jit(solution)/shard_map/ppermute | solution.py:315
  15.6 9.1 %collective-permute-start.4 = (f32[16,64,128]{2,1,0:T(8,128)S(1)}, f32[16,64,128]{2,1,0:T(8,128)S(1)}, u32[]{:S(2)}, u32[]{:S(2)}) collective-permute-start(f32[16,64,128]{2,1,0:T(8,128)S(1)} %shard_map.126.mine), channel_id=1, source_target_pairs={{0,1},{1,0},{2,3},{3,2},{4,5},{5,4},{6,7},{7,6},{8,9},{9,8},{10,11... | collective-permute-start | bytes 1572872 | tf_op jit(solution)/shard_map/ppermute | solution.py:315
  17.4 8.5 %collective-permute-start.7 = (f32[64,256]{1,0:T(8,128)S(1)}, f32[64,256]{1,0:T(8,128)S(1)}, u32[]{:S(2)}, u32[]{:S(2)}) collective-permute-start(f32[64,256]{1,0:T(8,128)S(1)} %get-tuple-element.39), channel_id=1, source_target_pairs={{0,4},{4,0},{8,12},{12,8},{1,5},{5,1},{9,13},{13,9},{2,6},{6,2},{1... | collective-permute-start | bytes 196616 | tf_op jit(solution)/shard_map/ppermute | solution.py:315
  18.5 10.9 %collective-permute-start.8 = (f32[64,256]{1,0:T(8,128)S(1)}, f32[64,256]{1,0:T(8,128)S(1)}, u32[]{:S(2)}, u32[]{:S(2)}) collective-permute-start(f32[64,256]{1,0:T(8,128)S(1)} %get-tuple-element.40), channel_id=1, source_target_pairs={{0,8},{4,12},{8,0},{12,4},{1,9},{5,13},{9,1},{13,5},{2,10},{6,14},... | collective-permute-start | bytes 196616 | tf_op jit(solution)/shard_map/ppermute | solution.py:315
  24.7 6.2 %collective-permute-start.9 = (f32[64,256]{1,0:T(8,128)S(1)}, f32[64,256]{1,0:T(8,128)S(1)}, u32[]{:S(2)}, u32[]{:S(2)}) collective-permute-start(f32[64,256]{1,0:T(8,128)S(1)} %get-tuple-element.41), channel_id=1, source_target_pairs={{0,12},{4,8},{8,4},{12,0},{1,13},{5,9},{9,5},{13,1},{2,14},{6,10},... | collective-permute-start | bytes 196616 | tf_op jit(solution)/shard_map/ppermute | solution.py:315
  25.3 5.6 %collective-permute-start.6 = (f32[64,256]{1,0:T(8,128)S(1)}, f32[64,256]{1,0:T(8,128)S(1)}, u32[]{:S(2)}, u32[]{:S(2)}) collective-permute-start(f32[64,256]{1,0:T(8,128)S(1)} %get-tuple-element.37), channel_id=1, source_target_pairs={{0,2},{2,0},{1,3},{3,1},{4,6},{6,4},{5,7},{7,5},{8,10},{10,8},{9,1... | collective-permute-start | bytes 196616 | tf_op jit(solution)/shard_map/ppermute | solution.py:315
  30.9 4.3 %collective-permute-start.10 = (f32[64,256]{1,0:T(8,128)S(1)}, f32[64,256]{1,0:T(8,128)S(1)}, u32[]{:S(2)}, u32[]{:S(2)}) collective-permute-start(f32[64,256]{1,0:T(8,128)S(1)} %get-tuple-element.43.after.refs_0_), channel_id=1, source_target_pairs={{0,2},{2,0},{1,3},{3,1},{4,6},{6,4},{5,7},{7,5},{8,10},{10,8},{9,1... | collective-permute-start | bytes 196616 | tf_op jit(solution)/shard_map/ppermute | solution.py:315
  36.1 4.5 %collective-permute-start.11 = (f32[16,64,128]{2,1,0:T(8,128)S(1)}, f32[16,64,128]{2,1,0:T(8,128)S(1)}, u32[]{:S(2)}, u32[]{:S(2)}) collective-permute-start(f32[16,64,128]{2,1,0:T(8,128)S(1)} %shard_map.131.mine), channel_id=1, source_target_pairs={{0,1},{1,0},{2,3},{3,2},{4,5},{5,4},{6,7},{7,6},{8,9},{9,8},{10,11... | collective-permute-start | bytes 1572872 | tf_op jit(solution)/shard_map/ppermute | solution.py:315
  36.2 6.8 %collective-permute-start.14 = (f32[64,256]{1,0:T(8,128)S(1)}, f32[64,256]{1,0:T(8,128)S(1)}, u32[]{:S(2)}, u32[]{:S(2)}) collective-permute-start(f32[64,256]{1,0:T(8,128)S(1)} %get-tuple-element.46.refs_0_), channel_id=1, source_target_pairs={{0,12},{4,8},{8,4},{12,0},{1,13},{5,9},{9,5},{13,1},{2,14},{6,10},... | collective-permute-start | bytes 196616 | tf_op jit(solution)/shard_map/ppermute | solution.py:315
  38.8 6.5 %collective-permute-start.13 = (f32[64,256]{1,0:T(8,128)S(1)}, f32[64,256]{1,0:T(8,128)S(1)}, u32[]{:S(2)}, u32[]{:S(2)}) collective-permute-start(f32[64,256]{1,0:T(8,128)S(1)} %get-tuple-element.46.refs_0_), channel_id=1, source_target_pairs={{0,8},{4,12},{8,0},{12,4},{1,9},{5,13},{9,1},{13,5},{2,10},{6,14},... | collective-permute-start | bytes 196616 | tf_op jit(solution)/shard_map/ppermute | solution.py:315
  38.8 6.5 %collective-permute-start.12 = (f32[64,256]{1,0:T(8,128)S(1)}, f32[64,256]{1,0:T(8,128)S(1)}, u32[]{:S(2)}, u32[]{:S(2)}) collective-permute-start(f32[64,256]{1,0:T(8,128)S(1)} %get-tuple-element.46.refs_0_), channel_id=1, source_target_pairs={{0,4},{4,0},{8,12},{12,8},{1,5},{5,1},{9,13},{13,9},{2,6},{6,2},{1... | collective-permute-start | bytes 196616 | tf_op jit(solution)/shard_map/ppermute | solution.py:315
  46.8 6.8 %collective-permute-start.15 = (f32[16,64,128]{2,1,0:T(8,128)S(1)}, f32[16,64,128]{2,1,0:T(8,128)S(1)}, u32[]{:S(2)}, u32[]{:S(2)}) collective-permute-start(f32[16,64,128]{2,1,0:T(8,128)S(1)} %shard_map.133.after.mine), channel_id=1, source_target_pairs={{0,1},{1,0},{2,3},{3,2},{4,5},{5,4},{6,7},{7,6},{8,9},{9,8},{10,11... | collective-permute-start | bytes 1572872 | tf_op jit(solution)/shard_map/ppermute | solution.py:315
  46.9 2.2 %collective-permute-start.16 = (f32[16,32,128]{2,1,0:T(8,128)S(1)}, f32[16,32,128]{2,1,0:T(8,128)S(1)}, u32[]{:S(2)}, u32[]{:S(2)}) collective-permute-start(f32[16,32,128]{2,1,0:T(8,128)S(1)} %get-tuple-element.45.after), channel_id=1, source_target_pairs={{0,1},{1,0},{2,3},{3,2},{4,5},{5,4},{6,7},{7,6},{8,9},{9,8},{10,11... | collective-permute-start | bytes 786440 | tf_op jit(solution)/shard_map/ppermute | solution.py:315
  49.2 6.8 %collective-permute-start.17 = (f32[4,32,128]{2,1,0:T(8,128)S(1)}, f32[4,32,128]{2,1,0:T(8,128)S(1)}, u32[]{:S(2)}, u32[]{:S(2)}) collective-permute-start(f32[4,32,128]{2,1,0:T(8,128)S(1)} %get-tuple-element.50), channel_id=1, source_target_pairs={{0,4},{4,0},{8,12},{12,8},{1,5},{5,1},{9,13},{13,9},{2,6},{6,2},{1... | collective-permute-start | bytes 196616 | tf_op jit(solution)/shard_map/ppermute | solution.py:315
  50.1 7.6 %collective-permute-start.18 = (f32[4,32,128]{2,1,0:T(8,128)S(1)}, f32[4,32,128]{2,1,0:T(8,128)S(1)}, u32[]{:S(2)}, u32[]{:S(2)}) collective-permute-start(f32[4,32,128]{2,1,0:T(8,128)S(1)} %get-tuple-element.51), channel_id=1, source_target_pairs={{0,8},{4,12},{8,0},{12,4},{1,9},{5,13},{9,1},{13,5},{2,10},{6,14},... | collective-permute-start | bytes 196616 | tf_op jit(solution)/shard_map/ppermute | solution.py:315
  52.4 6.2 %collective-permute-start.19 = (f32[4,32,128]{2,1,0:T(8,128)S(1)}, f32[4,32,128]{2,1,0:T(8,128)S(1)}, u32[]{:S(2)}, u32[]{:S(2)}) collective-permute-start(f32[4,32,128]{2,1,0:T(8,128)S(1)} %get-tuple-element.52), channel_id=1, source_target_pairs={{0,12},{4,8},{8,4},{12,0},{1,13},{5,9},{9,5},{13,1},{2,14},{6,10},... | collective-permute-start | bytes 196616 | tf_op jit(solution)/shard_map/ppermute | solution.py:315
  58.7 1.6 %collective-permute-start.20 = (f32[16,32,128]{2,1,0:T(8,128)S(1)}, f32[16,32,128]{2,1,0:T(8,128)S(1)}, u32[]{:S(2)}, u32[]{:S(2)}) collective-permute-start(f32[16,32,128]{2,1,0:T(8,128)S(1)} %get-tuple-element.54), channel_id=1, source_target_pairs={{0,1},{1,0},{2,3},{3,2},{4,5},{5,4},{6,7},{7,6},{8,9},{9,8},{10,11... | collective-permute-start | bytes 786440 | tf_op jit(solution)/shard_map/ppermute | solution.py:315
  60.3 9.3 %collective-permute-start.21 = (f32[16,32,128]{2,1,0:T(8,128)S(1)}, f32[16,32,128]{2,1,0:T(8,128)S(1)}, u32[]{:S(2)}, u32[]{:S(2)}) collective-permute-start(f32[16,32,128]{2,1,0:T(8,128)S(1)} %shard_map.138.refs_0_), channel_id=1, source_target_pairs={{0,2},{2,0},{1,3},{3,1},{4,6},{6,4},{5,7},{7,5},{8,10},{10,8},{9,1... | collective-permute-start | bytes 786440 | tf_op jit(solution)/shard_map/ppermute | solution.py:315
  60.4 6.8 %collective-permute-start.25 = (f32[4,32,128]{2,1,0:T(8,128)S(1)}, f32[4,32,128]{2,1,0:T(8,128)S(1)}, u32[]{:S(2)}, u32[]{:S(2)}) collective-permute-start(f32[4,32,128]{2,1,0:T(8,128)S(1)} %shard_map.136.after.refs_0_), channel_id=1, source_target_pairs={{0,12},{4,8},{8,4},{12,0},{1,13},{5,9},{9,5},{13,1},{2,14},{6,10},... | collective-permute-start | bytes 196616 | tf_op jit(solution)/shard_map/ppermute | solution.py:315
  62.9 6.6 %collective-permute-start.24 = (f32[4,32,128]{2,1,0:T(8,128)S(1)}, f32[4,32,128]{2,1,0:T(8,128)S(1)}, u32[]{:S(2)}, u32[]{:S(2)}) collective-permute-start(f32[4,32,128]{2,1,0:T(8,128)S(1)} %shard_map.136.after.refs_0_), channel_id=1, source_target_pairs={{0,8},{4,12},{8,0},{12,4},{1,9},{5,13},{9,1},{13,5},{2,10},{6,14},... | collective-permute-start | bytes 196616 | tf_op jit(solution)/shard_map/ppermute | solution.py:315
  63.0 6.5 %collective-permute-start.23 = (f32[4,32,128]{2,1,0:T(8,128)S(1)}, f32[4,32,128]{2,1,0:T(8,128)S(1)}, u32[]{:S(2)}, u32[]{:S(2)}) collective-permute-start(f32[4,32,128]{2,1,0:T(8,128)S(1)} %shard_map.136.after.refs_0_), channel_id=1, source_target_pairs={{0,4},{4,0},{8,12},{12,8},{1,5},{5,1},{9,13},{13,9},{2,6},{6,2},{1... | collective-permute-start | bytes 196616 | tf_op jit(solution)/shard_map/ppermute | solution.py:315
  69.5 1.6 %collective-permute-start.26 = (f32[4,4,32,128]{3,2,1,0:T(8,128)S(1)}, f32[4,4,32,128]{3,2,1,0:T(8,128)S(1)}, u32[]{:S(2)}, u32[]{:S(2)}) collective-permute-start(f32[4,4,32,128]{3,2,1,0:T(8,128)S(1)} %shard_map.140.item_mine), channel_id=1, source_target_pairs={{0,1},{1,0},{2,3},{3,2},{4,5},{5,4},{6,7},{7,6},{8,9},{9,8},{10,11... | collective-permute-start | bytes 786440 | tf_op jit(solution)/shard_map/ppermute | solution.py:315
  69.6 1.8 %collective-permute-start.22 = (f32[16,32,128]{2,1,0:T(8,128)S(1)}, f32[16,32,128]{2,1,0:T(8,128)S(1)}, u32[]{:S(2)}, u32[]{:S(2)}) collective-permute-start(f32[16,32,128]{2,1,0:T(8,128)S(1)} %shard_map.139.user_mine), channel_id=1, source_target_pairs={{0,1},{1,0},{2,3},{3,2},{4,5},{5,4},{6,7},{7,6},{8,9},{9,8},{10,11... | collective-permute-start | bytes 786440 | tf_op jit(solution)/shard_map/ppermute | solution.py:315

commit v6 on v5

--- a/solution.py
+++ b/solution.py
@@ -12,6 +12,8 @@
 PACK = 4
 GROUP = 4
 ID_ROWS = 64
+LIGHT = 0
+HEAVY = 10 ** 11
 
 VMEM = pl.BlockSpec(memory_space=pltpu.VMEM)
 SMEM = pl.BlockSpec(memory_space=pltpu.SMEM)
@@ -184,7 +186,7 @@
         outs[peer][...] = fold(pick(table, ids[peer], rows, 2 * size), width)
 
 
-def scatter(rows, peers, after, *refs):
+def scatter(rows, peers, *refs):
     pieces, ids, out, table = refs[:peers], refs[peers:2 * peers], refs[2 * peers], refs[-1]
     blocks, width, size = out.shape
     tile = 2 * size
@@ -391,14 +393,13 @@
         moved=4 * width * trips * (len(user_parts) + len(item_parts) + 2),
     )
 
-    def added(rows, own, axis, peer_ids, blocks, after):
+    def added(rows, own, axis, peer_ids, blocks, weight):
         peers = len(peer_ids)
         arrays = [own] + [swap(own, axis, peers, o) for o in range(1, peers)]
         return call(
             functools.partial(scatter, rows, peers), shape(blocks, width, size),
-            (after, *arrays, *peer_ids), [ANY] + [VMEM] * (2 * peers),
-            [pltpu.VMEM((peers, 3 * width, trips), BF16)],
-            peers * blocks * hot_flops, 4 * blocks * width * size,
+            (*arrays, *peer_ids), [VMEM] * (2 * peers),
+            [pltpu.VMEM((peers, 3 * width, trips), BF16)], weight, 0,
         )
 
     def second(across, grad, order, source_scale, target_scale, after, divided):
@@ -414,22 +415,15 @@
             product_flops, product_bytes,
         )
 
-    user_grad = added([0], pieces, "item", ids_user, user_blocks, pieces)
-    user_grad = added([0], pieces, "item", ids_user, user_blocks, pieces)
-    def divided(total, after):
-        blocks = total.shape[0]
-        return call(halves, [shape(blocks, half, size)] * 2, (total, after), [VMEM, ANY],
-                    moved=8 * blocks * width * size)
-
-    user_grad = added([0], pieces, "item", ids_user, user_blocks, pieces)
+    user_grad = added([0], pieces, "item", ids_user, user_blocks, LIGHT)
+    item_grad = added([1, 2], pushed, "user", ids_item, item_blocks, HEAVY)
     user_half_grad, item_keep, item_send = second(
-        False, user_grad, item_order, user_scale, item_scale, pieces, True)
-    item_grad = added([1, 2], pushed, "user", ids_item, item_blocks, item_send)
+        False, user_grad, item_order, user_scale, item_scale, item_grad, True)
 
     per = item_blocks // users
     dealt = call(
         functools.partial(add_deal, users), [shape(per, half, size)] * users,
-        (item_keep, swap(item_send), item_grad), [VMEM, VMEM, ANY],
+        (item_keep, swap(item_send), pieces), [VMEM, VMEM, ANY],
         moved=12 * item_blocks * half * size,
     )
     item_half_grad, user_back = second(

time: 73.2 us -> 70.7 us (0.966)
  waiting for transfers between devices: 24.8 us -> 15.5 us
  starting transfers between devices: 30.2 us -> 37.3 us
    ppermute x27, waiting for transfers between devices: 24.8 us -> 15.5 us  [swap(): return lax.ppermute(values, axis, [(i, i ^ offset) for i in range(peers)])]
    ppermute x27, starting transfers between devices: 30.2 us -> 37.3 us  [swap(): return lax.ppermute(values, axis, [(i, i ^ offset) for i in range(peers)])]
  transfers between devices with their start and end apart: 27 -> 27, of which waited for: 15 -> 14; matrix products, arithmetic and copies ran while one was open for 0% -> 0% of each run, Pallas kernels for 16% -> 20%
where the time goes in v6:
time: 70.7 us; the launch traced here: 70.4 us
  starting transfers between devices  37.3 us (53%)
  waiting for transfers between devices  15.5 us (22%)
  Pallas kernels  15.3 us (22%)
  between operations  1.65 us (2%)
    ppermute x27, starting transfers between devices, swap(): return lax.ppermute(values, axis, [(i, i ^ offset) for i in range(peers)])  37.3 us
    ppermute x27, waiting for transfers between devices, swap(): return lax.ppermute(values, axis, [(i, i ^ offset) for i in range(peers)])  15.5 us
    pallas_call x20, Pallas kernels, call(): pl.pallas_call(kernel, out_shape=outs, in_specs=specs, out_specs=jax.tree...  15.3 us
  transfers between devices with their start and end apart: 27, of which 14 were waited for; matrix products, arithmetic and copies ran while one was open for 0% of the time, Pallas kernels for 20%

profile of v6, /device:TPU:0, one launch (start us, length us, event | category | flops | bytes accessed | tf_op | source)
XLA Modules:
  0.0 70.4 jit_solution(6597777021696329215)
XLA Ops:
  0.7 0.6 copy-done.3
  1.3 0.0 copy-done.2
  1.3 0.0 copy-done.1
  1.4 3.0 %collective-permute-start.3 = (s32[64,256]{1,0:T(8,128)S(1)}, s32[64,256]{1,0:T(8,128)S(1)}, u32[]{:S(2)}, u32[]{:S(2)}) collective-permute-start(s32[64,256]{1,0:T(8,128)S(1)} %shard_map.123.after.refs_0_.ids.refs_2_.refs_4_), channel_id=1, source_target_pairs={{0,2},{2,0},{1,3},{3,1},{4,6},{6,4},{5,7},{7,5},{8,10},{10,8},{9,1... | collective-permute-start | bytes 196616 | tf_op jit(solution)/shard_map/ppermute | solution.py:317
  4.3 3.6 %collective-permute-start.2 = (s32[64,256]{1,0:T(8,128)S(1)}, s32[64,256]{1,0:T(8,128)S(1)}, u32[]{:S(2)}, u32[]{:S(2)}) collective-permute-start(s32[64,256]{1,0:T(8,128)S(1)} %shard_map.123.after.refs_0_.ids.refs_2_.refs_4_), channel_id=1, source_target_pairs={{0,12},{4,8},{8,4},{12,0},{1,13},{5,9},{9,5},{13,1},{2,14},{6,10},... | collective-permute-start | bytes 196616 | tf_op jit(solution)/shard_map/ppermute | solution.py:317
  7.9 0.0 collective-permute-start.1
  8.0 0.8 %collective-permute-start = (s32[64,256]{1,0:T(8,128)S(1)}, s32[64,256]{1,0:T(8,128)S(1)}, u32[]{:S(2)}, u32[]{:S(2)}) collective-permute-start(s32[64,256]{1,0:T(8,128)S(1)} %shard_map.123.after.refs_0_.ids.refs_2_.refs_4_), channel_id=1, source_target_pairs={{0,4},{4,0},{8,12},{12,8},{1,5},{5,1},{9,13},{13,9},{2,6},{6,2},{1... | collective-permute-start | bytes 196616 | tf_op jit(solution)/shard_map/ppermute | solution.py:317
  9.4 0.9 %shard_map.124 = (bf16[17,64,128]{2,1,0:T(8,128)(2,1)S(1)}, bf16[17,64,128]{2,1,0:T(8,128)(2,1)S(1)}, f32[16,128]{1,0:T(8,128)S(1)}, f32[16,128]{1,0:T(8,128)S(1...) custom-call(s32[1]{0:T(128)S(6)} %copy.13.count, s32[288]{0:T(512)S(1)} %copy-done.8, s32[288]{0:T(512)S(1)} %copy-done.9, ...), custom_call_target="tpu_custom_call" | custom-call | flops 603979776 | bytes 9437184 | tf_op jit(solution)/shard_map/pallas_call | solution.py:25
  10.4 0.0 copy-done
  10.4 1.8 %shard_map.125.refs_0_.mine = f32[16,64,128]{2,1,0:T(8,128)S(1)} custom-call(s32[8,384]{1,0:T(8,128)S(1)} %get-tuple-element.29.order, bf16[288,128,128]{2,1,0:T(8,128)(2,1)S(1)} %copy-done, bf16[17,64,128]{2,1,0:T(8,128)(2,1)S(1)} %get-tuple-element.32.source, s32[64,256]{1,0:T(8,128)S(1)} %shard_map.123.after.refs_0_.ids.refs_2_.refs_4_), custom_call_target="tpu_custom_call" | custom-call | flops 603979776 | bytes 9437184 | tf_op jit(solution)/shard_map/pallas_call | solution.py:25
  12.2 0.1 collective-permute-start.5
  12.3 0.0 collective-permute-done.2.refs_3_.refs_7_
  12.3 1.0 %collective-permute-done.1.refs_2_.refs_6_ = s32[64,256]{1,0:T(8,128)S(1)} collective-permute-done((s32[64,256]{1,0:T(8,128)S(1)}, s32[64,256]{1,0:T(8,128)S(1)}, u32[]{:S(2)}, u32[]{:S(2)}) %collective-permute-start.1) | collective-permute-done | bytes 65568 | tf_op jit(solution)/shard_map/ppermute | solution.py:317
  13.3 0.1 collective-permute-done.refs_1_.refs_5_
  13.4 2.2 %shard_map.126.mine = f32[16,64,128]{2,1,0:T(8,128)S(1)} custom-call(s32[8,384]{1,0:T(8,128)S(1)} %get-tuple-element.30.order, bf16[288,128,128]{2,1,0:T(8,128)(2,1)S(1)} %copy-done, bf16[17,64,128]{2,1,0:T(8,128)(2,1)S(1)} %get-tuple-element.31.source, f32[16,64,128]{2,1,0:T(8,128)S(1)} %shard_map.125.refs_0_.mine, ...), custom_call_target="tpu_custom_call" | custom-call | flops 603979776 | bytes 9437184 | tf_op jit(solution)/shard_map/pallas_call | solution.py:25
  15.6 0.1 collective-permute-start.4
  15.7 0.0 collective-permute-done.5.other
  15.7 1.2 %shard_map.127 = (f32[64,256]{1,0:T(8,128)S(1)}, f32[64,256]{1,0:T(8,128)S(1)}, f32[64,256]{1,0:T(8,128)S(1)}, f32[64,256]{1,0:T(8,128)S(1)}) custom-call(f32[16,64,128]{2,1,0:T(8,128)S(1)} %shard_map.125.refs_0_.mine, f32[16,64,128]{2,1,0:T(8,128)S(1)} %collective-permute-done.5.other, f32[16,128]{1,0:T(8,128)S(1)} %get-tuple-element.34.scale.target_scale.source_scale, ...), custom_call_target="tpu_custom_call" | custom-call | flops 805306368 | bytes 1048576 | tf_op jit(solution)/shard_map/pallas_call | solution.py:25
  17.0 2.4 %collective-permute-start.7 = (f32[64,256]{1,0:T(8,128)S(1)}, f32[64,256]{1,0:T(8,128)S(1)}, u32[]{:S(2)}, u32[]{:S(2)}) collective-permute-start(f32[64,256]{1,0:T(8,128)S(1)} %get-tuple-element.39), channel_id=1, source_target_pairs={{0,4},{4,0},{8,12},{12,8},{1,5},{5,1},{9,13},{13,9},{2,6},{6,2},{1... | collective-permute-start | bytes 196616 | tf_op jit(solution)/shard_map/ppermute | solution.py:317
  19.4 1.7 %collective-permute-start.8 = (f32[64,256]{1,0:T(8,128)S(1)}, f32[64,256]{1,0:T(8,128)S(1)}, u32[]{:S(2)}, u32[]{:S(2)}) collective-permute-start(f32[64,256]{1,0:T(8,128)S(1)} %get-tuple-element.40), channel_id=1, source_target_pairs={{0,8},{4,12},{8,0},{12,4},{1,9},{5,13},{9,1},{13,5},{2,10},{6,14},... | collective-permute-start | bytes 196616 | tf_op jit(solution)/shard_map/ppermute | solution.py:317
  21.1 0.7 %collective-permute-start.9 = (f32[64,256]{1,0:T(8,128)S(1)}, f32[64,256]{1,0:T(8,128)S(1)}, u32[]{:S(2)}, u32[]{:S(2)}) collective-permute-start(f32[64,256]{1,0:T(8,128)S(1)} %get-tuple-element.41), channel_id=1, source_target_pairs={{0,12},{4,8},{8,4},{12,0},{1,13},{5,9},{9,5},{13,1},{2,14},{6,10},... | collective-permute-start | bytes 196616 | tf_op jit(solution)/shard_map/ppermute | solution.py:317
  21.8 0.6 shard_map.128
  22.4 4.8 %collective-permute-start.6 = (f32[64,256]{1,0:T(8,128)S(1)}, f32[64,256]{1,0:T(8,128)S(1)}, u32[]{:S(2)}, u32[]{:S(2)}) collective-permute-start(f32[64,256]{1,0:T(8,128)S(1)} %get-tuple-element.37), channel_id=1, source_target_pairs={{0,2},{2,0},{1,3},{3,1},{4,6},{6,4},{5,7},{7,5},{8,10},{10,8},{9,1... | collective-permute-start | bytes 196616 | tf_op jit(solution)/shard_map/ppermute | solution.py:317
  27.2 0.5 shard_map.129
  27.7 0.0 collective-permute-done.7.refs_4_
  27.7 0.1 collective-permute-done.8.refs_5_
  27.8 1.7 %collective-permute-done.6.refs_1_ = f32[64,256]{1,0:T(8,128)S(1)} collective-permute-done((f32[64,256]{1,0:T(8,128)S(1)}, f32[64,256]{1,0:T(8,128)S(1)}, u32[]{:S(2)}, u32[]{:S(2)}) %collective-permute-start.6) | collective-permute-done | bytes 65568 | tf_op jit(solution)/shard_map/ppermute | solution.py:317
  29.5 0.1 shard_map.130
  29.5 2.1 %collective-permute-start.10 = (f32[64,256]{1,0:T(8,128)S(1)}, f32[64,256]{1,0:T(8,128)S(1)}, u32[]{:S(2)}, u32[]{:S(2)}) collective-permute-start(f32[64,256]{1,0:T(8,128)S(1)} %get-tuple-element.43.refs_0_.after), channel_id=1, source_target_pairs={{0,2},{2,0},{1,3},{3,1},{4,6},{6,4},{5,7},{7,5},{8,10},{10,8},{9,1... | collective-permute-start | bytes 196616 | tf_op jit(solution)/shard_map/ppermute | solution.py:317
  31.6 1.2 %collective-permute-start.14 = (f32[64,256]{1,0:T(8,128)S(1)}, f32[64,256]{1,0:T(8,128)S(1)}, u32[]{:S(2)}, u32[]{:S(2)}) collective-permute-start(f32[64,256]{1,0:T(8,128)S(1)} %get-tuple-element.44.refs_0_), channel_id=1, source_target_pairs={{0,12},{4,8},{8,4},{12,0},{1,13},{5,9},{9,5},{13,1},{2,14},{6,10},... | collective-permute-start | bytes 196616 | tf_op jit(solution)/shard_map/ppermute | solution.py:317
  32.8 1.2 %collective-permute-start.13 = (f32[64,256]{1,0:T(8,128)S(1)}, f32[64,256]{1,0:T(8,128)S(1)}, u32[]{:S(2)}, u32[]{:S(2)}) collective-permute-start(f32[64,256]{1,0:T(8,128)S(1)} %get-tuple-element.44.refs_0_), channel_id=1, source_target_pairs={{0,8},{4,12},{8,0},{12,4},{1,9},{5,13},{9,1},{13,5},{2,10},{6,14},... | collective-permute-start | bytes 196616 | tf_op jit(solution)/shard_map/ppermute | solution.py:317
  34.0 2.0 %collective-permute-start.12 = (f32[64,256]{1,0:T(8,128)S(1)}, f32[64,256]{1,0:T(8,128)S(1)}, u32[]{:S(2)}, u32[]{:S(2)}) collective-permute-start(f32[64,256]{1,0:T(8,128)S(1)} %get-tuple-element.44.refs_0_), channel_id=1, source_target_pairs={{0,4},{4,0},{8,12},{12,8},{1,5},{5,1},{9,13},{13,9},{2,6},{6,2},{1... | collective-permute-start | bytes 196616 | tf_op jit(solution)/shard_map/ppermute | solution.py:317
  36.0 0.0 collective-permute-done.10.refs_1_
  36.0 0.8 %shard_map.131.mine = f32[16,64,128]{2,1,0:T(8,128)S(1)} custom-call(f32[64,256]{1,0:T(8,128)S(1)} %get-tuple-element.43.refs_0_.after, f32[64,256]{1,0:T(8,128)S(1)} %collective-permute-done.10.refs_1_, s32[64,256]{1,0:T(8,128)S(1)} %shard_map.123.after.refs_0_.ids.refs_2_.refs_4_, s32[64,256]{1,0:T(8,128)S(1)} %collective-permute-done.3.refs_4_.refs_1_.refs_3_), custom_call_target="tpu_custom_call" | custom-call | tf_op jit(solution)/shard_map/pallas_call | solution.py:25
  36.8 0.1 collective-permute-start.11
  36.9 0.9 %collective-permute-done.14.refs_3_ = f32[64,256]{1,0:T(8,128)S(1)} collective-permute-done((f32[64,256]{1,0:T(8,128)S(1)}, f32[64,256]{1,0:T(8,128)S(1)}, u32[]{:S(2)}, u32[]{:S(2)}) %collective-permute-start.14) | collective-permute-done | bytes 65568 | tf_op jit(solution)/shard_map/ppermute | solution.py:317
  37.8 1.9 %collective-permute-done.13.refs_2_ = f32[64,256]{1,0:T(8,128)S(1)} collective-permute-done((f32[64,256]{1,0:T(8,128)S(1)}, f32[64,256]{1,0:T(8,128)S(1)}, u32[]{:S(2)}, u32[]{:S(2)}) %collective-permute-start.13) | collective-permute-done | bytes 65568 | tf_op jit(solution)/shard_map/ppermute | solution.py:317
  39.7 1.5 %shard_map.132.after.mine = f32[16,64,128]{2,1,0:T(8,128)S(1)} custom-call(f32[64,256]{1,0:T(8,128)S(1)} %get-tuple-element.44.refs_0_, f32[64,256]{1,0:T(8,128)S(1)} %collective-permute-done.12.refs_1_, f32[64,256]{1,0:T(8,128)S(1)} %collective-permute-done.13.refs_2_, f32[64,256]{1,0:T(8,128)S(1)} %collective-permute-done.14.refs_3_, ...), custom_call_target="tpu_custom_call" | custom-call | flops 99999997952 | tf_op jit(solution)/shard_map/pallas_call | solution.py:25
  41.2 0.1 collective-permute-start.15
  41.3 1.9 %shard_map.133 = (f32[16,64,128]{2,1,0:T(8,128)S(1)}, f32[16,32,128]{2,1,0:T(8,128)S(1)}, f32[16,32,128]{2,1,0:T(8,128)S(1)}) custom-call(s32[8,384]{1,0:T(8,128)S(1)} %get-tuple-element.29.order, f32[16,64,128]{2,1,0:T(8,128)S(1)} %shard_map.131.mine, f32[16,64,128]{2,1,0:T(8,128)S(1)} %collective-permute-done.11.other, ...), custom_call_target="tpu_custom_call" | custom-call | flops 603979776 | bytes 9437184 | tf_op jit(solution)/shard_map/pallas_call | solution.py:25
  43.2 0.5 collective-permute-start.16
  43.8 1.2 %collective-permute-done.16.received = f32[16,32,128]{2,1,0:T(8,128)S(1)} collective-permute-done((f32[16,32,128]{2,1,0:T(8,128)S(1)}, f32[16,32,128]{2,1,0:T(8,128)S(1)}, u32[]{:S(2)}, u32[]{:S(2)}) %collective-permute-start.16) | collective-permute-done | bytes 262176 | tf_op jit(solution)/shard_map/ppermute | solution.py:317
  45.0 1.3 %collective-permute-start.17 = (f32[4,32,128]{2,1,0:T(8,128)S(1)}, f32[4,32,128]{2,1,0:T(8,128)S(1)}, u32[]{:S(2)}, u32[]{:S(2)}) collective-permute-start(f32[4,32,128]{2,1,0:T(8,128)S(1)} %get-tuple-element.50), channel_id=1, source_target_pairs={{0,4},{4,0},{8,12},{12,8},{1,5},{5,1},{9,13},{13,9},{2,6},{6,2},{1... | collective-permute-start | bytes 196616 | tf_op jit(solution)/shard_map/ppermute | solution.py:317
  46.3 1.1 %collective-permute-start.18 = (f32[4,32,128]{2,1,0:T(8,128)S(1)}, f32[4,32,128]{2,1,0:T(8,128)S(1)}, u32[]{:S(2)}, u32[]{:S(2)}) collective-permute-start(f32[4,32,128]{2,1,0:T(8,128)S(1)} %get-tuple-element.51), channel_id=1, source_target_pairs={{0,8},{4,12},{8,0},{12,4},{1,9},{5,13},{9,1},{13,5},{2,10},{6,14},... | collective-permute-start | bytes 196616 | tf_op jit(solution)/shard_map/ppermute | solution.py:317
  47.4 2.0 %collective-permute-start.19 = (f32[4,32,128]{2,1,0:T(8,128)S(1)}, f32[4,32,128]{2,1,0:T(8,128)S(1)}, u32[]{:S(2)}, u32[]{:S(2)}) collective-permute-start(f32[4,32,128]{2,1,0:T(8,128)S(1)} %get-tuple-element.52), channel_id=1, source_target_pairs={{0,12},{4,8},{8,4},{12,0},{1,13},{5,9},{9,5},{13,1},{2,14},{6,10},... | collective-permute-start | bytes 196616 | tf_op jit(solution)/shard_map/ppermute | solution.py:317
  49.5 2.4 %shard_map.135 = (f32[16,64,128]{2,1,0:T(8,128)S(1)}, f32[16,64,128]{2,1,0:T(8,128)S(1)}) custom-call(s32[8,384]{1,0:T(8,128)S(1)} %get-tuple-element.30.order, f32[16,64,128]{2,1,0:T(8,128)S(1)} %shard_map.132.after.mine, f32[16,64,128]{2,1,0:T(8,128)S(1)} %collective-permute-done.15.other, f32[16,128]{1,0:T(8,128)S(1)} %get-tuple-element.34.scale.target_scale.source_scale, ...), custom_call_target="tpu_custom_call" | custom-call | flops 603979776 | bytes 9437184 | tf_op jit(solution)/shard_map/pallas_call | solution.py:25
  51.8 0.0 collective-permute-done.17.refs_1_
  51.8 2.6 %collective-permute-done.18.refs_2_ = f32[4,32,128]{2,1,0:T(8,128)S(1)} collective-permute-done((f32[4,32,128]{2,1,0:T(8,128)S(1)}, f32[4,32,128]{2,1,0:T(8,128)S(1)}, u32[]{:S(2)}, u32[]{:S(2)}) %collective-permute-start.18) | collective-permute-done | bytes 65568 | tf_op jit(solution)/shard_map/ppermute | solution.py:317
  54.4 0.0 collective-permute-done.19.refs_3_
  54.5 0.1 collective-permute-start.20
  54.6 1.5 %collective-permute-done.20.refs_1_ = f32[16,32,128]{2,1,0:T(8,128)S(1)} collective-permute-done((f32[16,32,128]{2,1,0:T(8,128)S(1)}, f32[16,32,128]{2,1,0:T(8,128)S(1)}, u32[]{:S(2)}, u32[]{:S(2)}) %collective-permute-start.20) | collective-permute-done | bytes 262176 | tf_op jit(solution)/shard_map/ppermute | solution.py:317
  56.1 3.5 %collective-permute-start.21 = (f32[16,32,128]{2,1,0:T(8,128)S(1)}, f32[16,32,128]{2,1,0:T(8,128)S(1)}, u32[]{:S(2)}, u32[]{:S(2)}) collective-permute-start(f32[16,32,128]{2,1,0:T(8,128)S(1)} %shard_map.138.refs_0_), channel_id=1, source_target_pairs={{0,2},{2,0},{1,3},{3,1},{4,6},{6,4},{5,7},{7,5},{8,10},{10,8},{9,1... | collective-permute-start | bytes 786440 | tf_op jit(solution)/shard_map/ppermute | solution.py:317
  59.6 0.3 collective-permute-start.25
  59.9 0.8 %collective-permute-start.24 = (f32[4,32,128]{2,1,0:T(8,128)S(1)}, f32[4,32,128]{2,1,0:T(8,128)S(1)}, u32[]{:S(2)}, u32[]{:S(2)}) collective-permute-start(f32[4,32,128]{2,1,0:T(8,128)S(1)} %shard_map.136.after.refs_0_), channel_id=1, source_target_pairs={{0,8},{4,12},{8,0},{12,4},{1,9},{5,13},{9,1},{13,5},{2,10},{6,14},... | collective-permute-start | bytes 196616 | tf_op jit(solution)/shard_map/ppermute | solution.py:317
  60.7 3.3 %collective-permute-start.23 = (f32[4,32,128]{2,1,0:T(8,128)S(1)}, f32[4,32,128]{2,1,0:T(8,128)S(1)}, u32[]{:S(2)}, u32[]{:S(2)}) collective-permute-start(f32[4,32,128]{2,1,0:T(8,128)S(1)} %shard_map.136.after.refs_0_), channel_id=1, source_target_pairs={{0,4},{4,0},{8,12},{12,8},{1,5},{5,1},{9,13},{13,9},{2,6},{6,2},{1... | collective-permute-start | bytes 196616 | tf_op jit(solution)/shard_map/ppermute | solution.py:317
  64.0 2.4 %collective-permute-done.25.refs_3_ = f32[4,32,128]{2,1,0:T(8,128)S(1)} collective-permute-done((f32[4,32,128]{2,1,0:T(8,128)S(1)}, f32[4,32,128]{2,1,0:T(8,128)S(1)}, u32[]{:S(2)}, u32[]{:S(2)}) %collective-permute-start.25) | collective-permute-done | bytes 65568 | tf_op jit(solution)/shard_map/ppermute | solution.py:317
  66.4 0.5 collective-permute-done.24.refs_2_
  66.9 0.4 collective-permute-done.23.refs_1_
  67.4 0.1 collective-permute-start.26
  67.4 0.0 collective-permute-done.21.refs_1_
  67.5 0.5 collective-permute-start.22
  68.0 0.9 %collective-permute-done.26.item_other = f32[4,4,32,128]{3,2,1,0:T(8,128)S(1)} collective-permute-done((f32[4,4,32,128]{3,2,1,0:T(8,128)S(1)}, f32[4,4,32,128]{3,2,1,0:T(8,128)S(1)}, u32[]{:S(2)}, u32[]{:S(2)}) %collective-permute-start.26) | collective-permute-done | bytes 262176 | tf_op jit(solution)/shard_map/ppermute | solution.py:317
  69.0 0.4 collective-permute-done.22.user_other
  69.3 1.1 %shard_map.141 = (f32[64,2048]{1,0:T(8,128)}, f32[64,2048]{1,0:T(8,128)}) custom-call(f32[16,64,128]{2,1,0:T(8,128)S(1)} %get-tuple-element.45.user_half_grad, f32[16,32,128]{2,1,0:T(8,128)S(1)} %shard_map.139.user_mine, f32[16,32,128]{2,1,0:T(8,128)S(1)} %collective-permute-done.22.user_other, f32[16,64,128]{2,1,0:T(8,128)S(1)} %get-tuple-element.55.item_half_grad, ...), custom_call_target="tpu_custom_call" | custom-call | bytes 3145728 | tf_op jit(solution)/shard_map/pallas_call | solution.py:25
  (30 shorter events, 0.2 us)
Async XLA Ops:
  0.6 0.7 copy-start.3
  0.6 0.7 copy-start.2
  0.7 0.7 copy-start.1
  0.7 8.7 %copy-start.5 = (bf16[64,2048]{1,0:T(8,128)(2,1)S(1)}, bf16[64,2048]{1,0:T(8,128)(2,1)}, u32[]{:S(2)}) copy-start(bf16[64,2048]{1,0:T(8,128)(2,1)} %item_emb.3) | copy-start | bytes 786436
  0.7 8.7 %copy-start.4 = (bf16[64,2048]{1,0:T(8,128)(2,1)S(1)}, bf16[64,2048]{1,0:T(8,128)(2,1)}, u32[]{:S(2)}) copy-start(bf16[64,2048]{1,0:T(8,128)(2,1)} %user_emb.3) | copy-start | bytes 786436
  0.7 8.7 %copy-start.9 = (s32[288]{0:T(512)S(1)}, s32[288]{0:T(512)}, u32[]{:S(2)}) copy-start(s32[288]{0:T(512)} %columns.1) | copy-start | bytes 3460
  0.7 8.7 %copy-start.8 = (s32[288]{0:T(512)S(1)}, s32[288]{0:T(512)}, u32[]{:S(2)}) copy-start(s32[288]{0:T(512)} %rows.1) | copy-start | bytes 3460
  0.7 8.7 %copy-start.7 = (s32[2048]{0:T(1024)S(1)}, s32[2048]{0:T(1024)}, u32[]{:S(2)}) copy-start(s32[2048]{0:T(1024)} %param.14) | copy-start | bytes 24580
  0.7 8.7 %copy-start.6 = (s32[2048]{0:T(1024)S(1)}, s32[2048]{0:T(1024)}, u32[]{:S(2)}) copy-start(s32[2048]{0:T(1024)} %param.13) | copy-start | bytes 24580
  0.7 9.7 %copy-start = (bf16[288,128,128]{2,1,0:T(8,128)(2,1)S(1)}, bf16[288,128,128]{2,1,0:T(8,128)(2,1)}, u32[]{:S(2)}) copy-start(bf16[288,128,128]{2,1,0:T(8,128)(2,1)} %vals.7) | copy-start | bytes 28311556
  1.4 10.9 %collective-permute-start.3 = (s32[64,256]{1,0:T(8,128)S(1)}, s32[64,256]{1,0:T(8,128)S(1)}, u32[]{:S(2)}, u32[]{:S(2)}) collective-permute-start(s32[64,256]{1,0:T(8,128)S(1)} %shard_map.123.after.refs_0_.ids.refs_2_.refs_4_), channel_id=1, source_target_pairs={{0,2},{2,0},{1,3},{3,1},{4,6},{6,4},{5,7},{7,5},{8,10},{10,8},{9,1... | collective-permute-start | bytes 196616 | tf_op jit(solution)/shard_map/ppermute | solution.py:317
  4.3 8.0 %collective-permute-start.2 = (s32[64,256]{1,0:T(8,128)S(1)}, s32[64,256]{1,0:T(8,128)S(1)}, u32[]{:S(2)}, u32[]{:S(2)}) collective-permute-start(s32[64,256]{1,0:T(8,128)S(1)} %shard_map.123.after.refs_0_.ids.refs_2_.refs_4_), channel_id=1, source_target_pairs={{0,12},{4,8},{8,4},{12,0},{1,13},{5,9},{9,5},{13,1},{2,14},{6,10},... | collective-permute-start | bytes 196616 | tf_op jit(solution)/shard_map/ppermute | solution.py:317
  7.9 5.4 %collective-permute-start.1 = (s32[64,256]{1,0:T(8,128)S(1)}, s32[64,256]{1,0:T(8,128)S(1)}, u32[]{:S(2)}, u32[]{:S(2)}) collective-permute-start(s32[64,256]{1,0:T(8,128)S(1)} %shard_map.123.after.refs_0_.ids.refs_2_.refs_4_), channel_id=1, source_target_pairs={{0,8},{4,12},{8,0},{12,4},{1,9},{5,13},{9,1},{13,5},{2,10},{6,14},... | collective-permute-start | bytes 196616 | tf_op jit(solution)/shard_map/ppermute | solution.py:317
  8.0 5.4 %collective-permute-start = (s32[64,256]{1,0:T(8,128)S(1)}, s32[64,256]{1,0:T(8,128)S(1)}, u32[]{:S(2)}, u32[]{:S(2)}) collective-permute-start(s32[64,256]{1,0:T(8,128)S(1)} %shard_map.123.after.refs_0_.ids.refs_2_.refs_4_), channel_id=1, source_target_pairs={{0,4},{4,0},{8,12},{12,8},{1,5},{5,1},{9,13},{13,9},{2,6},{6,2},{1... | collective-permute-start | bytes 196616 | tf_op jit(solution)/shard_map/ppermute | solution.py:317
  12.2 3.5 %collective-permute-start.5 = (f32[16,64,128]{2,1,0:T(8,128)S(1)}, f32[16,64,128]{2,1,0:T(8,128)S(1)}, u32[]{:S(2)}, u32[]{:S(2)}) collective-permute-start(f32[16,64,128]{2,1,0:T(8,128)S(1)} %shard_map.125.refs_0_.mine), channel_id=1, source_target_pairs={{0,1},{1,0},{2,3},{3,2},{4,5},{5,4},{6,7},{7,6},{8,9},{9,8},{10,11... | collective-permute-start | bytes 1572872 | tf_op jit(solution)/shard_map/ppermute | solution.py:317
  15.6 6.2 %collective-permute-start.4 = (f32[16,64,128]{2,1,0:T(8,128)S(1)}, f32[16,64,128]{2,1,0:T(8,128)S(1)}, u32[]{:S(2)}, u32[]{:S(2)}) collective-permute-start(f32[16,64,128]{2,1,0:T(8,128)S(1)} %shard_map.126.mine), channel_id=1, source_target_pairs={{0,1},{1,0},{2,3},{3,2},{4,5},{5,4},{6,7},{7,6},{8,9},{9,8},{10,11... | collective-permute-start | bytes 1572872 | tf_op jit(solution)/shard_map/ppermute | solution.py:317
  17.0 10.7 %collective-permute-start.7 = (f32[64,256]{1,0:T(8,128)S(1)}, f32[64,256]{1,0:T(8,128)S(1)}, u32[]{:S(2)}, u32[]{:S(2)}) collective-permute-start(f32[64,256]{1,0:T(8,128)S(1)} %get-tuple-element.39), channel_id=1, source_target_pairs={{0,4},{4,0},{8,12},{12,8},{1,5},{5,1},{9,13},{13,9},{2,6},{6,2},{1... | collective-permute-start | bytes 196616 | tf_op jit(solution)/shard_map/ppermute | solution.py:317
  19.4 8.4 %collective-permute-start.8 = (f32[64,256]{1,0:T(8,128)S(1)}, f32[64,256]{1,0:T(8,128)S(1)}, u32[]{:S(2)}, u32[]{:S(2)}) collective-permute-start(f32[64,256]{1,0:T(8,128)S(1)} %get-tuple-element.40), channel_id=1, source_target_pairs={{0,8},{4,12},{8,0},{12,4},{1,9},{5,13},{9,1},{13,5},{2,10},{6,14},... | collective-permute-start | bytes 196616 | tf_op jit(solution)/shard_map/ppermute | solution.py:317
  21.1 6.7 %collective-permute-start.9 = (f32[64,256]{1,0:T(8,128)S(1)}, f32[64,256]{1,0:T(8,128)S(1)}, u32[]{:S(2)}, u32[]{:S(2)}) collective-permute-start(f32[64,256]{1,0:T(8,128)S(1)} %get-tuple-element.41), channel_id=1, source_target_pairs={{0,12},{4,8},{8,4},{12,0},{1,13},{5,9},{9,5},{13,1},{2,14},{6,10},... | collective-permute-start | bytes 196616 | tf_op jit(solution)/shard_map/ppermute | solution.py:317
  22.4 7.1 %collective-permute-start.6 = (f32[64,256]{1,0:T(8,128)S(1)}, f32[64,256]{1,0:T(8,128)S(1)}, u32[]{:S(2)}, u32[]{:S(2)}) collective-permute-start(f32[64,256]{1,0:T(8,128)S(1)} %get-tuple-element.37), channel_id=1, source_target_pairs={{0,2},{2,0},{1,3},{3,1},{4,6},{6,4},{5,7},{7,5},{8,10},{10,8},{9,1... | collective-permute-start | bytes 196616 | tf_op jit(solution)/shard_map/ppermute | solution.py:317
  29.5 6.5 %collective-permute-start.10 = (f32[64,256]{1,0:T(8,128)S(1)}, f32[64,256]{1,0:T(8,128)S(1)}, u32[]{:S(2)}, u32[]{:S(2)}) collective-permute-start(f32[64,256]{1,0:T(8,128)S(1)} %get-tuple-element.43.refs_0_.after), channel_id=1, source_target_pairs={{0,2},{2,0},{1,3},{3,1},{4,6},{6,4},{5,7},{7,5},{8,10},{10,8},{9,1... | collective-permute-start | bytes 196616 | tf_op jit(solution)/shard_map/ppermute | solution.py:317
  31.6 6.2 %collective-permute-start.14 = (f32[64,256]{1,0:T(8,128)S(1)}, f32[64,256]{1,0:T(8,128)S(1)}, u32[]{:S(2)}, u32[]{:S(2)}) collective-permute-start(f32[64,256]{1,0:T(8,128)S(1)} %get-tuple-element.44.refs_0_), channel_id=1, source_target_pairs={{0,12},{4,8},{8,4},{12,0},{1,13},{5,9},{9,5},{13,1},{2,14},{6,10},... | collective-permute-start | bytes 196616 | tf_op jit(solution)/shard_map/ppermute | solution.py:317
  32.8 6.8 %collective-permute-start.13 = (f32[64,256]{1,0:T(8,128)S(1)}, f32[64,256]{1,0:T(8,128)S(1)}, u32[]{:S(2)}, u32[]{:S(2)}) collective-permute-start(f32[64,256]{1,0:T(8,128)S(1)} %get-tuple-element.44.refs_0_), channel_id=1, source_target_pairs={{0,8},{4,12},{8,0},{12,4},{1,9},{5,13},{9,1},{13,5},{2,10},{6,14},... | collective-permute-start | bytes 196616 | tf_op jit(solution)/shard_map/ppermute | solution.py:317
  34.0 5.6 %collective-permute-start.12 = (f32[64,256]{1,0:T(8,128)S(1)}, f32[64,256]{1,0:T(8,128)S(1)}, u32[]{:S(2)}, u32[]{:S(2)}) collective-permute-start(f32[64,256]{1,0:T(8,128)S(1)} %get-tuple-element.44.refs_0_), channel_id=1, source_target_pairs={{0,4},{4,0},{8,12},{12,8},{1,5},{5,1},{9,13},{13,9},{2,6},{6,2},{1... | collective-permute-start | bytes 196616 | tf_op jit(solution)/shard_map/ppermute | solution.py:317
  36.8 4.4 %collective-permute-start.11 = (f32[16,64,128]{2,1,0:T(8,128)S(1)}, f32[16,64,128]{2,1,0:T(8,128)S(1)}, u32[]{:S(2)}, u32[]{:S(2)}) collective-permute-start(f32[16,64,128]{2,1,0:T(8,128)S(1)} %shard_map.131.mine), channel_id=1, source_target_pairs={{0,1},{1,0},{2,3},{3,2},{4,5},{5,4},{6,7},{7,6},{8,9},{9,8},{10,11... | collective-permute-start | bytes 1572872 | tf_op jit(solution)/shard_map/ppermute | solution.py:317
  41.2 8.3 %collective-permute-start.15 = (f32[16,64,128]{2,1,0:T(8,128)S(1)}, f32[16,64,128]{2,1,0:T(8,128)S(1)}, u32[]{:S(2)}, u32[]{:S(2)}) collective-permute-start(f32[16,64,128]{2,1,0:T(8,128)S(1)} %shard_map.132.after.mine), channel_id=1, source_target_pairs={{0,1},{1,0},{2,3},{3,2},{4,5},{5,4},{6,7},{7,6},{8,9},{9,8},{10,11... | collective-permute-start | bytes 1572872 | tf_op jit(solution)/shard_map/ppermute | solution.py:317
  43.2 1.7 %collective-permute-start.16 = (f32[16,32,128]{2,1,0:T(8,128)S(1)}, f32[16,32,128]{2,1,0:T(8,128)S(1)}, u32[]{:S(2)}, u32[]{:S(2)}) collective-permute-start(f32[16,32,128]{2,1,0:T(8,128)S(1)} %get-tuple-element.47), channel_id=1, source_target_pairs={{0,1},{1,0},{2,3},{3,2},{4,5},{5,4},{6,7},{7,6},{8,9},{9,8},{10,11... | collective-permute-start | bytes 786440 | tf_op jit(solution)/shard_map/ppermute | solution.py:317
  45.0 6.8 %collective-permute-start.17 = (f32[4,32,128]{2,1,0:T(8,128)S(1)}, f32[4,32,128]{2,1,0:T(8,128)S(1)}, u32[]{:S(2)}, u32[]{:S(2)}) collective-permute-start(f32[4,32,128]{2,1,0:T(8,128)S(1)} %get-tuple-element.50), channel_id=1, source_target_pairs={{0,4},{4,0},{8,12},{12,8},{1,5},{5,1},{9,13},{13,9},{2,6},{6,2},{1... | collective-permute-start | bytes 196616 | tf_op jit(solution)/shard_map/ppermute | solution.py:317
  46.3 8.1 %collective-permute-start.18 = (f32[4,32,128]{2,1,0:T(8,128)S(1)}, f32[4,32,128]{2,1,0:T(8,128)S(1)}, u32[]{:S(2)}, u32[]{:S(2)}) collective-permute-start(f32[4,32,128]{2,1,0:T(8,128)S(1)} %get-tuple-element.51), channel_id=1, source_target_pairs={{0,8},{4,12},{8,0},{12,4},{1,9},{5,13},{9,1},{13,5},{2,10},{6,14},... | collective-permute-start | bytes 196616 | tf_op jit(solution)/shard_map/ppermute | solution.py:317
  47.4 7.0 %collective-permute-start.19 = (f32[4,32,128]{2,1,0:T(8,128)S(1)}, f32[4,32,128]{2,1,0:T(8,128)S(1)}, u32[]{:S(2)}, u32[]{:S(2)}) collective-permute-start(f32[4,32,128]{2,1,0:T(8,128)S(1)} %get-tuple-element.52), channel_id=1, source_target_pairs={{0,12},{4,8},{8,4},{12,0},{1,13},{5,9},{9,5},{13,1},{2,14},{6,10},... | collective-permute-start | bytes 196616 | tf_op jit(solution)/shard_map/ppermute | solution.py:317
  54.5 1.6 %collective-permute-start.20 = (f32[16,32,128]{2,1,0:T(8,128)S(1)}, f32[16,32,128]{2,1,0:T(8,128)S(1)}, u32[]{:S(2)}, u32[]{:S(2)}) collective-permute-start(f32[16,32,128]{2,1,0:T(8,128)S(1)} %get-tuple-element.54), channel_id=1, source_target_pairs={{0,1},{1,0},{2,3},{3,2},{4,5},{5,4},{6,7},{7,6},{8,9},{9,8},{10,11... | collective-permute-start | bytes 786440 | tf_op jit(solution)/shard_map/ppermute | solution.py:317
  56.1 11.3 %collective-permute-start.21 = (f32[16,32,128]{2,1,0:T(8,128)S(1)}, f32[16,32,128]{2,1,0:T(8,128)S(1)}, u32[]{:S(2)}, u32[]{:S(2)}) collective-permute-start(f32[16,32,128]{2,1,0:T(8,128)S(1)} %shard_map.138.refs_0_), channel_id=1, source_target_pairs={{0,2},{2,0},{1,3},{3,1},{4,6},{6,4},{5,7},{7,5},{8,10},{10,8},{9,1... | collective-permute-start | bytes 786440 | tf_op jit(solution)/shard_map/ppermute | solution.py:317
  59.6 6.8 %collective-permute-start.25 = (f32[4,32,128]{2,1,0:T(8,128)S(1)}, f32[4,32,128]{2,1,0:T(8,128)S(1)}, u32[]{:S(2)}, u32[]{:S(2)}) collective-permute-start(f32[4,32,128]{2,1,0:T(8,128)S(1)} %shard_map.136.after.refs_0_), channel_id=1, source_target_pairs={{0,12},{4,8},{8,4},{12,0},{1,13},{5,9},{9,5},{13,1},{2,14},{6,10},... | collective-permute-start | bytes 196616 | tf_op jit(solution)/shard_map/ppermute | solution.py:317
  59.9 7.0 %collective-permute-start.24 = (f32[4,32,128]{2,1,0:T(8,128)S(1)}, f32[4,32,128]{2,1,0:T(8,128)S(1)}, u32[]{:S(2)}, u32[]{:S(2)}) collective-permute-start(f32[4,32,128]{2,1,0:T(8,128)S(1)} %shard_map.136.after.refs_0_), channel_id=1, source_target_pairs={{0,8},{4,12},{8,0},{12,4},{1,9},{5,13},{9,1},{13,5},{2,10},{6,14},... | collective-permute-start | bytes 196616 | tf_op jit(solution)/shard_map/ppermute | solution.py:317
  60.7 6.6 %collective-permute-start.23 = (f32[4,32,128]{2,1,0:T(8,128)S(1)}, f32[4,32,128]{2,1,0:T(8,128)S(1)}, u32[]{:S(2)}, u32[]{:S(2)}) collective-permute-start(f32[4,32,128]{2,1,0:T(8,128)S(1)} %shard_map.136.after.refs_0_), channel_id=1, source_target_pairs={{0,4},{4,0},{8,12},{12,8},{1,5},{5,1},{9,13},{13,9},{2,6},{6,2},{1... | collective-permute-start | bytes 196616 | tf_op jit(solution)/shard_map/ppermute | solution.py:317
  67.4 1.6 %collective-permute-start.26 = (f32[4,4,32,128]{3,2,1,0:T(8,128)S(1)}, f32[4,4,32,128]{3,2,1,0:T(8,128)S(1)}, u32[]{:S(2)}, u32[]{:S(2)}) collective-permute-start(f32[4,4,32,128]{3,2,1,0:T(8,128)S(1)} %shard_map.140.item_mine), channel_id=1, source_target_pairs={{0,1},{1,0},{2,3},{3,2},{4,5},{5,4},{6,7},{7,6},{8,9},{9,8},{10,11... | collective-permute-start | bytes 786440 | tf_op jit(solution)/shard_map/ppermute | solution.py:317
  67.5 1.8 %collective-permute-start.22 = (f32[16,32,128]{2,1,0:T(8,128)S(1)}, f32[16,32,128]{2,1,0:T(8,128)S(1)}, u32[]{:S(2)}, u32[]{:S(2)}) collective-permute-start(f32[16,32,128]{2,1,0:T(8,128)S(1)} %shard_map.139.user_mine), channel_id=1, source_target_pairs={{0,1},{1,0},{2,3},{3,2},{4,5},{5,4},{6,7},{7,6},{8,9},{9,8},{10,11... | collective-permute-start | bytes 786440 | tf_op jit(solution)/shard_map/ppermute | solution.py:317
